TPU v7x, 256 devices: a whole 4x4x8 slice. The times are simulated.
256 devices in a mesh: acq: 64 (over z, x, core), rng: 4 (over y).
Axes of the slice: x: 4, y: 4, z: 8, core: 2. Of those that a mesh axis runs over, the one named last changes fastest.
Arguments:
- scenes: bfloat16 [128, 2, 256, 8192], P('acq', None, None, 'rng'), may hold values from -30 to 30, as said below
- pairs: int32 [384, 2], P('acq'), may hold values from 0 to 127, as said below
- pair_owner: int32 [384], replicated, may hold values from 0 to 383, each once
- design_pinv: float32 [128, 384], replicated, may hold values from -0.3125 to 0.3125
Outputs:
- series: float32 [64, 128, 512], P('acq', None, 'rng')
Inputs may be any that keep to these rules, and one draw needn't show every extreme that they name: Rows d * 6 to (d + 1) * 6 - 1 hold distinct pairs whose two acquisitions lie between (d - 1) * 2 and (d + 2) * 2 - 1, the reference lower than the secondary. `scenes`: every pixel's phase atan2(imaginary, real) lies within -0.75 to 0.75, its magnitude between 0.1 and 30.
All inputs are finite; a program needn't handle non-finite values.
Results may differ from a plain program's by a relative error of at most 0.0003.
Values may be sent and summed in bfloat16 or wider, within the bound.
No kernel may reach another device: no remote copies, remote signals or barrier semaphores. Data moves between devices by JAX's collectives and lax.ppermute only.
A program may use at most 128 MiB of HBM per device.

v0:
```python
import jax
import jax.numpy as jnp
from jax import lax
from jax.sharding import PartitionSpec as P

LOOK_R = 4
LOOK_C = 16


def with_halo(block, sides, width):
    for axis, dim in sides:
        count = lax.axis_size(axis)
        forward = [(i, i + 1) for i in range(count - 1)]
        backward = [(target, source) for source, target in forward]
        low = lax.ppermute(
            lax.slice_in_dim(block, block.shape[dim] - width, None, axis=dim), axis, forward
        )
        high = lax.ppermute(lax.slice_in_dim(block, 0, width, axis=dim), axis, backward)
        block = jnp.concatenate([low, block, high], axis=dim)
    return block


def multilook(values):
    rows, cols = values.shape
    return values.reshape(rows // LOOK_R, LOOK_R, cols // LOOK_C, LOOK_C).sum(axis=(1, 3))


def pair_phases(stack, pair_rows):

    def one_pair(pair):
        first = lax.dynamic_index_in_dim(stack, pair[0], 0, keepdims=False).astype(jnp.float32)
        second = lax.dynamic_index_in_dim(stack, pair[1], 0, keepdims=False).astype(jnp.float32)
        real_part = first[0] * second[0] + first[1] * second[1]
        imag_part = first[1] * second[0] - first[0] * second[1]
        return jnp.arctan2(multilook(imag_part), multilook(real_part))

    return lax.map(one_pair, pair_rows)


def body(scenes, pairs, pair_owner, design_pinv):
    acq_local = scenes.shape[0]
    pair_local = pairs.shape[0]
    extended = with_halo(scenes, (("acq", 0),), acq_local)
    offset = lax.axis_index("acq") * acq_local - acq_local
    local_pairs = pairs - offset
    phase = jnp.transpose(pair_phases(extended, local_pairs), (1, 0, 2))
    start = lax.axis_index("acq") * pair_local
    own_slots = lax.dynamic_slice_in_dim(pair_owner, start, pair_local)
    own_pinv = jnp.take(design_pinv, own_slots, axis=1)
    return lax.psum_scatter(
        jnp.einsum("ap,rpc->rac", own_pinv, phase, precision=lax.Precision.HIGHEST),
        "acq",
        scatter_dimension=0,
        tiled=True,
    )


def solution(mesh):
    placed = (P("acq", None, None, "rng"), P("acq", None), P(), P())
    return jax.shard_map(
        body, mesh=mesh, in_specs=placed, out_specs=P("acq", None, "rng"), check_vma=False
    )
```

profile of v0, /device:TPU:1, one launch (start us, length us, event | category | flops | bytes accessed | tf_op | source)
XLA Modules:
  0.0 491.2 jit_solution(7459230854768573168)
XLA Ops:
  16.7 40.8 %collective-permute-done.1 = bf16[2,2,256,2048]{3,2,1,0:T(8,128)(2,1)} collective-permute-done((bf16[2,2,256,2048]{3,2,1,0:T(8,128)(2,1)}, bf16[2,2,256,2048]{3,2,1,0:T(8,128)(2,1)}, u32[]{:S(2)}, u32[]{:S(2)}) %collective-permute-start.1) | collective-permute-done | bytes 4194336 | tf_op jit(solution)/shard_map/ppermute | solution.py:18
  59.4 10.6 %pad_maximum_fusion = bf16[6,2,256,2048]{3,2,1,0:T(8,128)(2,1)} fusion(bf16[2,2,256,2048]{3,2,1,0:T(8,128)(2,1)} %collective-permute-done.1, bf16[2,2,256,2048]{3,2,1,0:T(8,128)(2,1)} %param.6, bf16[2,2,256,2048]{3,2,1,0:T(8,128)(2,1)} %collective-permute-done), kind=kLoop, calls=%fused_computation.7 | loop fusion | flops 12582912 | bytes 25165824 | tf_op jit(solution)/shard_map/concatenate | solution.py:19
  69.9 260.1 %while.10 = (s32[]{:T(128)}, f32[6,64,128]{2,1,0:T(8,128)S(1)}, s32[6,2]{0,1:T(2,128)S(1)}, bf16[6,2,256,2048]{3,2,1,0:T(8,128)(2,1)}, s32[]{:T(128)}, /*index=5*/s32[]{:T(128)}, s32[]{:T(128)}, f32[]{:T(128)}) while((s32[]{:T(128)}, f32[6,64,128]{2,1,0:T(8,128)S(1)}, s32[6,2]{0,1:T(2,128)S(1)}, bf16[6,2,256,2048]{3,2,1,0:T(8,128)(2,1)}, ...), condition=%wide.region_3.4_spmd, body=%wide.region_0.3_spmd.sunk | while | flops 6275080 | bytes 37912792 | solution.py:37
  79.9 10.4 %sub.28 = f32[64,4,128,16]{3,2,1,0:T(8,128)} reshape(f32[1,1,256,2048]{3,2,1,0:T(8,128)} %get-tuple-element.79) | data formatting | bytes 4194304 | tf_op jit(solution)/shard_map/while/body/eval_jaxpr/sub | solution.py:34
  90.2 7.0 %reduce_sum.20 = f32[64,128]{1,0:T(8,128)S(1)} reduce(f32[64,4,128,16]{3,2,1,0:T(8,128)} %sub.28, f32[]{:T(128)} %constant.25.clone.1..sunk), dimensions={1,3}, to_apply=%region_1.1 | reduce | flops 516096 | bytes 2129924 | tf_op jit(solution)/shard_map/while/body/eval_jaxpr/reduce_sum | solution.py:25
  97.2 9.0 %add.48 = f32[64,4,128,16]{3,2,1,0:T(8,128)} reshape(f32[1,1,256,2048]{3,2,1,0:T(8,128)S(1)} %get-tuple-element.80) | data formatting | bytes 4194304 | tf_op jit(solution)/shard_map/while/body/eval_jaxpr/add | solution.py:33
  106.2 7.0 %reduce_sum.21 = f32[64,128]{1,0:T(8,128)S(1)} reduce(f32[64,4,128,16]{3,2,1,0:T(8,128)} %add.48, f32[]{:T(128)} %constant.25.clone.1..sunk), dimensions={1,3}, to_apply=%region_2.2 | reduce | flops 516096 | bytes 2129924 | tf_op jit(solution)/shard_map/while/body/eval_jaxpr/reduce_sum | solution.py:25
  123.2 10.4 %sub.28 = f32[64,4,128,16]{3,2,1,0:T(8,128)} reshape(f32[1,1,256,2048]{3,2,1,0:T(8,128)} %get-tuple-element.79) | data formatting | bytes 4194304 | tf_op jit(solution)/shard_map/while/body/eval_jaxpr/sub | solution.py:34
  133.6 7.0 %reduce_sum.20 = f32[64,128]{1,0:T(8,128)S(1)} reduce(f32[64,4,128,16]{3,2,1,0:T(8,128)} %sub.28, f32[]{:T(128)} %constant.25.clone.1..sunk), dimensions={1,3}, to_apply=%region_1.1 | reduce | flops 516096 | bytes 2129924 | tf_op jit(solution)/shard_map/while/body/eval_jaxpr/reduce_sum | solution.py:25
  140.6 9.0 %add.48 = f32[64,4,128,16]{3,2,1,0:T(8,128)} reshape(f32[1,1,256,2048]{3,2,1,0:T(8,128)S(1)} %get-tuple-element.80) | data formatting | bytes 4194304 | tf_op jit(solution)/shard_map/while/body/eval_jaxpr/add | solution.py:33
  149.5 7.0 %reduce_sum.21 = f32[64,128]{1,0:T(8,128)S(1)} reduce(f32[64,4,128,16]{3,2,1,0:T(8,128)} %add.48, f32[]{:T(128)} %constant.25.clone.1..sunk), dimensions={1,3}, to_apply=%region_2.2 | reduce | flops 516096 | bytes 2129924 | tf_op jit(solution)/shard_map/while/body/eval_jaxpr/reduce_sum | solution.py:25
  166.6 10.4 %sub.28 = f32[64,4,128,16]{3,2,1,0:T(8,128)} reshape(f32[1,1,256,2048]{3,2,1,0:T(8,128)} %get-tuple-element.79) | data formatting | bytes 4194304 | tf_op jit(solution)/shard_map/while/body/eval_jaxpr/sub | solution.py:34
  176.9 7.0 %reduce_sum.20 = f32[64,128]{1,0:T(8,128)S(1)} reduce(f32[64,4,128,16]{3,2,1,0:T(8,128)} %sub.28, f32[]{:T(128)} %constant.25.clone.1..sunk), dimensions={1,3}, to_apply=%region_1.1 | reduce | flops 516096 | bytes 2129924 | tf_op jit(solution)/shard_map/while/body/eval_jaxpr/reduce_sum | solution.py:25
  183.9 9.0 %add.48 = f32[64,4,128,16]{3,2,1,0:T(8,128)} reshape(f32[1,1,256,2048]{3,2,1,0:T(8,128)S(1)} %get-tuple-element.80) | data formatting | bytes 4194304 | tf_op jit(solution)/shard_map/while/body/eval_jaxpr/add | solution.py:33
  192.9 7.0 %reduce_sum.21 = f32[64,128]{1,0:T(8,128)S(1)} reduce(f32[64,4,128,16]{3,2,1,0:T(8,128)} %add.48, f32[]{:T(128)} %constant.25.clone.1..sunk), dimensions={1,3}, to_apply=%region_2.2 | reduce | flops 516096 | bytes 2129924 | tf_op jit(solution)/shard_map/while/body/eval_jaxpr/reduce_sum | solution.py:25
  209.9 10.4 %sub.28 = f32[64,4,128,16]{3,2,1,0:T(8,128)} reshape(f32[1,1,256,2048]{3,2,1,0:T(8,128)} %get-tuple-element.79) | data formatting | bytes 4194304 | tf_op jit(solution)/shard_map/while/body/eval_jaxpr/sub | solution.py:34
  220.3 7.0 %reduce_sum.20 = f32[64,128]{1,0:T(8,128)S(1)} reduce(f32[64,4,128,16]{3,2,1,0:T(8,128)} %sub.28, f32[]{:T(128)} %constant.25.clone.1..sunk), dimensions={1,3}, to_apply=%region_1.1 | reduce | flops 516096 | bytes 2129924 | tf_op jit(solution)/shard_map/while/body/eval_jaxpr/reduce_sum | solution.py:25
  227.3 9.0 %add.48 = f32[64,4,128,16]{3,2,1,0:T(8,128)} reshape(f32[1,1,256,2048]{3,2,1,0:T(8,128)S(1)} %get-tuple-element.80) | data formatting | bytes 4194304 | tf_op jit(solution)/shard_map/while/body/eval_jaxpr/add | solution.py:33
  253.3 10.4 %sub.28 = f32[64,4,128,16]{3,2,1,0:T(8,128)} reshape(f32[1,1,256,2048]{3,2,1,0:T(8,128)} %get-tuple-element.79) | data formatting | bytes 4194304 | tf_op jit(solution)/shard_map/while/body/eval_jaxpr/sub | solution.py:34
  270.6 9.0 %add.48 = f32[64,4,128,16]{3,2,1,0:T(8,128)} reshape(f32[1,1,256,2048]{3,2,1,0:T(8,128)S(1)} %get-tuple-element.80) | data formatting | bytes 4194304 | tf_op jit(solution)/shard_map/while/body/eval_jaxpr/add | solution.py:33
  296.6 10.4 %sub.28 = f32[64,4,128,16]{3,2,1,0:T(8,128)} reshape(f32[1,1,256,2048]{3,2,1,0:T(8,128)} %get-tuple-element.79) | data formatting | bytes 4194304 | tf_op jit(solution)/shard_map/while/body/eval_jaxpr/sub | solution.py:34
  314.0 9.0 %add.48 = f32[64,4,128,16]{3,2,1,0:T(8,128)} reshape(f32[1,1,256,2048]{3,2,1,0:T(8,128)S(1)} %get-tuple-element.80) | data formatting | bytes 4194304 | tf_op jit(solution)/shard_map/while/body/eval_jaxpr/add | solution.py:33
  330.0 8.2 %convolution_bitcast_fusion = f32[64,128,128]{1,2,0:T(8,128)} fusion(f32[64,6,128]{2,0,1:T(8,128)S(1)} %bitcast.21, f32[6,128]{1,0:T(8,128)S(1)} %gather_fusion, pred[6]{0:T(512)(128)(4,1)S(1)} %get-tuple-element.36), kind=kOutput, calls=%fused_computation.8 | convolution fusion | flops 75498240 | bytes 4393990 | tf_op jit(solution)/shard_map/ap,rpc->rac/dot_general | solution.py:51
  338.2 144.6 %reduce-scatter.4.cloned.1.call-done = f32[1,128,128]{1,2,0:T(8,128)} async-done(((f32[64,128,128]{1,2,0:T(8,128)}), f32[1,128,128]{1,2,0:T(8,128)}) %reduce-scatter.4.cloned.1.call-update) | async-done | bytes 65552
  (47 shorter events, 85.8 us)
Async XLA Ops:
  6.5 476.3 %reduce-scatter.4.cloned.1.call-start = ((), (), s32[]{:S(2)}) async-start(), calls=%async_computation.1 | async-start | bytes 4259840
  6.5 51.0 %collective-permute-start.1 = (bf16[2,2,256,2048]{3,2,1,0:T(8,128)(2,1)}, bf16[2,2,256,2048]{3,2,1,0:T(8,128)(2,1)}, u32[]{:S(2)}, u32[]{:S(2)}) collective-permute-start(bf16[2,2,256,2048]{3,2,1,0:T(8,128)(2,1)} %param.6), channel_id=1, source_target_pairs={{4,0},{8,4},{12,8},{16,12},{20,16},{24,20},{28,24},{32,28},{36,32}... | collective-permute-start | bytes 12582920 | tf_op jit(solution)/shard_map/ppermute | solution.py:18
  11.7 47.7 %collective-permute-start = (bf16[2,2,256,2048]{3,2,1,0:T(8,128)(2,1)}, bf16[2,2,256,2048]{3,2,1,0:T(8,128)(2,1)}, u32[]{:S(2)}, u32[]{:S(2)}) collective-permute-start(bf16[2,2,256,2048]{3,2,1,0:T(8,128)(2,1)} %param.6), channel_id=1, source_target_pairs={{0,4},{4,8},{8,12},{12,16},{16,20},{20,24},{24,28},{28,32},{32,36}... | collective-permute-start | bytes 12582920 | tf_op jit(solution)/shard_map/ppermute | solution.py:15
Sparse Core Ops, SparseCore 0:
  338.4 144.3 reduce-scatter.3
where the time goes:
time: 497 us; the launch traced here: 491 us
  waiting for transfers between devices  187 us (38%)
  other arithmetic  129 us (26%)
  local copies, waits for them, and re-layouts  124 us (25%)
  loops' own time  23 us (5%)
  between operations  13.4 us (3%)
  matrix products  8.23 us (2%)
  starting transfers between devices  7.07 us (1%)
    unnamed x2, waiting for transfers between devices  145 us
    reduce_sum x12, other arithmetic, multilook(): values.reshape(rows // LOOK_R, LOOK_R, cols // LOOK_C, LOOK_C)  83.7 us
    sub x6, local copies, waits for them, and re-layouts, one_pair(): imag_part = first[1] * second[0] - first[0] * second[1]  62.2 us
    add x6, local copies, waits for them, and re-layouts, one_pair(): real_part = first[0] * second[0] + first[1] * second[1]  53.8 us
    ppermute x1, waiting for transfers between devices, with_halo(): lax.ppermute(lax.slice_in_dim(block, 0, width, axis=dim), axis, backward)  40.8 us
    another operation x1, loops' own time, pair_phases(): return lax.map(one_pair, pair_rows)  23 us
    convert_element_type x6, other arithmetic, one_pair(): lax.dynamic_index_in_dim(stack, pair[0], 0, keepdims=False)  19.8 us
    add x6, other arithmetic, one_pair(): real_part = first[0] * second[0] + first[1] * second[1]  13.2 us
  transfers between devices with their start and end apart: 3, of which 3 were waited for; matrix products, arithmetic and copies ran while one was open for 1% of the time, Pallas kernels for 0%

commit v1 on v0

v1 whole, which is shorter than its diff:
```python
import functools

import jax
import jax.numpy as jnp
import numpy as np
from jax import lax
from jax.experimental import pallas as pl
from jax.experimental.pallas import tpu as pltpu
from jax.sharding import PartitionSpec as P

LOOK_R = 4
LOOK_C = 16
LANES = 128
CHUNKS = 4
SLOT_PAD = 8
HIGHEST = lax.Precision.HIGHEST

ATAN = (
    0.0030499680532062342, -0.016827448459262765, 0.04385559893448732,
    -0.07596809856148054, 0.1068142102724691, -0.14213196195363814,
    0.19993716142481088, -0.33333120780995057, 0.9999999880828068,
)


def atan_ratio(imag, real):
    size = jnp.abs(imag)
    steep = size > real
    ratio = jnp.minimum(size, real) / jnp.maximum(size, real)
    square = ratio * ratio
    poly = jnp.full_like(square, ATAN[0])
    for coefficient in ATAN[1:]:
        poly = poly * square + coefficient
    angle = poly * ratio
    angle = jnp.where(steep, np.float32(np.pi / 2) - angle, angle)
    return jnp.where(imag < 0, -angle, angle)


def phase_kernel(pairs_ref, low_ref, own_ref, high_ref, ones_ref, out_ref, stack, sums):
    pair_count = pairs_ref.shape[0]
    acq = own_ref.shape[0]
    rows = own_ref.shape[2]
    looked = rows // LOOK_R
    blocks = own_ref.shape[3] // LANES

    def column_block(j, carry):
        lanes = pl.ds(pl.multiple_of(j * LANES, LANES), LANES)
        for side, ref in enumerate((low_ref, own_ref, high_ref)):
            for a in range(acq):
                for part in range(2):
                    stack[side * acq + a, part] = ref[a, part, :, lanes].astype(jnp.float32)
        for p in range(pair_count):
            first, second = pairs_ref[p, 0], pairs_ref[p, 1]
            real = imag = None
            for i in range(LOOK_R):
                pick = pl.ds(i, looked, stride=LOOK_R)
                ar, ai = stack[first, 0, pick, :], stack[first, 1, pick, :]
                cr, ci = stack[second, 0, pick, :], stack[second, 1, pick, :]
                re, im = ar * cr + ai * ci, ai * cr - ar * ci
                real = re if real is None else real + re
                imag = im if imag is None else imag + im
            sums[pl.ds(p * looked, looked), lanes] = real
            sums[pl.ds((pair_count + p) * looked, looked), lanes] = imag
        return carry

    lax.fori_loop(0, blocks, column_block, 0)
    both = jnp.dot(sums[...], ones_ref[...], precision=HIGHEST, preferred_element_type=jnp.float32)
    half = pair_count * looked
    angle = atan_ratio(both[half:], both[:half])
    out_ref[...] = jnp.zeros_like(out_ref)
    for p in range(pair_count):
        out_ref[:, p, :] = angle[p * looked : (p + 1) * looked]


def chunk_phase(pairs, low, scenes, high, ones, k):
    acq, parts, rows, cols = low.shape
    looked = rows // LOOK_R
    pair_count = pairs.shape[0]
    whole = pl.BlockSpec((acq, parts, rows, cols), lambda i: (0, 0, 0, 0))
    return pl.pallas_call(
        phase_kernel,
        grid=(1,),
        out_shape=jax.ShapeDtypeStruct((looked, SLOT_PAD, cols // LOOK_C), jnp.float32),
        in_specs=[
            pl.BlockSpec(memory_space=pltpu.SMEM),
            whole,
            pl.BlockSpec((acq, parts, rows, cols), lambda i: (0, 0, k, 0)),
            whole,
            pl.BlockSpec((cols, cols // LOOK_C), lambda i: (0, 0)),
        ],
        out_specs=pl.BlockSpec((looked, SLOT_PAD, cols // LOOK_C), lambda i: (0, 0, 0)),
        scratch_shapes=[
            pltpu.VMEM((3 * acq, parts, rows, LANES), jnp.float32),
            pltpu.VMEM((2 * pair_count * looked, cols), jnp.float32),
        ],
        compiler_params=pltpu.CompilerParams(vmem_limit_bytes=48 * 2**20),
        name="pair_phase",
    )(pairs, low, scenes, high, ones)


def slots_kernel(owner_ref, pinv_ref, out_ref):
    count = pinv_ref.shape[1]
    row = lax.broadcasted_iota(jnp.int32, (count, owner_ref.shape[1]), 0)
    pick = (row == owner_ref[...]).astype(jnp.float32)
    out_ref[...] = jnp.dot(pinv_ref[...], pick, precision=HIGHEST, preferred_element_type=jnp.float32)


def series_kernel(slots_ref, phase_ref, out_ref):
    phase = phase_ref[...].reshape(slots_ref.shape[1], phase_ref.shape[2])
    out_ref[...] = jnp.dot(
        slots_ref[...], phase, precision=HIGHEST, preferred_element_type=jnp.float32
    )[None]


def body(scenes, pairs, pair_owner, design_pinv):
    acq, parts, rows, cols = scenes.shape
    pair_count = pairs.shape[0]
    count = lax.axis_size("acq")
    local = pairs - (lax.axis_index("acq") - 1) * acq
    forward = [(i, i + 1) for i in range(count - 1)]
    backward = [(t, s) for s, t in forward]
    ones = (
        lax.broadcasted_iota(jnp.int32, (cols, cols // LOOK_C), 0) // LOOK_C
        == lax.broadcasted_iota(jnp.int32, (cols, cols // LOOK_C), 1)
    ).astype(jnp.float32)

    owner = jnp.pad(pair_owner.reshape(count, pair_count), ((0, 0), (0, SLOT_PAD - pair_count)), constant_values=-1)
    slots = pl.pallas_call(
        slots_kernel,
        out_shape=jax.ShapeDtypeStruct((design_pinv.shape[0], count * SLOT_PAD), jnp.float32),
        name="slot_pinv",
    )(owner.reshape(1, count * SLOT_PAD), design_pinv)

    step = rows // CHUNKS
    phases = []
    for k in range(CHUNKS):
        chunk = lax.slice_in_dim(scenes, k * step, (k + 1) * step, axis=2)
        low = lax.ppermute(chunk, "acq", forward)
        high = lax.ppermute(chunk, "acq", backward)
        phases.append(chunk_phase(local, low, scenes, high, ones, k))
    phase = jnp.concatenate(phases, axis=0)
    phase = lax.all_to_all(phase, "acq", split_axis=0, concat_axis=0)
    return pl.pallas_call(
        series_kernel,
        out_shape=jax.ShapeDtypeStruct((1, slots.shape[0], phase.shape[2]), jnp.float32),
        name="series",
    )(slots, phase)


def solution(mesh):
    placed = (P("acq", None, None, "rng"), P("acq", None), P(), P())
    return jax.shard_map(
        body, mesh=mesh, in_specs=placed, out_specs=P("acq", None, "rng"), check_vma=False
    )
```

time: 497 us -> 94.4 us (0.19); the launches traced: 491 us -> 93.9 us
  waiting for transfers between devices: 187 us -> 25.5 us
  other arithmetic: 129 us -> 1.6 us
  local copies, waits for them, and re-layouts: 124 us -> 7.91 us
  starting transfers between devices: 7.07 us -> 35 us
  Pallas kernels: 0 us -> 23.7 us
  loops' own time: 23 us -> 0 us
  between operations: 13.4 us -> 0.19 us
  matrix products: 8.23 us -> 0 us
    unnamed x2 -> x0, waiting for transfers between devices: 145 us -> none
    reduce_sum x12 -> x0, other arithmetic: 83.7 us -> none  [multilook(): values.reshape(rows // LOOK_R, LOOK_R, cols // LOOK_C, LOOK_C)]
    sub x6 -> x0, local copies, waits for them, and re-layouts: 62.2 us -> none  [one_pair(): imag_part = first[1] * second[0] - first[0] * second[1]]
    add x6 -> x0, local copies, waits for them, and re-layouts: 53.8 us -> none  [one_pair(): real_part = first[0] * second[0] + first[1] * second[1]]
    ppermute x2 -> x8, waiting for transfers between devices: 42.6 us -> 15.5 us  [the longest x4 8.95 us: body(): high = lax.ppermute(chunk, 'acq', backward)]
    pallas_call x0 -> x6, Pallas kernels: none -> 23.7 us  [the longest x4 19.4 us: chunk_phase(): pl.pallas_call(phase_kernel, grid=(1,), out_shape=jax.ShapeDtypeStruct((l...]
    another operation x1 -> x0, loops' own time: 23 us -> none  [pair_phases(): return lax.map(one_pair, pair_rows)]
    convert_element_type x6 -> x1, other arithmetic: 19.8 us -> 0.87 us  [body(): ones = (lax.broadcasted_iota(jnp.int32, (cols, cols // LOOK_C), 0) // LOO...]
  transfers between devices with their start and end apart: 3 -> 9, of which waited for: 3 -> 7; matrix products, arithmetic and copies ran while one was open for 1% -> 2% of each run, Pallas kernels for 0% -> 18%
where the time goes in v1:
time: 94.4 us; the launch traced here: 93.9 us
  starting transfers between devices  35 us (37%)
  waiting for transfers between devices  25.5 us (27%)
  Pallas kernels  23.7 us (25%)
  local copies, waits for them, and re-layouts  7.91 us (8%)
  other arithmetic  1.6 us (2%)
    pallas_call x4, Pallas kernels, chunk_phase(): pl.pallas_call(phase_kernel, grid=(1,), out_shape=jax.ShapeDtypeStruct((l...  19.4 us
    all_to_all x1, starting transfers between devices, body(): phase = lax.all_to_all(phase, 'acq', split_axis=0, concat_axis=0)  13.6 us
    ppermute x4, starting transfers between devices, body(): low = lax.ppermute(chunk, 'acq', forward)  13.6 us
    all_to_all x1, waiting for transfers between devices, body(): phase = lax.all_to_all(phase, 'acq', split_axis=0, concat_axis=0)  10 us
    ppermute x4, waiting for transfers between devices, body(): high = lax.ppermute(chunk, 'acq', backward)  8.95 us
    ppermute x4, starting transfers between devices, body(): high = lax.ppermute(chunk, 'acq', backward)  7.74 us
    ppermute x4, waiting for transfers between devices, body(): low = lax.ppermute(chunk, 'acq', forward)  6.53 us
    slice x1, local copies, waits for them, and re-layouts, body(): chunk = lax.slice_in_dim(scenes, k * step, (k + 1) * step, axis=2)  4.04 us
  transfers between devices with their start and end apart: 9, of which 7 were waited for; matrix products, arithmetic and copies ran while one was open for 2% of the time, Pallas kernels for 18%

profile of v1, /device:TPU:1, one launch (start us, length us, event | category | flops | bytes accessed | tf_op | source)
XLA Modules:
  0.0 93.9 jit_solution(17510678254835332085)
XLA Ops:
  0.0 4.0 %fusion.4 = (bf16[2,2,64,2048]{3,2,1,0:T(8,128)(2,1)}, bf16[2,2,64,2048]{3,2,1,0:T(8,128)(2,1)}, bf16[2,2,64,2048]{3,2,1,0:T(8,128)(2,1)}, bf16[2,2,64,2048]{3,2,1,0:T(8,128)(2,1)S(1)}) fusion(bf16[2,2,256,2048]{3,2,1,0:T(8,128)(2,1)} %own_ref.7), kind=kLoop, calls=%fused_computation.11 | loop fusion | bytes 8388608 | tf_op jit(solution)/shard_map/slice | solution.py:136
  4.0 4.5 %collective-permute-start.6 = (bf16[2,2,64,2048]{3,2,1,0:T(8,128)(2,1)S(1)}, bf16[2,2,64,2048]{3,2,1,0:T(8,128)(2,1)S(1)}, u32[]{:S(2)}, u32[]{:S(2)}) collective-permute-start(bf16[2,2,64,2048]{3,2,1,0:T(8,128)(2,1)S(1)} %get-tuple-element.8), channel_id=1, source_target_pairs={{0,4},{4,8},{8,12},{12,16},{16,20},{20,24},{24,28},{28,32},{32,36}... | collective-permute-start | bytes 3145736 | tf_op jit(solution)/shard_map/ppermute | solution.py:137
  8.5 2.0 %collective-permute-start.7 = (bf16[2,2,64,2048]{3,2,1,0:T(8,128)(2,1)S(1)}, bf16[2,2,64,2048]{3,2,1,0:T(8,128)(2,1)S(1)}, u32[]{:S(2)}, u32[]{:S(2)}) collective-permute-start(bf16[2,2,64,2048]{3,2,1,0:T(8,128)(2,1)S(1)} %get-tuple-element.8), channel_id=1, source_target_pairs={{4,0},{8,4},{12,8},{16,12},{20,16},{24,20},{28,24},{32,28},{36,32}... | collective-permute-start | bytes 3145736 | tf_op jit(solution)/shard_map/ppermute | solution.py:138
  10.6 3.6 %collective-permute-start.4 = (bf16[2,2,64,2048]{3,2,1,0:T(8,128)(2,1)}, bf16[2,2,64,2048]{3,2,1,0:T(8,128)(2,1)S(1)}, u32[]{:S(2)}, u32[]{:S(2)}) collective-permute-start(bf16[2,2,64,2048]{3,2,1,0:T(8,128)(2,1)} %get-tuple-element.6), channel_id=1, source_target_pairs={{0,4},{4,8},{8,12},{12,16},{16,20},{20,24},{24,28},{28,32},{32,36}... | collective-permute-start | bytes 3145736 | tf_op jit(solution)/shard_map/ppermute | solution.py:137
  14.1 1.9 %collective-permute-start.5 = (bf16[2,2,64,2048]{3,2,1,0:T(8,128)(2,1)}, bf16[2,2,64,2048]{3,2,1,0:T(8,128)(2,1)}, u32[]{:S(2)}, u32[]{:S(2)}) collective-permute-start(bf16[2,2,64,2048]{3,2,1,0:T(8,128)(2,1)} %get-tuple-element.6), channel_id=1, source_target_pairs={{4,0},{8,4},{12,8},{16,12},{20,16},{24,20},{28,24},{32,28},{36,32}... | collective-permute-start | bytes 3145736 | tf_op jit(solution)/shard_map/ppermute | solution.py:138
  16.1 3.6 %collective-permute-start.2 = (bf16[2,2,64,2048]{3,2,1,0:T(8,128)(2,1)}, bf16[2,2,64,2048]{3,2,1,0:T(8,128)(2,1)S(1)}, u32[]{:S(2)}, u32[]{:S(2)}) collective-permute-start(bf16[2,2,64,2048]{3,2,1,0:T(8,128)(2,1)} %get-tuple-element.7), channel_id=1, source_target_pairs={{0,4},{4,8},{8,12},{12,16},{16,20},{20,24},{24,28},{28,32},{32,36}... | collective-permute-start | bytes 3145736 | tf_op jit(solution)/shard_map/ppermute | solution.py:137
  20.3 1.9 %collective-permute-start.3 = (bf16[2,2,64,2048]{3,2,1,0:T(8,128)(2,1)}, bf16[2,2,64,2048]{3,2,1,0:T(8,128)(2,1)}, u32[]{:S(2)}, u32[]{:S(2)}) collective-permute-start(bf16[2,2,64,2048]{3,2,1,0:T(8,128)(2,1)} %get-tuple-element.7), channel_id=1, source_target_pairs={{4,0},{8,4},{12,8},{16,12},{20,16},{24,20},{28,24},{32,28},{36,32}... | collective-permute-start | bytes 3145736 | tf_op jit(solution)/shard_map/ppermute | solution.py:138
  22.2 2.5 %collective-permute-done.7.high_ref = bf16[2,2,64,2048]{3,2,1,0:T(8,128)(2,1)S(1)} collective-permute-done((bf16[2,2,64,2048]{3,2,1,0:T(8,128)(2,1)S(1)}, bf16[2,2,64,2048]{3,2,1,0:T(8,128)(2,1)S(1)}, u32[]{:S(2)}, u32[]{:S(2)}) %collective-permute-start.7) | collective-permute-done | bytes 1048608 | tf_op jit(solution)/shard_map/ppermute | solution.py:138
  24.7 1.0 %copy-done = bf16[2,2,64,2048]{3,2,1,0:T(8,128)(2,1)} copy-done((bf16[2,2,64,2048]{3,2,1,0:T(8,128)(2,1)}, bf16[2,2,64,2048]{3,2,1,0:T(8,128)(2,1)S(1)}, u32[]{:S(2)}) %copy-start) | copy-done | bytes 1048600
  25.7 1.9 %collective-permute-start = (bf16[2,2,64,2048]{3,2,1,0:T(8,128)(2,1)}, bf16[2,2,64,2048]{3,2,1,0:T(8,128)(2,1)}, u32[]{:S(2)}, u32[]{:S(2)}) collective-permute-start(bf16[2,2,64,2048]{3,2,1,0:T(8,128)(2,1)} %get-tuple-element.5), channel_id=1, source_target_pairs={{0,4},{4,8},{8,12},{12,16},{16,20},{20,24},{24,28},{28,32},{32,36}... | collective-permute-start | bytes 3145736 | tf_op jit(solution)/shard_map/ppermute | solution.py:137
  27.6 4.0 %collective-permute-done.4.low_ref = bf16[2,2,64,2048]{3,2,1,0:T(8,128)(2,1)S(1)} collective-permute-done((bf16[2,2,64,2048]{3,2,1,0:T(8,128)(2,1)}, bf16[2,2,64,2048]{3,2,1,0:T(8,128)(2,1)S(1)}, u32[]{:S(2)}, u32[]{:S(2)}) %collective-permute-start.4) | collective-permute-done | bytes 1048608 | tf_op jit(solution)/shard_map/ppermute | solution.py:137
  31.6 1.9 %collective-permute-start.1 = (bf16[2,2,64,2048]{3,2,1,0:T(8,128)(2,1)}, bf16[2,2,64,2048]{3,2,1,0:T(8,128)(2,1)}, u32[]{:S(2)}, u32[]{:S(2)}) collective-permute-start(bf16[2,2,64,2048]{3,2,1,0:T(8,128)(2,1)} %get-tuple-element.5), channel_id=1, source_target_pairs={{4,0},{8,4},{12,8},{16,12},{20,16},{24,20},{28,24},{32,28},{36,32}... | collective-permute-start | bytes 3145736 | tf_op jit(solution)/shard_map/ppermute | solution.py:138
  34.6 1.2 %copy-done.1 = bf16[2,2,64,2048]{3,2,1,0:T(8,128)(2,1)S(1)} copy-done((bf16[2,2,64,2048]{3,2,1,0:T(8,128)(2,1)S(1)}, bf16[2,2,64,2048]{3,2,1,0:T(8,128)(2,1)}, u32[]{:S(2)}) %copy-start.1) | copy-done | bytes 1048600
  35.8 4.5 %pair_phase.7 = f32[16,8,128]{2,1,0:T(8,128)S(1)} custom-call(s32[6,2]{1,0:T(8,128)S(1)} %broadcast_subtract_fusion.pairs_ref, bf16[2,2,64,2048]{3,2,1,0:T(8,128)(2,1)S(1)} %collective-permute-done.6.low_ref, bf16[2,2,256,2048]{3,2,1,0:T(8,128)(2,1)} %own_ref.7, bf16[2,2,64,2048]{3,2,1,0:T(8,128)(2,1)S(1)} %copy-done.1, f32[2048,128]{1,0:T(8,128)S(1)} %fusion.ones_ref), custom_call_target="tpu_custom_call" | custom-call | tf_op jit(solution)/shard_map/pair_phase/pallas_call | solution.py:79
  40.3 4.8 %pair_phase.6 = f32[16,8,128]{2,1,0:T(8,128)S(1)} custom-call(s32[6,2]{1,0:T(8,128)S(1)} %broadcast_subtract_fusion.pairs_ref, bf16[2,2,64,2048]{3,2,1,0:T(8,128)(2,1)S(1)} %collective-permute-done.4.low_ref, bf16[2,2,256,2048]{3,2,1,0:T(8,128)(2,1)} %own_ref.7, bf16[2,2,64,2048]{3,2,1,0:T(8,128)(2,1)} %collective-permute-done.5.high_ref, ...), custom_call_target="tpu_custom_call" | custom-call | tf_op jit(solution)/shard_map/pair_phase/pallas_call | solution.py:79
  45.2 2.1 %collective-permute-done.3.high_ref = bf16[2,2,64,2048]{3,2,1,0:T(8,128)(2,1)} collective-permute-done((bf16[2,2,64,2048]{3,2,1,0:T(8,128)(2,1)}, bf16[2,2,64,2048]{3,2,1,0:T(8,128)(2,1)}, u32[]{:S(2)}, u32[]{:S(2)}) %collective-permute-start.3) | collective-permute-done | bytes 1048608 | tf_op jit(solution)/shard_map/ppermute | solution.py:138
  47.2 4.8 %pair_phase.5 = f32[16,8,128]{2,1,0:T(8,128)S(1)} custom-call(s32[6,2]{1,0:T(8,128)S(1)} %broadcast_subtract_fusion.pairs_ref, bf16[2,2,64,2048]{3,2,1,0:T(8,128)(2,1)S(1)} %collective-permute-done.2.low_ref, bf16[2,2,256,2048]{3,2,1,0:T(8,128)(2,1)} %own_ref.7, bf16[2,2,64,2048]{3,2,1,0:T(8,128)(2,1)} %collective-permute-done.3.high_ref, ...), custom_call_target="tpu_custom_call" | custom-call | tf_op jit(solution)/shard_map/pair_phase/pallas_call | solution.py:79
  52.1 2.0 %collective-permute-done.low_ref = bf16[2,2,64,2048]{3,2,1,0:T(8,128)(2,1)} collective-permute-done((bf16[2,2,64,2048]{3,2,1,0:T(8,128)(2,1)}, bf16[2,2,64,2048]{3,2,1,0:T(8,128)(2,1)}, u32[]{:S(2)}, u32[]{:S(2)}) %collective-permute-start) | collective-permute-done | bytes 1048608 | tf_op jit(solution)/shard_map/ppermute | solution.py:137
  54.1 4.4 %collective-permute-done.1.high_ref = bf16[2,2,64,2048]{3,2,1,0:T(8,128)(2,1)} collective-permute-done((bf16[2,2,64,2048]{3,2,1,0:T(8,128)(2,1)}, bf16[2,2,64,2048]{3,2,1,0:T(8,128)(2,1)}, u32[]{:S(2)}, u32[]{:S(2)}) %collective-permute-start.1) | collective-permute-done | bytes 1048608 | tf_op jit(solution)/shard_map/ppermute | solution.py:138
  58.5 5.2 %pair_phase.4 = f32[16,8,128]{2,1,0:T(8,128)S(1)} custom-call(s32[6,2]{1,0:T(8,128)S(1)} %broadcast_subtract_fusion.pairs_ref, bf16[2,2,64,2048]{3,2,1,0:T(8,128)(2,1)} %collective-permute-done.low_ref, bf16[2,2,256,2048]{3,2,1,0:T(8,128)(2,1)} %own_ref.7, bf16[2,2,64,2048]{3,2,1,0:T(8,128)(2,1)} %collective-permute-done.1.high_ref, ...), custom_call_target="tpu_custom_call" | custom-call | tf_op jit(solution)/shard_map/pair_phase/pallas_call | solution.py:79
  64.4 13.6 %all-to-all-start = ((f32[64,8,128]{2,1,0:T(8,128)}), f32[64,8,128]{2,1,0:T(8,128)S(1)}, u32[]{:S(2)}, u32[]{:S(2)}) async-start(f32[64,8,128]{2,1,0:T(8,128)} %pad_maximum_fusion), calls=%async_computation | async-start | bytes 524288 | tf_op jit(solution)/shard_map/all_to_all | solution.py:141
  78.8 2.3 %slot_pinv.1.slots_ref = f32[128,512]{1,0:T(8,128)} custom-call(s32[1,512]{1,0:T(1,128)} %reshape.7.owner_ref, f32[128,384]{1,0:T(8,128)} %pinv_ref.1), custom_call_target="tpu_custom_call" | custom-call | tf_op jit(solution)/shard_map/slot_pinv/pallas_call | solution.py:127
  81.1 10.0 %all-to-all-done.phase_ref = f32[64,8,128]{2,1,0:T(8,128)S(1)} async-done(((f32[64,8,128]{2,1,0:T(8,128)}), f32[64,8,128]{2,1,0:T(8,128)S(1)}, u32[]{:S(2)}, u32[]{:S(2)}) %all-to-all-start) | async-done | bytes 262176 | tf_op jit(solution)/shard_map/all_to_all | solution.py:141
  91.9 2.0 %series.1 = f32[1,128,128]{2,1,0:T(8,128)} custom-call(f32[128,512]{1,0:T(8,128)} %slot_pinv.1.slots_ref, f32[64,8,128]{2,1,0:T(8,128)} %copy-done.2), custom_call_target="tpu_custom_call" | custom-call | tf_op jit(solution)/shard_map/series/pallas_call | solution.py:142
  (20 shorter events, 3.8 us)
Async XLA Ops:
  0.0 33.5 %copy-start.4 = (s32[6,2]{0,1:T(2,128)S(1)}, s32[6,2]{0,1:T(2,128)}, u32[]{:S(2)}) copy-start(s32[6,2]{0,1:T(2,128)} %param.5) | copy-start | bytes 148
  4.0 16.2 %collective-permute-start.6 = (bf16[2,2,64,2048]{3,2,1,0:T(8,128)(2,1)S(1)}, bf16[2,2,64,2048]{3,2,1,0:T(8,128)(2,1)S(1)}, u32[]{:S(2)}, u32[]{:S(2)}) collective-permute-start(bf16[2,2,64,2048]{3,2,1,0:T(8,128)(2,1)S(1)} %get-tuple-element.8), channel_id=1, source_target_pairs={{0,4},{4,8},{8,12},{12,16},{16,20},{20,24},{24,28},{28,32},{32,36}... | collective-permute-start | bytes 3145736 | tf_op jit(solution)/shard_map/ppermute | solution.py:137
  8.5 16.1 %collective-permute-start.7 = (bf16[2,2,64,2048]{3,2,1,0:T(8,128)(2,1)S(1)}, bf16[2,2,64,2048]{3,2,1,0:T(8,128)(2,1)S(1)}, u32[]{:S(2)}, u32[]{:S(2)}) collective-permute-start(bf16[2,2,64,2048]{3,2,1,0:T(8,128)(2,1)S(1)} %get-tuple-element.8), channel_id=1, source_target_pairs={{4,0},{8,4},{12,8},{16,12},{20,16},{24,20},{28,24},{32,28},{36,32}... | collective-permute-start | bytes 3145736 | tf_op jit(solution)/shard_map/ppermute | solution.py:138
  10.6 21.1 %collective-permute-start.4 = (bf16[2,2,64,2048]{3,2,1,0:T(8,128)(2,1)}, bf16[2,2,64,2048]{3,2,1,0:T(8,128)(2,1)S(1)}, u32[]{:S(2)}, u32[]{:S(2)}) collective-permute-start(bf16[2,2,64,2048]{3,2,1,0:T(8,128)(2,1)} %get-tuple-element.6), channel_id=1, source_target_pairs={{0,4},{4,8},{8,12},{12,16},{16,20},{20,24},{24,28},{28,32},{32,36}... | collective-permute-start | bytes 3145736 | tf_op jit(solution)/shard_map/ppermute | solution.py:137
  14.1 26.2 %collective-permute-start.5 = (bf16[2,2,64,2048]{3,2,1,0:T(8,128)(2,1)}, bf16[2,2,64,2048]{3,2,1,0:T(8,128)(2,1)}, u32[]{:S(2)}, u32[]{:S(2)}) collective-permute-start(bf16[2,2,64,2048]{3,2,1,0:T(8,128)(2,1)} %get-tuple-element.6), channel_id=1, source_target_pairs={{4,0},{8,4},{12,8},{16,12},{20,16},{24,20},{28,24},{32,28},{36,32}... | collective-permute-start | bytes 3145736 | tf_op jit(solution)/shard_map/ppermute | solution.py:138
  16.1 29.1 %collective-permute-start.2 = (bf16[2,2,64,2048]{3,2,1,0:T(8,128)(2,1)}, bf16[2,2,64,2048]{3,2,1,0:T(8,128)(2,1)S(1)}, u32[]{:S(2)}, u32[]{:S(2)}) collective-permute-start(bf16[2,2,64,2048]{3,2,1,0:T(8,128)(2,1)} %get-tuple-element.7), channel_id=1, source_target_pairs={{0,4},{4,8},{8,12},{12,16},{16,20},{20,24},{24,28},{28,32},{32,36}... | collective-permute-start | bytes 3145736 | tf_op jit(solution)/shard_map/ppermute | solution.py:137
  20.3 27.0 %collective-permute-start.3 = (bf16[2,2,64,2048]{3,2,1,0:T(8,128)(2,1)}, bf16[2,2,64,2048]{3,2,1,0:T(8,128)(2,1)}, u32[]{:S(2)}, u32[]{:S(2)}) collective-permute-start(bf16[2,2,64,2048]{3,2,1,0:T(8,128)(2,1)} %get-tuple-element.7), channel_id=1, source_target_pairs={{4,0},{8,4},{12,8},{16,12},{20,16},{24,20},{28,24},{32,28},{36,32}... | collective-permute-start | bytes 3145736 | tf_op jit(solution)/shard_map/ppermute | solution.py:138
  24.7 1.0 %copy-start = (bf16[2,2,64,2048]{3,2,1,0:T(8,128)(2,1)}, bf16[2,2,64,2048]{3,2,1,0:T(8,128)(2,1)S(1)}, u32[]{:S(2)}) copy-start(bf16[2,2,64,2048]{3,2,1,0:T(8,128)(2,1)S(1)} %collective-permute-done.7.high_ref) | copy-start | bytes 3145732
  25.7 28.4 %collective-permute-start = (bf16[2,2,64,2048]{3,2,1,0:T(8,128)(2,1)}, bf16[2,2,64,2048]{3,2,1,0:T(8,128)(2,1)}, u32[]{:S(2)}, u32[]{:S(2)}) collective-permute-start(bf16[2,2,64,2048]{3,2,1,0:T(8,128)(2,1)} %get-tuple-element.5), channel_id=1, source_target_pairs={{0,4},{4,8},{8,12},{12,16},{16,20},{20,24},{24,28},{28,32},{32,36}... | collective-permute-start | bytes 3145736 | tf_op jit(solution)/shard_map/ppermute | solution.py:137
  31.6 26.9 %collective-permute-start.1 = (bf16[2,2,64,2048]{3,2,1,0:T(8,128)(2,1)}, bf16[2,2,64,2048]{3,2,1,0:T(8,128)(2,1)}, u32[]{:S(2)}, u32[]{:S(2)}) collective-permute-start(bf16[2,2,64,2048]{3,2,1,0:T(8,128)(2,1)} %get-tuple-element.5), channel_id=1, source_target_pairs={{4,0},{8,4},{12,8},{16,12},{20,16},{24,20},{28,24},{32,28},{36,32}... | collective-permute-start | bytes 3145736 | tf_op jit(solution)/shard_map/ppermute | solution.py:138
  34.5 1.2 %copy-start.1 = (bf16[2,2,64,2048]{3,2,1,0:T(8,128)(2,1)S(1)}, bf16[2,2,64,2048]{3,2,1,0:T(8,128)(2,1)}, u32[]{:S(2)}) copy-start(bf16[2,2,64,2048]{3,2,1,0:T(8,128)(2,1)} %copy-done) | copy-start | bytes 3145732
  52.1 25.9 %copy-start.3 = (s32[384]{0:T(512)S(1)}, s32[384]{0:T(512)}, u32[]{:S(2)}) copy-start(s32[384]{0:T(512)} %param.6) | copy-start | bytes 4612
  64.4 26.8 %all-to-all-start = ((f32[64,8,128]{2,1,0:T(8,128)}), f32[64,8,128]{2,1,0:T(8,128)S(1)}, u32[]{:S(2)}, u32[]{:S(2)}) async-start(f32[64,8,128]{2,1,0:T(8,128)} %pad_maximum_fusion), calls=%async_computation | async-start | bytes 524288 | tf_op jit(solution)/shard_map/all_to_all | solution.py:141
  91.2 0.7 copy-start.2

commit v2 on v1

v2 whole, which is shorter than its diff:
```python
import jax
import jax.numpy as jnp
import numpy as np
from jax import lax
from jax.experimental import pallas as pl
from jax.experimental.pallas import tpu as pltpu
from jax.sharding import PartitionSpec as P

LOOK_R = 4
LOOK_C = 16
LANES = 128
CHUNKS = (64, 64, 96, 32)
SLOT_PAD = 8
UNROLL_A = 2
UNROLL_B = 2

ATAN = (
    0.0030499680532062342, -0.016827448459262765, 0.04385559893448732,
    -0.07596809856148054, 0.1068142102724691, -0.14213196195363814,
    0.19993716142481088, -0.33333120780995057, 0.9999999880828068,
)


def atan_ratio(imag, real):
    size = jnp.abs(imag)
    steep = size > real
    ratio = jnp.minimum(size, real) / jnp.maximum(size, real)
    square = ratio * ratio
    poly = jnp.full_like(square, ATAN[0])
    for coefficient in ATAN[1:]:
        poly = poly * square + coefficient
    angle = poly * ratio
    angle = jnp.where(steep, np.float32(np.pi / 2) - angle, angle)
    return jnp.where(imag < 0, -angle, angle)


def cut_kernel(scenes_ref, *refs):
    *outs, sems = refs
    copies, start = [], 0
    for k, out in enumerate(outs):
        rows = out.shape[2]
        copy = pltpu.make_async_copy(scenes_ref.at[:, :, pl.ds(start, rows), :], out, sems.at[k])
        copy.start()
        copies.append(copy)
        start += rows
    for copy in copies:
        copy.wait()


def cut_rows(scenes):
    acq, parts, _, cols = scenes.shape
    anywhere = pl.BlockSpec(memory_space=pl.ANY)
    return pl.pallas_call(
        cut_kernel,
        out_shape=[jax.ShapeDtypeStruct((acq, parts, rows, cols), scenes.dtype) for rows in CHUNKS],
        in_specs=[anywhere],
        out_specs=[anywhere] * len(CHUNKS),
        scratch_shapes=[pltpu.SemaphoreType.DMA((len(CHUNKS),))],
        name="cut_rows",
    )(scenes)


def split(x):
    high = x.astype(jnp.bfloat16)
    rest = x - high.astype(jnp.float32)
    mid = rest.astype(jnp.bfloat16)
    return high, mid, (rest - mid.astype(jnp.float32)).astype(jnp.bfloat16)


def phase_kernel(pairs_ref, low_ref, own_ref, high_ref, ones_ref, *refs):
    *earlier, out_ref, stack, sums = refs
    pair_count = pairs_ref.shape[0]
    acq, _, rows, cols = own_ref.shape
    looked = rows // LOOK_R
    blocks = cols // LANES

    def widen(j, carry):
        lanes = pl.ds(pl.multiple_of(j * LANES, LANES), LANES)
        for side, ref in enumerate((low_ref, own_ref, high_ref)):
            for a in range(acq):
                for part in range(2):
                    stack[side * acq + a, part, j] = ref[a, part, :, lanes].astype(jnp.float32)
        return carry

    lax.fori_loop(0, blocks, widen, 0, unroll=UNROLL_A)
    picks = [(pairs_ref[p, 0], pairs_ref[p, 1]) for p in range(pair_count)]

    def form(j, carry):
        lanes = pl.ds(pl.multiple_of(j * LANES, LANES), LANES)
        for p, (first, second) in enumerate(picks):
            real = imag = None
            for i in range(LOOK_R):
                pick = pl.ds(i, looked, stride=LOOK_R)
                ar, ai = stack[first, 0, j, pick, :], stack[first, 1, j, pick, :]
                cr, ci = stack[second, 0, j, pick, :], stack[second, 1, j, pick, :]
                re, im = ar * cr + ai * ci, ai * cr - ar * ci
                real = re if real is None else real + re
                imag = im if imag is None else imag + im
            for piece, value in enumerate(split(jnp.concatenate([real, imag], axis=0))):
                sums[piece, pl.ds(p * 2 * looked, 2 * looked), lanes] = value
        return carry

    lax.fori_loop(0, blocks, form, 0, unroll=UNROLL_B)
    pieces = sums[...].reshape(3 * sums.shape[1], cols)
    dots = jnp.dot(pieces, ones_ref[...], preferred_element_type=jnp.float32)
    dots = dots.reshape(3, pair_count, 2, looked, dots.shape[1])
    both = dots[0] + (dots[1] + dots[2])
    angle = atan_ratio(both[:, 1], both[:, 0])
    start = 0
    for ref in earlier:
        out_ref[pl.ds(start, ref.shape[0])] = ref[...]
        start += ref.shape[0]
    for p in range(pair_count):
        out_ref[pl.ds(start, looked), p, :] = angle[p]
    for p in range(pair_count, SLOT_PAD):
        out_ref[pl.ds(start, looked), p, :] = jnp.zeros_like(angle[0])


def chunk_phase(pairs, low, own, high, ones, earlier=()):
    acq, parts, rows, cols = low.shape
    looked = rows // LOOK_R
    pair_count = pairs.shape[0]
    total = looked + sum(x.shape[0] for x in earlier)
    vmem = pl.BlockSpec(memory_space=pltpu.VMEM)
    return pl.pallas_call(
        phase_kernel,
        out_shape=jax.ShapeDtypeStruct((total, SLOT_PAD, cols // LOOK_C), jnp.float32),
        in_specs=[pl.BlockSpec(memory_space=pltpu.SMEM)] + [vmem] * (4 + len(earlier)),
        out_specs=vmem,
        scratch_shapes=[
            pltpu.VMEM((3 * acq, parts, cols // LANES, rows, LANES), jnp.float32),
            pltpu.VMEM((3, 2 * pair_count * looked, cols), jnp.bfloat16),
        ],
        compiler_params=pltpu.CompilerParams(vmem_limit_bytes=28 * 2**20),
        name="pair_phase",
    )(pairs, low, own, high, ones, *earlier)


def slots_kernel(owner_ref, pinv_ref, out_ref):
    count = pinv_ref.shape[1]
    row = lax.broadcasted_iota(jnp.int32, (count, owner_ref.shape[1]), 0)
    pick = (row == owner_ref[...]).astype(jnp.bfloat16)
    for piece, value in enumerate(split(pinv_ref[...])):
        out_ref[piece] = jnp.dot(value, pick, preferred_element_type=jnp.float32).astype(jnp.bfloat16)


def series_kernel(slots_ref, phase_ref, out_ref):
    acqs, width = slots_ref.shape[1:]
    phase = split(phase_ref[...].reshape(width, phase_ref.shape[2]))
    total = None
    for piece in reversed(range(3)):
        rows = slots_ref[pl.ds(0, 3 - piece)].reshape((3 - piece) * acqs, width)
        dots = jnp.dot(rows, phase[piece], preferred_element_type=jnp.float32)
        for k in reversed(range(3 - piece)):
            part = dots[k * acqs : (k + 1) * acqs]
            total = part if total is None else total + part
    out_ref[0] = total


def body(scenes, pairs, pair_owner, design_pinv):
    acq, parts, rows, cols = scenes.shape
    pair_count = pairs.shape[0]
    count = lax.axis_size("acq")
    local = pairs - (lax.axis_index("acq") - 1) * acq
    forward = [(i, i + 1) for i in range(count - 1)]
    backward = [(t, s) for s, t in forward]

    chunks = cut_rows(scenes)
    halos = [(lax.ppermute(c, "acq", forward), lax.ppermute(c, "acq", backward)) for c in chunks]

    ones = (
        lax.broadcasted_iota(jnp.int32, (cols, cols // LOOK_C), 0) // LOOK_C
        == lax.broadcasted_iota(jnp.int32, (cols, cols // LOOK_C), 1)
    ).astype(jnp.bfloat16)
    owner = jnp.pad(pair_owner.reshape(count, pair_count), ((0, 0), (0, SLOT_PAD - pair_count)), constant_values=-1)
    slots = pl.pallas_call(
        slots_kernel,
        out_shape=jax.ShapeDtypeStruct((3, design_pinv.shape[0], count * SLOT_PAD), jnp.bfloat16),
        name="slot_pinv",
    )(owner.reshape(1, count * SLOT_PAD), design_pinv)

    phases = []
    for k, (chunk, (low, high)) in enumerate(zip(chunks, halos)):
        if k == 0:
            low, slots = lax.optimization_barrier((low, slots))
        last = k == len(chunks) - 1
        phases.append(chunk_phase(local, low, chunk, high, ones, phases if last else ()))
    phase = lax.all_to_all(phases[-1], "acq", split_axis=0, concat_axis=0)
    return pl.pallas_call(
        series_kernel,
        out_shape=jax.ShapeDtypeStruct((1, slots.shape[1], phase.shape[2]), jnp.float32),
        name="series",
    )(slots, phase)


def solution(mesh):
    placed = (P("acq", None, None, "rng"), P("acq", None), P(), P())
    return jax.shard_map(
        body, mesh=mesh, in_specs=placed, out_specs=P("acq", None, "rng"), check_vma=False
    )
```

time: 94.4 us -> 218 us (2.31)
  Pallas kernels: 23.7 us -> 149 us
  blocking collectives: 0 us -> 26.7 us
  starting transfers between devices: 35 us -> 22.6 us
  waiting for transfers between devices: 25.5 us -> 13.8 us
  local copies, waits for them, and re-layouts: 7.91 us -> 4.33 us
    pallas_call x5 -> x6, Pallas kernels: 21.7 us -> 147 us  [the longest x1 128 us: cut_rows(): pl.pallas_call(cut_kernel, out_shape=[jax.ShapeDtypeStruct((acq, parts, r...]
    all_to_all x0 -> x1, blocking collectives: none -> 26.7 us  [body(): phase = lax.all_to_all(phases[-1], 'acq', split_axis=0, concat_axis=0)]
    all_to_all x1 -> x0, starting transfers between devices: 13.6 us -> none  [body(): phase = lax.all_to_all(phase, 'acq', split_axis=0, concat_axis=0)]
    all_to_all x1 -> x0, waiting for transfers between devices: 10 us -> none  [body(): phase = lax.all_to_all(phase, 'acq', split_axis=0, concat_axis=0)]
    slice x1 -> x0, local copies, waits for them, and re-layouts: 4.04 us -> none  [body(): chunk = lax.slice_in_dim(scenes, k * step, (k + 1) * step, axis=2)]
  transfers between devices with their start and end apart: 9 -> 8, of which waited for: 7 -> 3; matrix products, arithmetic and copies ran while one was open for 2% -> 1% of each run, Pallas kernels for 18% -> 7%
where the time goes in v2:
time: 218 us
  Pallas kernels  149 us (68%)
  blocking collectives  26.7 us (12%)
  starting transfers between devices  22.6 us (10%)
  waiting for transfers between devices  13.8 us (6%)
  local copies, waits for them, and re-layouts  4.33 us (2%)
    pallas_call x1, Pallas kernels, cut_rows(): pl.pallas_call(cut_kernel, out_shape=[jax.ShapeDtypeStruct((acq, parts, r...  128 us
    all_to_all x1, blocking collectives, body(): phase = lax.all_to_all(phases[-1], 'acq', split_axis=0, concat_axis=0)  26.7 us
    pallas_call x4, Pallas kernels, chunk_phase(): pl.pallas_call(phase_kernel, out_shape=jax.ShapeDtypeStruct((total, SLOT_...  16.2 us
    ppermute x4, starting transfers between devices, body(): lax.ppermute(c, 'acq', forward)  14.3 us
    ppermute x4, waiting for transfers between devices, body(): lax.ppermute(c, 'acq', backward)  10.8 us
    ppermute x4, starting transfers between devices, body(): lax.ppermute(c, 'acq', backward)  8.32 us
  transfers between devices with their start and end apart: 8, of which 3 were waited for; matrix products, arithmetic and copies ran while one was open for 1% of the time, Pallas kernels for 7%

profile of v2, /device:TPU:1, one launch (start us, length us, event | category | flops | bytes accessed | tf_op | source)
XLA Modules:
  0.0 218.0 jit_solution(4031606253266315360)
XLA Ops:
  0.0 128.2 %cut_rows.1 = (bf16[2,2,64,2048]{3,2,1,0:T(8,128)(2,1)}, bf16[2,2,64,2048]{3,2,1,0:T(8,128)(2,1)}, bf16[2,2,96,2048]{3,2,1,0:T(8,128)(2,1)}, bf16[2,2,32,2048]{3,2,1,0:T(8,128)(2,1)}) custom-call(bf16[2,2,256,2048]{3,2,1,0:T(8,128)(2,1)} %scenes_ref.1), custom_call_target="tpu_custom_call" | custom-call | tf_op jit(solution)/shard_map/cut_rows/pallas_call | solution.py:53
  128.2 4.5 %collective-permute-start = (bf16[2,2,64,2048]{3,2,1,0:T(8,128)(2,1)}, bf16[2,2,64,2048]{3,2,1,0:T(8,128)(2,1)S(1)}, u32[]{:S(2)}, u32[]{:S(2)}) collective-permute-start(bf16[2,2,64,2048]{3,2,1,0:T(8,128)(2,1)} %get-tuple-element.11.own_ref), channel_id=1, source_target_pairs={{0,4},{4,8},{8,12},{12,16},{16,20},{20,24},{24,28},{28,32},{32,36}... | collective-permute-start | bytes 3145736 | tf_op jit(solution)/shard_map/ppermute | solution.py:169
  132.7 2.0 collective-permute-start.3
  134.7 3.6 %collective-permute-start.4 = (bf16[2,2,64,2048]{3,2,1,0:T(8,128)(2,1)}, bf16[2,2,64,2048]{3,2,1,0:T(8,128)(2,1)}, u32[]{:S(2)}, u32[]{:S(2)}) collective-permute-start(bf16[2,2,64,2048]{3,2,1,0:T(8,128)(2,1)} %get-tuple-element.15.own_ref), channel_id=1, source_target_pairs={{0,4},{4,8},{8,12},{12,16},{16,20},{20,24},{24,28},{28,32},{32,36}... | collective-permute-start | bytes 3145736 | tf_op jit(solution)/shard_map/ppermute | solution.py:169
  138.3 1.9 collective-permute-start.6
  140.2 2.5 %collective-permute-start.7 = (bf16[2,2,96,2048]{3,2,1,0:T(8,128)(2,1)}, bf16[2,2,96,2048]{3,2,1,0:T(8,128)(2,1)S(1)}, u32[]{:S(2)}, u32[]{:S(2)}) collective-permute-start(bf16[2,2,96,2048]{3,2,1,0:T(8,128)(2,1)} %get-tuple-element.16.own_ref), channel_id=1, source_target_pairs={{4,0},{8,4},{12,8},{16,12},{20,16},{24,20},{28,24},{32,28},{36,32}... | collective-permute-start | bytes 4718600 | tf_op jit(solution)/shard_map/ppermute | solution.py:169
  142.7 2.0 collective-permute-done.low_ref
  144.8 1.0 copy-done.3
  145.7 1.9 collective-permute-start.5
  147.8 0.7 reshape.7.owner_ref
  148.6 2.1 slot_pinv.1.slots_ref
  150.7 4.3 %collective-permute-start.1 = (bf16[2,2,32,2048]{3,2,1,0:T(8,128)(2,1)}, bf16[2,2,32,2048]{3,2,1,0:T(8,128)(2,1)S(1)}, u32[]{:S(2)}, u32[]{:S(2)}) collective-permute-start(bf16[2,2,32,2048]{3,2,1,0:T(8,128)(2,1)} %get-tuple-element.13.own_ref), channel_id=1, source_target_pairs={{0,4},{4,8},{8,12},{12,16},{16,20},{20,24},{24,28},{28,32},{32,36}... | collective-permute-start | bytes 1572872 | tf_op jit(solution)/shard_map/ppermute | solution.py:169
  155.0 1.0 collective-permute-done.4.low_ref
  156.0 1.9 collective-permute-start.2
  157.9 1.7 fusion.ones_ref
  159.6 1.2 copy-done.2
  160.9 1.2 copy-done.4
  162.1 4.3 %pair_phase.4.refs_0_ = f32[16,8,128]{2,1,0:T(8,128)S(1)} custom-call(s32[6,2]{1,0:T(8,128)S(1)} %broadcast_subtract_fusion.pairs_ref, bf16[2,2,64,2048]{3,2,1,0:T(8,128)(2,1)S(1)} %copy-done.4, bf16[2,2,64,2048]{3,2,1,0:T(8,128)(2,1)S(1)} %copy-done.2, bf16[2,2,64,2048]{3,2,1,0:T(8,128)(2,1)} %collective-permute-done.3.high_ref, ...), custom_call_target="tpu_custom_call" | custom-call | tf_op jit(solution)/shard_map/pair_phase/pallas_call | solution.py:125
  166.4 10.8 %collective-permute-done.5.high_ref = bf16[2,2,64,2048]{3,2,1,0:T(8,128)(2,1)} collective-permute-done((bf16[2,2,64,2048]{3,2,1,0:T(8,128)(2,1)}, bf16[2,2,64,2048]{3,2,1,0:T(8,128)(2,1)}, u32[]{:S(2)}, u32[]{:S(2)}) %collective-permute-start.5) | collective-permute-done | bytes 1048608 | tf_op jit(solution)/shard_map/ppermute | solution.py:169
  177.2 4.6 %pair_phase.5.refs_1_ = f32[16,8,128]{2,1,0:T(8,128)S(1)} custom-call(s32[6,2]{1,0:T(8,128)S(1)} %broadcast_subtract_fusion.pairs_ref, bf16[2,2,64,2048]{3,2,1,0:T(8,128)(2,1)} %collective-permute-done.4.low_ref, bf16[2,2,64,2048]{3,2,1,0:T(8,128)(2,1)S(1)} %copy-done.1, bf16[2,2,64,2048]{3,2,1,0:T(8,128)(2,1)} %collective-permute-done.5.high_ref, ...), custom_call_target="tpu_custom_call" | custom-call | tf_op jit(solution)/shard_map/pair_phase/pallas_call | solution.py:125
  181.9 5.0 %pair_phase.6.refs_2_ = f32[24,8,128]{2,1,0:T(8,128)S(1)} custom-call(s32[6,2]{1,0:T(8,128)S(1)} %broadcast_subtract_fusion.pairs_ref, bf16[2,2,96,2048]{3,2,1,0:T(8,128)(2,1)S(1)} %collective-permute-done.6.low_ref, bf16[2,2,96,2048]{3,2,1,0:T(8,128)(2,1)S(1)} %copy-done, bf16[2,2,96,2048]{3,2,1,0:T(8,128)(2,1)S(1)} %collective-permute-done.7.high_ref, ...), custom_call_target="tpu_custom_call" | custom-call | tf_op jit(solution)/shard_map/pair_phase/pallas_call | solution.py:125
  186.9 2.3 %pair_phase.7 = f32[64,8,128]{2,1,0:T(8,128)S(1)} custom-call(s32[6,2]{1,0:T(8,128)S(1)} %broadcast_subtract_fusion.pairs_ref, bf16[2,2,32,2048]{3,2,1,0:T(8,128)(2,1)S(1)} %collective-permute-done.1.low_ref, bf16[2,2,32,2048]{3,2,1,0:T(8,128)(2,1)S(1)} %copy-done.5, bf16[2,2,32,2048]{3,2,1,0:T(8,128)(2,1)S(1)} %collective-permute-done.2.high_ref, ...), custom_call_target="tpu_custom_call" | custom-call | tf_op jit(solution)/shard_map/pair_phase/pallas_call | solution.py:125
  189.2 26.7 %all_to_all.5.phase_ref = f32[64,8,128]{2,1,0:T(8,128)} all-to-all(f32[64,8,128]{2,1,0:T(8,128)S(1)} %pair_phase.7), channel_id=1, replica_groups=mesh['acq'=64,'rng'=4] {'acq'}, dimensions={0} | all-to-all | bytes 524288 | tf_op jit(solution)/shard_map/all_to_all | solution.py:188
  215.9 2.1 series.1
  (24 shorter events, 0.3 us)
Async XLA Ops:
  0.0 147.7 %copy-start.6 = (s32[384]{0:T(512)S(1)}, s32[384]{0:T(512)}, u32[]{:S(2)}) copy-start(s32[384]{0:T(512)} %param.6) | copy-start | bytes 4612
  0.0 148.5 %copy-start.7 = (s32[6,2]{0,1:T(2,128)S(1)}, s32[6,2]{0,1:T(2,128)}, u32[]{:S(2)}) copy-start(s32[6,2]{0,1:T(2,128)} %param.5) | copy-start | bytes 148
  128.2 16.6 %collective-permute-start = (bf16[2,2,64,2048]{3,2,1,0:T(8,128)(2,1)}, bf16[2,2,64,2048]{3,2,1,0:T(8,128)(2,1)S(1)}, u32[]{:S(2)}, u32[]{:S(2)}) collective-permute-start(bf16[2,2,64,2048]{3,2,1,0:T(8,128)(2,1)} %get-tuple-element.11.own_ref), channel_id=1, source_target_pairs={{0,4},{4,8},{8,12},{12,16},{16,20},{20,24},{24,28},{28,32},{32,36}... | collective-permute-start | bytes 3145736 | tf_op jit(solution)/shard_map/ppermute | solution.py:169
  132.7 18.0 %collective-permute-start.3 = (bf16[2,2,64,2048]{3,2,1,0:T(8,128)(2,1)}, bf16[2,2,64,2048]{3,2,1,0:T(8,128)(2,1)}, u32[]{:S(2)}, u32[]{:S(2)}) collective-permute-start(bf16[2,2,64,2048]{3,2,1,0:T(8,128)(2,1)} %get-tuple-element.11.own_ref), channel_id=1, source_target_pairs={{4,0},{8,4},{12,8},{16,12},{20,16},{24,20},{28,24},{32,28},{36,32}... | collective-permute-start | bytes 3145736 | tf_op jit(solution)/shard_map/ppermute | solution.py:169
  134.7 21.3 %collective-permute-start.4 = (bf16[2,2,64,2048]{3,2,1,0:T(8,128)(2,1)}, bf16[2,2,64,2048]{3,2,1,0:T(8,128)(2,1)}, u32[]{:S(2)}, u32[]{:S(2)}) collective-permute-start(bf16[2,2,64,2048]{3,2,1,0:T(8,128)(2,1)} %get-tuple-element.15.own_ref), channel_id=1, source_target_pairs={{0,4},{4,8},{8,12},{12,16},{16,20},{20,24},{24,28},{28,32},{32,36}... | collective-permute-start | bytes 3145736 | tf_op jit(solution)/shard_map/ppermute | solution.py:169
  138.3 43.5 %collective-permute-start.6 = (bf16[2,2,96,2048]{3,2,1,0:T(8,128)(2,1)}, bf16[2,2,96,2048]{3,2,1,0:T(8,128)(2,1)S(1)}, u32[]{:S(2)}, u32[]{:S(2)}) collective-permute-start(bf16[2,2,96,2048]{3,2,1,0:T(8,128)(2,1)} %get-tuple-element.16.own_ref), channel_id=1, source_target_pairs={{0,4},{4,8},{8,12},{12,16},{16,20},{20,24},{24,28},{28,32},{32,36}... | collective-permute-start | bytes 4718600 | tf_op jit(solution)/shard_map/ppermute | solution.py:169
  140.2 41.6 %collective-permute-start.7 = (bf16[2,2,96,2048]{3,2,1,0:T(8,128)(2,1)}, bf16[2,2,96,2048]{3,2,1,0:T(8,128)(2,1)S(1)}, u32[]{:S(2)}, u32[]{:S(2)}) collective-permute-start(bf16[2,2,96,2048]{3,2,1,0:T(8,128)(2,1)} %get-tuple-element.16.own_ref), channel_id=1, source_target_pairs={{4,0},{8,4},{12,8},{16,12},{20,16},{24,20},{28,24},{32,28},{36,32}... | collective-permute-start | bytes 4718600 | tf_op jit(solution)/shard_map/ppermute | solution.py:169
  144.8 1.0 copy-start.3
  145.7 31.5 %collective-permute-start.5 = (bf16[2,2,64,2048]{3,2,1,0:T(8,128)(2,1)}, bf16[2,2,64,2048]{3,2,1,0:T(8,128)(2,1)}, u32[]{:S(2)}, u32[]{:S(2)}) collective-permute-start(bf16[2,2,64,2048]{3,2,1,0:T(8,128)(2,1)} %get-tuple-element.15.own_ref), channel_id=1, source_target_pairs={{4,0},{8,4},{12,8},{16,12},{20,16},{24,20},{28,24},{32,28},{36,32}... | collective-permute-start | bytes 3145736 | tf_op jit(solution)/shard_map/ppermute | solution.py:169
  150.7 36.2 %collective-permute-start.1 = (bf16[2,2,32,2048]{3,2,1,0:T(8,128)(2,1)}, bf16[2,2,32,2048]{3,2,1,0:T(8,128)(2,1)S(1)}, u32[]{:S(2)}, u32[]{:S(2)}) collective-permute-start(bf16[2,2,32,2048]{3,2,1,0:T(8,128)(2,1)} %get-tuple-element.13.own_ref), channel_id=1, source_target_pairs={{0,4},{4,8},{8,12},{12,16},{16,20},{20,24},{24,28},{28,32},{32,36}... | collective-permute-start | bytes 1572872 | tf_op jit(solution)/shard_map/ppermute | solution.py:169
  156.0 30.9 %collective-permute-start.2 = (bf16[2,2,32,2048]{3,2,1,0:T(8,128)(2,1)}, bf16[2,2,32,2048]{3,2,1,0:T(8,128)(2,1)S(1)}, u32[]{:S(2)}, u32[]{:S(2)}) collective-permute-start(bf16[2,2,32,2048]{3,2,1,0:T(8,128)(2,1)} %get-tuple-element.13.own_ref), channel_id=1, source_target_pairs={{4,0},{8,4},{12,8},{16,12},{20,16},{24,20},{28,24},{32,28},{36,32}... | collective-permute-start | bytes 1572872 | tf_op jit(solution)/shard_map/ppermute | solution.py:169
  159.6 1.2 copy-start.2
  160.9 1.2 copy-start.4
  162.1 15.2 %copy-start.1 = (bf16[2,2,64,2048]{3,2,1,0:T(8,128)(2,1)S(1)}, bf16[2,2,64,2048]{3,2,1,0:T(8,128)(2,1)}, u32[]{:S(2)}) copy-start(bf16[2,2,64,2048]{3,2,1,0:T(8,128)(2,1)} %get-tuple-element.15.own_ref) | copy-start | bytes 3145732
  166.4 15.4 %copy-start = (bf16[2,2,96,2048]{3,2,1,0:T(8,128)(2,1)S(1)}, bf16[2,2,96,2048]{3,2,1,0:T(8,128)(2,1)}, u32[]{:S(2)}) copy-start(bf16[2,2,96,2048]{3,2,1,0:T(8,128)(2,1)} %get-tuple-element.16.own_ref) | copy-start | bytes 4718596
  181.8 5.1 %copy-start.5 = (bf16[2,2,32,2048]{3,2,1,0:T(8,128)(2,1)S(1)}, bf16[2,2,32,2048]{3,2,1,0:T(8,128)(2,1)}, u32[]{:S(2)}) copy-start(bf16[2,2,32,2048]{3,2,1,0:T(8,128)(2,1)} %get-tuple-element.13.own_ref) | copy-start | bytes 1572868

commit v3 on v2

--- a/solution.py
+++ b/solution.py
@@ -34,28 +34,23 @@
     return jnp.where(imag < 0, -angle, angle)
 
 
-def cut_kernel(scenes_ref, *refs):
-    *outs, sems = refs
-    copies, start = [], 0
-    for k, out in enumerate(outs):
+def cut_kernel(scenes_ref, *outs):
+    start = 0
+    for out in outs:
         rows = out.shape[2]
-        copy = pltpu.make_async_copy(scenes_ref.at[:, :, pl.ds(start, rows), :], out, sems.at[k])
-        copy.start()
-        copies.append(copy)
+        out[...] = scenes_ref[:, :, pl.ds(start, rows), :]
         start += rows
-    for copy in copies:
-        copy.wait()
 
 
 def cut_rows(scenes):
     acq, parts, _, cols = scenes.shape
-    anywhere = pl.BlockSpec(memory_space=pl.ANY)
+    vmem = pl.BlockSpec(memory_space=pltpu.VMEM)
     return pl.pallas_call(
         cut_kernel,
         out_shape=[jax.ShapeDtypeStruct((acq, parts, rows, cols), scenes.dtype) for rows in CHUNKS],
-        in_specs=[anywhere],
-        out_specs=[anywhere] * len(CHUNKS),
-        scratch_shapes=[pltpu.SemaphoreType.DMA((len(CHUNKS),))],
+        in_specs=[vmem],
+        out_specs=[vmem] * len(CHUNKS),
+        compiler_params=pltpu.CompilerParams(vmem_limit_bytes=16 * 2**20),
         name="cut_rows",
     )(scenes)
 
@@ -166,7 +161,11 @@
     backward = [(t, s) for s, t in forward]
 
     chunks = cut_rows(scenes)
-    halos = [(lax.ppermute(c, "acq", forward), lax.ppermute(c, "acq", backward)) for c in chunks]
+    halos = []
+    for k, chunk in enumerate(chunks):
+        if k >= 2:
+            chunk, halos[k - 2] = lax.optimization_barrier((chunk, halos[k - 2]))
+        halos.append((lax.ppermute(chunk, "acq", forward), lax.ppermute(chunk, "acq", backward)))
 
     ones = (
         lax.broadcasted_iota(jnp.int32, (cols, cols // LOOK_C), 0) // LOOK_C

time: 218 us -> 94.9 us (0.44)
  Pallas kernels: 149 us -> 22.1 us
  waiting for transfers between devices: 13.8 us -> 5.14 us
  local copies, waits for them, and re-layouts: 4.33 us -> 10.5 us
  blocking collectives: 26.7 us -> 29.4 us
  starting transfers between devices: 22.6 us -> 25.2 us
    pallas_call x1, Pallas kernels: 128 us -> 1.25 us  [cut_rows(): pl.pallas_call(cut_kernel, out_shape=[jax.ShapeDtypeStruct((acq, parts, r...]
    ppermute x8, waiting for transfers between devices: 13.8 us -> 5.14 us  [the longest x4 3.34 us: body(): lax.ppermute(chunk, 'acq', backward)]
    unnamed x17 -> x23, local copies, waits for them, and re-layouts: 3.52 us -> 9.74 us
    all_to_all x1, blocking collectives: 26.7 us -> 29.4 us  [body(): phase = lax.all_to_all(phases[-1], 'acq', split_axis=0, concat_axis=0)]
    ppermute x8, starting transfers between devices: 22.6 us -> 25.2 us  [the longest x4 13.8 us: body(): lax.ppermute(chunk, 'acq', forward)]
  transfers between devices with their start and end apart: 8 -> 8, of which waited for: 3 -> 3; matrix products, arithmetic and copies ran while one was open for 1% -> 3% of each run, Pallas kernels for 7% -> 17%
where the time goes in v3:
time: 94.9 us; the launch traced here: 94.4 us
  blocking collectives  29.4 us (31%)
  starting transfers between devices  25.2 us (27%)
  Pallas kernels  22.1 us (23%)
  local copies, waits for them, and re-layouts  10.5 us (11%)
  waiting for transfers between devices  5.14 us (5%)
  other arithmetic  1.72 us (2%)
    all_to_all x1, blocking collectives, body(): phase = lax.all_to_all(phases[-1], 'acq', split_axis=0, concat_axis=0)  29.4 us
    pallas_call x4, Pallas kernels, chunk_phase(): pl.pallas_call(phase_kernel, out_shape=jax.ShapeDtypeStruct((total, SLOT_...  16.7 us
    ppermute x4, starting transfers between devices, body(): lax.ppermute(chunk, 'acq', forward)  13.8 us
    ppermute x4, starting transfers between devices, body(): lax.ppermute(chunk, 'acq', backward)  11.4 us
    unnamed x23, local copies, waits for them, and re-layouts  9.74 us
    ppermute x4, waiting for transfers between devices, body(): lax.ppermute(chunk, 'acq', backward)  3.34 us
    pallas_call x1, Pallas kernels, body(): pl.pallas_call(slots_kernel, out_shape=jax.ShapeDtypeStruct((3, design_pi...  2.14 us
    pallas_call x1, Pallas kernels, body(): pl.pallas_call(series_kernel, out_shape=jax.ShapeDtypeStruct((1, slots.sh...  2.07 us
  transfers between devices with their start and end apart: 8, of which 3 were waited for; matrix products, arithmetic and copies ran while one was open for 3% of the time, Pallas kernels for 17%

profile of v3, /device:TPU:1, one launch (start us, length us, event | category | flops | bytes accessed | tf_op | source)
XLA Modules:
  0.0 94.4 jit_solution(3154156218124463143)
XLA Ops:
  0.0 2.2 %copy-done = bf16[2,2,256,2048]{3,2,1,0:T(8,128)(2,1)S(1)} copy-done((bf16[2,2,256,2048]{3,2,1,0:T(8,128)(2,1)S(1)}, bf16[2,2,256,2048]{3,2,1,0:T(8,128)(2,1)}, u32[]{:S(2)}) %copy-start) | copy-done | bytes 4194328
  2.2 1.3 %cut_rows.1 = (bf16[2,2,64,2048]{3,2,1,0:T(8,128)(2,1)S(1)}, bf16[2,2,64,2048]{3,2,1,0:T(8,128)(2,1)}, bf16[2,2,96,2048]{3,2,1,0:T(8,128)(2,1)S(1)}, bf16[2,2,32,2048]{3,2,1,0:T(8,128)(2,1)S(1)}) custom-call(bf16[2,2,256,2048]{3,2,1,0:T(8,128)(2,1)S(1)} %copy-done), custom_call_target="tpu_custom_call" | custom-call | tf_op jit(solution)/shard_map/cut_rows/pallas_call | solution.py:48
  4.3 5.1 %collective-permute-start.1 = (bf16[2,2,64,2048]{3,2,1,0:T(8,128)(2,1)S(1)}, bf16[2,2,64,2048]{3,2,1,0:T(8,128)(2,1)S(1)}, u32[]{:S(2)}, u32[]{:S(2)}) collective-permute-start(bf16[2,2,64,2048]{3,2,1,0:T(8,128)(2,1)S(1)} %get-tuple-element.18.own_ref), channel_id=1, source_target_pairs={{4,0},{8,4},{12,8},{16,12},{20,16},{24,20},{28,24},{32,28},{36,32}... | collective-permute-start | bytes 3145736 | tf_op jit(solution)/shard_map/ppermute | solution.py:168
  9.4 1.9 %collective-permute-start = (bf16[2,2,64,2048]{3,2,1,0:T(8,128)(2,1)S(1)}, bf16[2,2,64,2048]{3,2,1,0:T(8,128)(2,1)S(1)}, u32[]{:S(2)}, u32[]{:S(2)}) collective-permute-start(bf16[2,2,64,2048]{3,2,1,0:T(8,128)(2,1)S(1)} %get-tuple-element.18.own_ref), channel_id=1, source_target_pairs={{0,4},{4,8},{8,12},{12,16},{16,20},{20,24},{24,28},{28,32},{32,36}... | collective-permute-start | bytes 3145736 | tf_op jit(solution)/shard_map/ppermute | solution.py:168
  11.4 1.0 %copy-done.1 = bf16[2,2,64,2048]{3,2,1,0:T(8,128)(2,1)} copy-done((bf16[2,2,64,2048]{3,2,1,0:T(8,128)(2,1)}, bf16[2,2,64,2048]{3,2,1,0:T(8,128)(2,1)S(1)}, u32[]{:S(2)}) %copy-start.1) | copy-done | bytes 1048600
  12.4 2.5 %collective-permute-start.3 = (bf16[2,2,64,2048]{3,2,1,0:T(8,128)(2,1)}, bf16[2,2,64,2048]{3,2,1,0:T(8,128)(2,1)}, u32[]{:S(2)}, u32[]{:S(2)}) collective-permute-start(bf16[2,2,64,2048]{3,2,1,0:T(8,128)(2,1)} %get-tuple-element.22.own_ref), channel_id=1, source_target_pairs={{4,0},{8,4},{12,8},{16,12},{20,16},{24,20},{28,24},{32,28},{36,32}... | collective-permute-start | bytes 3145736 | tf_op jit(solution)/shard_map/ppermute | solution.py:168
  14.8 3.1 %collective-permute-start.2 = (bf16[2,2,64,2048]{3,2,1,0:T(8,128)(2,1)}, bf16[2,2,64,2048]{3,2,1,0:T(8,128)(2,1)}, u32[]{:S(2)}, u32[]{:S(2)}) collective-permute-start(bf16[2,2,64,2048]{3,2,1,0:T(8,128)(2,1)} %get-tuple-element.22.own_ref), channel_id=1, source_target_pairs={{0,4},{4,8},{8,12},{12,16},{16,20},{20,24},{24,28},{28,32},{32,36}... | collective-permute-start | bytes 3145736 | tf_op jit(solution)/shard_map/ppermute | solution.py:168
  17.9 3.3 %collective-permute-done.1.high_ref = bf16[2,2,64,2048]{3,2,1,0:T(8,128)(2,1)S(1)} collective-permute-done((bf16[2,2,64,2048]{3,2,1,0:T(8,128)(2,1)S(1)}, bf16[2,2,64,2048]{3,2,1,0:T(8,128)(2,1)S(1)}, u32[]{:S(2)}, u32[]{:S(2)}) %collective-permute-start.1) | collective-permute-done | bytes 1048608 | tf_op jit(solution)/shard_map/ppermute | solution.py:168
  23.1 1.0 %copy-done.5 = bf16[2,2,64,2048]{3,2,1,0:T(8,128)(2,1)} copy-done((bf16[2,2,64,2048]{3,2,1,0:T(8,128)(2,1)}, bf16[2,2,64,2048]{3,2,1,0:T(8,128)(2,1)S(1)}, u32[]{:S(2)}) %copy-start.5) | copy-done | bytes 1048600
  24.1 1.9 %collective-permute-start.7 = (bf16[2,2,96,2048]{3,2,1,0:T(8,128)(2,1)S(1)}, bf16[2,2,96,2048]{3,2,1,0:T(8,128)(2,1)S(1)}, u32[]{:S(2)}, u32[]{:S(2)}) collective-permute-start(bf16[2,2,96,2048]{3,2,1,0:T(8,128)(2,1)S(1)} %get-tuple-element.28.own_ref), channel_id=1, source_target_pairs={{4,0},{8,4},{12,8},{16,12},{20,16},{24,20},{28,24},{32,28},{36,32}... | collective-permute-start | bytes 4718600 | tf_op jit(solution)/shard_map/ppermute | solution.py:168
  26.0 4.4 %collective-permute-start.6 = (bf16[2,2,96,2048]{3,2,1,0:T(8,128)(2,1)S(1)}, bf16[2,2,96,2048]{3,2,1,0:T(8,128)(2,1)}, u32[]{:S(2)}, u32[]{:S(2)}) collective-permute-start(bf16[2,2,96,2048]{3,2,1,0:T(8,128)(2,1)S(1)} %get-tuple-element.28.own_ref), channel_id=1, source_target_pairs={{0,4},{4,8},{8,12},{12,16},{16,20},{20,24},{24,28},{28,32},{32,36}... | collective-permute-start | bytes 4718600 | tf_op jit(solution)/shard_map/ppermute | solution.py:168
  31.3 2.1 %slot_pinv.1.slots_ref = bf16[3,128,512]{2,1,0:T(8,128)(2,1)} custom-call(s32[1,512]{1,0:T(1,128)} %reshape.7.owner_ref, f32[128,384]{1,0:T(8,128)} %pinv_ref.1), custom_call_target="tpu_custom_call" | custom-call | tf_op jit(solution)/shard_map/slot_pinv/pallas_call | solution.py:175
  34.4 1.9 %collective-permute-start.5 = (bf16[2,2,32,2048]{3,2,1,0:T(8,128)(2,1)}, bf16[2,2,32,2048]{3,2,1,0:T(8,128)(2,1)S(1)}, u32[]{:S(2)}, u32[]{:S(2)}) collective-permute-start(bf16[2,2,32,2048]{3,2,1,0:T(8,128)(2,1)} %copy-done.7), channel_id=1, source_target_pairs={{4,0},{8,4},{12,8},{16,12},{20,16},{24,20},{28,24},{32,28},{36,32}... | collective-permute-start | bytes 1572872 | tf_op jit(solution)/shard_map/ppermute | solution.py:168
  36.3 4.4 %collective-permute-start.4 = (bf16[2,2,32,2048]{3,2,1,0:T(8,128)(2,1)}, bf16[2,2,32,2048]{3,2,1,0:T(8,128)(2,1)S(1)}, u32[]{:S(2)}, u32[]{:S(2)}) collective-permute-start(bf16[2,2,32,2048]{3,2,1,0:T(8,128)(2,1)} %copy-done.7), channel_id=1, source_target_pairs={{0,4},{4,8},{8,12},{12,16},{16,20},{20,24},{24,28},{28,32},{32,36}... | collective-permute-start | bytes 1572872 | tf_op jit(solution)/shard_map/ppermute | solution.py:168
  40.7 1.7 %fusion.ones_ref = bf16[2048,128]{1,0:T(8,128)(2,1)S(1)} fusion(s32[2048]{0:T(1024)S(1)} %get-tuple-element.29, s32[2048]{0:T(1024)S(1)} %get-tuple-element.30, pred[2048]{0:T(1024)(128)(4,1)S(1)} %fusion.3), kind=kLoop, calls=%fused_computation.1 | loop fusion | flops 786432 | bytes 542720 | tf_op jit(solution)/shard_map/convert_element_type | solution.py:173
  42.5 1.2 %copy-done.2 = bf16[2,2,64,2048]{3,2,1,0:T(8,128)(2,1)S(1)} copy-done((bf16[2,2,64,2048]{3,2,1,0:T(8,128)(2,1)S(1)}, bf16[2,2,64,2048]{3,2,1,0:T(8,128)(2,1)}, u32[]{:S(2)}) %copy-start.2) | copy-done | bytes 1048600
  43.7 1.2 %copy-done.4 = bf16[2,2,64,2048]{3,2,1,0:T(8,128)(2,1)S(1)} copy-done((bf16[2,2,64,2048]{3,2,1,0:T(8,128)(2,1)S(1)}, bf16[2,2,64,2048]{3,2,1,0:T(8,128)(2,1)}, u32[]{:S(2)}) %copy-start.4) | copy-done | bytes 1048600
  44.9 1.2 %copy-done.6 = bf16[2,2,64,2048]{3,2,1,0:T(8,128)(2,1)S(1)} copy-done((bf16[2,2,64,2048]{3,2,1,0:T(8,128)(2,1)S(1)}, bf16[2,2,64,2048]{3,2,1,0:T(8,128)(2,1)}, u32[]{:S(2)}) %copy-start.6) | copy-done | bytes 1048600
  46.1 3.6 %pair_phase.4.refs_0_ = f32[16,8,128]{2,1,0:T(8,128)S(1)} custom-call(s32[6,2]{1,0:T(8,128)S(1)} %broadcast_subtract_fusion.pairs_ref, bf16[2,2,64,2048]{3,2,1,0:T(8,128)(2,1)S(1)} %copy-done.6, bf16[2,2,64,2048]{3,2,1,0:T(8,128)(2,1)S(1)} %copy-done.2, bf16[2,2,64,2048]{3,2,1,0:T(8,128)(2,1)S(1)} %copy-done.4, bf16[2048,128]{1,0:T(8,128)(2,1)S(1)} %fusion.ones_ref), custom_call_target="tpu_custom_call" | custom-call | tf_op jit(solution)/shard_map/pair_phase/pallas_call | solution.py:120
  49.7 4.9 %pair_phase.5.refs_1_ = f32[16,8,128]{2,1,0:T(8,128)S(1)} custom-call(s32[6,2]{1,0:T(8,128)S(1)} %broadcast_subtract_fusion.pairs_ref, bf16[2,2,64,2048]{3,2,1,0:T(8,128)(2,1)} %collective-permute-done.2.low_ref, bf16[2,2,64,2048]{3,2,1,0:T(8,128)(2,1)} %get-tuple-element.22.own_ref, bf16[2,2,64,2048]{3,2,1,0:T(8,128)(2,1)} %collective-permute-done.3.high_ref, ...), custom_call_target="tpu_custom_call" | custom-call | tf_op jit(solution)/shard_map/pair_phase/pallas_call | solution.py:120
  54.7 5.9 %pair_phase.6.refs_2_ = f32[24,8,128]{2,1,0:T(8,128)S(1)} custom-call(s32[6,2]{1,0:T(8,128)S(1)} %broadcast_subtract_fusion.pairs_ref, bf16[2,2,96,2048]{3,2,1,0:T(8,128)(2,1)} %collective-permute-done.6.low_ref, bf16[2,2,96,2048]{3,2,1,0:T(8,128)(2,1)S(1)} %get-tuple-element.28.own_ref, bf16[2,2,96,2048]{3,2,1,0:T(8,128)(2,1)S(1)} %collective-permute-done.7.high_ref, ...), custom_call_target="tpu_custom_call" | custom-call | tf_op jit(solution)/shard_map/pair_phase/pallas_call | solution.py:120
  60.6 2.3 %pair_phase.7 = f32[64,8,128]{2,1,0:T(8,128)S(1)} custom-call(s32[6,2]{1,0:T(8,128)S(1)} %broadcast_subtract_fusion.pairs_ref, bf16[2,2,32,2048]{3,2,1,0:T(8,128)(2,1)S(1)} %collective-permute-done.4.low_ref, bf16[2,2,32,2048]{3,2,1,0:T(8,128)(2,1)S(1)} %copy-done.8, bf16[2,2,32,2048]{3,2,1,0:T(8,128)(2,1)S(1)} %collective-permute-done.5.high_ref, ...), custom_call_target="tpu_custom_call" | custom-call | tf_op jit(solution)/shard_map/pair_phase/pallas_call | solution.py:120
  62.9 29.4 %all_to_all.5.phase_ref = f32[64,8,128]{2,1,0:T(8,128)} all-to-all(f32[64,8,128]{2,1,0:T(8,128)S(1)} %pair_phase.7), channel_id=1, replica_groups=mesh['acq'=64,'rng'=4] {'acq'}, dimensions={0} | all-to-all | bytes 524288 | tf_op jit(solution)/shard_map/all_to_all | solution.py:187
  92.3 2.1 %series.1 = f32[1,128,128]{2,1,0:T(8,128)} custom-call(bf16[3,128,512]{2,1,0:T(8,128)(2,1)} %slot_pinv.1.slots_ref, f32[64,8,128]{2,1,0:T(8,128)} %all_to_all.5.phase_ref), custom_call_target="tpu_custom_call" | custom-call | tf_op jit(solution)/shard_map/series/pallas_call | solution.py:188
  (30 shorter events, 4.6 us)
Async XLA Ops:
  0.0 2.2 %copy-start = (bf16[2,2,256,2048]{3,2,1,0:T(8,128)(2,1)S(1)}, bf16[2,2,256,2048]{3,2,1,0:T(8,128)(2,1)}, u32[]{:S(2)}) copy-start(bf16[2,2,256,2048]{3,2,1,0:T(8,128)(2,1)} %scenes_ref.1) | copy-start | bytes 12582916
  2.2 28.2 %copy-start.10 = (s32[6,2]{0,1:T(2,128)S(1)}, s32[6,2]{0,1:T(2,128)}, u32[]{:S(2)}) copy-start(s32[6,2]{0,1:T(2,128)} %param.5) | copy-start | bytes 148
  2.2 28.3 %copy-start.9 = (s32[384]{0:T(512)S(1)}, s32[384]{0:T(512)}, u32[]{:S(2)}) copy-start(s32[384]{0:T(512)} %param.6) | copy-start | bytes 4612
  3.4 0.8 copy-start.7
  4.3 17.0 %collective-permute-start.1 = (bf16[2,2,64,2048]{3,2,1,0:T(8,128)(2,1)S(1)}, bf16[2,2,64,2048]{3,2,1,0:T(8,128)(2,1)S(1)}, u32[]{:S(2)}, u32[]{:S(2)}) collective-permute-start(bf16[2,2,64,2048]{3,2,1,0:T(8,128)(2,1)S(1)} %get-tuple-element.18.own_ref), channel_id=1, source_target_pairs={{4,0},{8,4},{12,8},{16,12},{20,16},{24,20},{28,24},{32,28},{36,32}... | collective-permute-start | bytes 3145736 | tf_op jit(solution)/shard_map/ppermute | solution.py:168
  9.4 13.7 %collective-permute-start = (bf16[2,2,64,2048]{3,2,1,0:T(8,128)(2,1)S(1)}, bf16[2,2,64,2048]{3,2,1,0:T(8,128)(2,1)S(1)}, u32[]{:S(2)}, u32[]{:S(2)}) collective-permute-start(bf16[2,2,64,2048]{3,2,1,0:T(8,128)(2,1)S(1)} %get-tuple-element.18.own_ref), channel_id=1, source_target_pairs={{0,4},{4,8},{8,12},{12,16},{16,20},{20,24},{24,28},{28,32},{32,36}... | collective-permute-start | bytes 3145736 | tf_op jit(solution)/shard_map/ppermute | solution.py:168
  11.4 1.0 %copy-start.1 = (bf16[2,2,64,2048]{3,2,1,0:T(8,128)(2,1)}, bf16[2,2,64,2048]{3,2,1,0:T(8,128)(2,1)S(1)}, u32[]{:S(2)}) copy-start(bf16[2,2,64,2048]{3,2,1,0:T(8,128)(2,1)S(1)} %get-tuple-element.18.own_ref) | copy-start | bytes 3145732
  12.4 21.1 %collective-permute-start.3 = (bf16[2,2,64,2048]{3,2,1,0:T(8,128)(2,1)}, bf16[2,2,64,2048]{3,2,1,0:T(8,128)(2,1)}, u32[]{:S(2)}, u32[]{:S(2)}) collective-permute-start(bf16[2,2,64,2048]{3,2,1,0:T(8,128)(2,1)} %get-tuple-element.22.own_ref), channel_id=1, source_target_pairs={{4,0},{8,4},{12,8},{16,12},{20,16},{24,20},{28,24},{32,28},{36,32}... | collective-permute-start | bytes 3145736 | tf_op jit(solution)/shard_map/ppermute | solution.py:168
  14.8 19.6 %collective-permute-start.2 = (bf16[2,2,64,2048]{3,2,1,0:T(8,128)(2,1)}, bf16[2,2,64,2048]{3,2,1,0:T(8,128)(2,1)}, u32[]{:S(2)}, u32[]{:S(2)}) collective-permute-start(bf16[2,2,64,2048]{3,2,1,0:T(8,128)(2,1)} %get-tuple-element.22.own_ref), channel_id=1, source_target_pairs={{0,4},{4,8},{8,12},{12,16},{16,20},{20,24},{24,28},{28,32},{32,36}... | collective-permute-start | bytes 3145736 | tf_op jit(solution)/shard_map/ppermute | solution.py:168
  21.3 1.0 %copy-start.3 = (bf16[2,2,64,2048]{3,2,1,0:T(8,128)(2,1)}, bf16[2,2,64,2048]{3,2,1,0:T(8,128)(2,1)S(1)}, u32[]{:S(2)}) copy-start(bf16[2,2,64,2048]{3,2,1,0:T(8,128)(2,1)S(1)} %collective-permute-done.1.high_ref) | copy-start | bytes 3145732
  23.1 1.0 %copy-start.5 = (bf16[2,2,64,2048]{3,2,1,0:T(8,128)(2,1)}, bf16[2,2,64,2048]{3,2,1,0:T(8,128)(2,1)S(1)}, u32[]{:S(2)}) copy-start(bf16[2,2,64,2048]{3,2,1,0:T(8,128)(2,1)S(1)} %collective-permute-done.low_ref) | copy-start | bytes 3145732
  24.1 30.6 %collective-permute-start.7 = (bf16[2,2,96,2048]{3,2,1,0:T(8,128)(2,1)S(1)}, bf16[2,2,96,2048]{3,2,1,0:T(8,128)(2,1)S(1)}, u32[]{:S(2)}, u32[]{:S(2)}) collective-permute-start(bf16[2,2,96,2048]{3,2,1,0:T(8,128)(2,1)S(1)} %get-tuple-element.28.own_ref), channel_id=1, source_target_pairs={{4,0},{8,4},{12,8},{16,12},{20,16},{24,20},{28,24},{32,28},{36,32}... | collective-permute-start | bytes 4718600 | tf_op jit(solution)/shard_map/ppermute | solution.py:168
  26.0 28.7 %collective-permute-start.6 = (bf16[2,2,96,2048]{3,2,1,0:T(8,128)(2,1)S(1)}, bf16[2,2,96,2048]{3,2,1,0:T(8,128)(2,1)}, u32[]{:S(2)}, u32[]{:S(2)}) collective-permute-start(bf16[2,2,96,2048]{3,2,1,0:T(8,128)(2,1)S(1)} %get-tuple-element.28.own_ref), channel_id=1, source_target_pairs={{0,4},{4,8},{8,12},{12,16},{16,20},{20,24},{24,28},{28,32},{32,36}... | collective-permute-start | bytes 4718600 | tf_op jit(solution)/shard_map/ppermute | solution.py:168
  34.4 26.1 %collective-permute-start.5 = (bf16[2,2,32,2048]{3,2,1,0:T(8,128)(2,1)}, bf16[2,2,32,2048]{3,2,1,0:T(8,128)(2,1)S(1)}, u32[]{:S(2)}, u32[]{:S(2)}) collective-permute-start(bf16[2,2,32,2048]{3,2,1,0:T(8,128)(2,1)} %copy-done.7), channel_id=1, source_target_pairs={{4,0},{8,4},{12,8},{16,12},{20,16},{24,20},{28,24},{32,28},{36,32}... | collective-permute-start | bytes 1572872 | tf_op jit(solution)/shard_map/ppermute | solution.py:168
  36.3 24.2 %collective-permute-start.4 = (bf16[2,2,32,2048]{3,2,1,0:T(8,128)(2,1)}, bf16[2,2,32,2048]{3,2,1,0:T(8,128)(2,1)S(1)}, u32[]{:S(2)}, u32[]{:S(2)}) collective-permute-start(bf16[2,2,32,2048]{3,2,1,0:T(8,128)(2,1)} %copy-done.7), channel_id=1, source_target_pairs={{0,4},{4,8},{8,12},{12,16},{16,20},{20,24},{24,28},{28,32},{32,36}... | collective-permute-start | bytes 1572872 | tf_op jit(solution)/shard_map/ppermute | solution.py:168
  42.5 1.2 %copy-start.2 = (bf16[2,2,64,2048]{3,2,1,0:T(8,128)(2,1)S(1)}, bf16[2,2,64,2048]{3,2,1,0:T(8,128)(2,1)}, u32[]{:S(2)}) copy-start(bf16[2,2,64,2048]{3,2,1,0:T(8,128)(2,1)} %copy-done.1) | copy-start | bytes 3145732
  43.7 1.2 %copy-start.4 = (bf16[2,2,64,2048]{3,2,1,0:T(8,128)(2,1)S(1)}, bf16[2,2,64,2048]{3,2,1,0:T(8,128)(2,1)}, u32[]{:S(2)}) copy-start(bf16[2,2,64,2048]{3,2,1,0:T(8,128)(2,1)} %copy-done.3) | copy-start | bytes 3145732
  44.9 1.2 %copy-start.6 = (bf16[2,2,64,2048]{3,2,1,0:T(8,128)(2,1)S(1)}, bf16[2,2,64,2048]{3,2,1,0:T(8,128)(2,1)}, u32[]{:S(2)}) copy-start(bf16[2,2,64,2048]{3,2,1,0:T(8,128)(2,1)} %copy-done.5) | copy-start | bytes 3145732
  54.6 5.9 %copy-start.8 = (bf16[2,2,32,2048]{3,2,1,0:T(8,128)(2,1)S(1)}, bf16[2,2,32,2048]{3,2,1,0:T(8,128)(2,1)}, u32[]{:S(2)}) copy-start(bf16[2,2,32,2048]{3,2,1,0:T(8,128)(2,1)} %copy-done.7) | copy-start | bytes 1572868

commit v4 on v3

v4 whole, which is shorter than its diff:
```python
import functools

import jax
import jax.numpy as jnp
import numpy as np
from jax import lax
from jax.experimental import pallas as pl
from jax.experimental.pallas import tpu as pltpu
from jax.sharding import PartitionSpec as P

LOOK_R = 4
LOOK_C = 16
LANES = 128
CHUNKS = (128, 96, 32)
BAND = 32
SLOT_PAD = 8
UNROLL_A = 2
UNROLL_B = 2

ATAN = (
    0.0030499680532062342, -0.016827448459262765, 0.04385559893448732,
    -0.07596809856148054, 0.1068142102724691, -0.14213196195363814,
    0.19993716142481088, -0.33333120780995057, 0.9999999880828068,
)


def atan_ratio(imag, real):
    size = jnp.abs(imag)
    steep = size > real
    ratio = jnp.minimum(size, real) / jnp.maximum(size, real)
    square = ratio * ratio
    poly = jnp.full_like(square, ATAN[0])
    for coefficient in ATAN[1:]:
        poly = poly * square + coefficient
    angle = poly * ratio
    angle = jnp.where(steep, np.float32(np.pi / 2) - angle, angle)
    return jnp.where(imag < 0, -angle, angle)


def split(x, count):
    pieces = []
    for _ in range(count):
        pieces.append(x.astype(jnp.bfloat16))
        x = x - pieces[-1].astype(jnp.float32)
    return pieces


def phase_kernel(start, pairs_ref, far_ref, own_ref, near_ref, ones_ref, *refs):
    *earlier, out_ref, stack, sums = refs
    pair_count = pairs_ref.shape[0]
    acq, _, rows, cols = far_ref.shape
    bands, looked = rows // BAND, BAND // LOOK_R
    blocks = cols // LANES
    picks = [(pairs_ref[p, 0], pairs_ref[p, 1]) for p in range(pair_count)]

    def band(b, carry):
        own_rows = pl.ds(pl.multiple_of(start + b * BAND, BAND), BAND)
        far_rows = pl.ds(pl.multiple_of(b * BAND, BAND), BAND)

        def widen(j, carry):
            lanes = pl.ds(pl.multiple_of(j * LANES, LANES), LANES)
            for side, (ref, at) in enumerate(((far_ref, far_rows), (own_ref, own_rows), (near_ref, own_rows))):
                for a in range(acq):
                    for part in range(2):
                        stack[side * acq + a, part, j] = ref[a, part, at, lanes].astype(jnp.float32)
            return carry

        def form(j, carry):
            lanes = pl.ds(pl.multiple_of(j * LANES, LANES), LANES)
            for p, (first, second) in enumerate(picks):
                real = imag = None
                for i in range(LOOK_R):
                    pick = pl.ds(i, looked, stride=LOOK_R)
                    ar, ai = stack[first, 0, j, pick, :], stack[first, 1, j, pick, :]
                    cr, ci = stack[second, 0, j, pick, :], stack[second, 1, j, pick, :]
                    re, im = ar * cr + ai * ci, ai * cr - ar * ci
                    real = re if real is None else real + re
                    imag = im if imag is None else imag + im
                for piece, value in enumerate(split(jnp.concatenate([real, imag], axis=0), 2)):
                    sums[piece, b, pl.ds(p * 2 * looked, 2 * looked), lanes] = value
            return carry

        lax.fori_loop(0, blocks, widen, 0, unroll=2)
        lax.fori_loop(0, blocks, form, 0, unroll=2)
        return carry

    lax.fori_loop(0, bands, band, 0)
    pieces = sums[...].reshape(2 * bands * sums.shape[2], cols)
    dots = jnp.dot(pieces, ones_ref[...], preferred_element_type=jnp.float32)
    dots = dots.reshape(2, bands, pair_count, 2, looked, dots.shape[1])
    both = dots[0] + dots[1]
    angle = atan_ratio(both[:, :, 1], both[:, :, 0])
    at = 0
    for ref in earlier:
        out_ref[pl.ds(at, ref.shape[0])] = ref[...]
        at += ref.shape[0]
    for b in range(bands):
        for p in range(SLOT_PAD):
            out_ref[pl.ds(at + b * looked, looked), p, :] = (
                angle[b, p] if p < pair_count else jnp.zeros_like(angle[b, 0])
            )


def chunk_phase(start, pairs, far, own, near, ones, earlier=()):
    acq, parts, rows, cols = far.shape
    looked = rows // LOOK_R
    pair_count = pairs.shape[0]
    total = looked + sum(x.shape[0] for x in earlier)
    vmem = pl.BlockSpec(memory_space=pltpu.VMEM)
    return pl.pallas_call(
        functools.partial(phase_kernel, start),
        out_shape=jax.ShapeDtypeStruct((total, SLOT_PAD, cols // LOOK_C), jnp.float32),
        in_specs=[pl.BlockSpec(memory_space=pltpu.SMEM)] + [vmem] * (4 + len(earlier)),
        out_specs=vmem,
        scratch_shapes=[
            pltpu.VMEM((3 * acq, parts, cols // LANES, BAND, LANES), jnp.float32),
            pltpu.VMEM((2, rows // BAND, 2 * pair_count * BAND // LOOK_R, cols), jnp.bfloat16),
        ],
        compiler_params=pltpu.CompilerParams(vmem_limit_bytes=24 * 2**20),
        name="pair_phase",
    )(pairs, far, own, near, ones, *earlier)


def slots_kernel(owner_ref, pinv_ref, out_ref):
    count = pinv_ref.shape[1]
    row = lax.broadcasted_iota(jnp.int32, (count, owner_ref.shape[1]), 0)
    pick = (row == owner_ref[...]).astype(jnp.bfloat16)
    for piece, value in enumerate(split(pinv_ref[...], 3)):
        out_ref[piece] = jnp.dot(value, pick, preferred_element_type=jnp.float32).astype(jnp.bfloat16)


def series_kernel(slots_ref, phase_ref, out_ref):
    acqs, width = slots_ref.shape[1:]
    phase = split(phase_ref[...].reshape(width, phase_ref.shape[2]), 3)
    total = None
    for piece in reversed(range(3)):
        rows = slots_ref[pl.ds(0, 3 - piece)].reshape((3 - piece) * acqs, width)
        dots = jnp.dot(rows, phase[piece], preferred_element_type=jnp.float32)
        for k in reversed(range(3 - piece)):
            part = dots[k * acqs : (k + 1) * acqs]
            total = part if total is None else total + part
    out_ref[0] = total


def body(scenes, pairs, pair_owner, design_pinv):
    acq, parts, rows, cols = scenes.shape
    pair_count = pairs.shape[0]
    count = lax.axis_size("acq")
    me = lax.axis_index("acq")
    near_pairs = [(i, i ^ 1) for i in range(count)]
    far_pairs = [(i, i + 1 if i % 2 else i - 1) for i in range(1, count - 1)]
    local = pairs - (me - 1) * acq
    local = jnp.where(me % 2 == 1, (2 - local // acq) * acq + local % acq, local)

    chunks, halos, start = [], [], 0
    rest, near = scenes, None
    for k, step in enumerate(CHUNKS):
        chunk = lax.slice_in_dim(rest, start, start + step, axis=2)
        rest, chunk = lax.optimization_barrier((rest, chunk))
        halos.append(lax.ppermute(chunk, "acq", far_pairs))
        chunks.append(start)
        start += step
        if k == 0:
            near = lax.ppermute(rest, "acq", near_pairs)
            rest, near = lax.optimization_barrier((rest, near))
        else:
            rest, halos[k - 1] = lax.optimization_barrier((rest, halos[k - 1]))

    ones = (
        lax.broadcasted_iota(jnp.int32, (cols, cols // LOOK_C), 0) // LOOK_C
        == lax.broadcasted_iota(jnp.int32, (cols, cols // LOOK_C), 1)
    ).astype(jnp.bfloat16)
    owner = jnp.pad(pair_owner.reshape(count, pair_count), ((0, 0), (0, SLOT_PAD - pair_count)), constant_values=-1)
    slots = pl.pallas_call(
        slots_kernel,
        out_shape=jax.ShapeDtypeStruct((3, design_pinv.shape[0], count * SLOT_PAD), jnp.bfloat16),
        name="slot_pinv",
    )(owner.reshape(1, count * SLOT_PAD), design_pinv)

    phases = []
    for k, (start, far) in enumerate(zip(chunks, halos)):
        if k == 0:
            far, slots = lax.optimization_barrier((far, slots))
        last = k == len(chunks) - 1
        phases.append(chunk_phase(start, local, far, scenes, near, ones, phases if last else ()))
    phase = lax.all_to_all(phases[-1], "acq", split_axis=0, concat_axis=0)
    return pl.pallas_call(
        series_kernel,
        out_shape=jax.ShapeDtypeStruct((1, slots.shape[1], phase.shape[2]), jnp.float32),
        name="series",
    )(slots, phase)


def solution(mesh):
    placed = (P("acq", None, None, "rng"), P("acq", None), P(), P())
    return jax.shard_map(
        body, mesh=mesh, in_specs=placed, out_specs=P("acq", None, "rng"), check_vma=False
    )
```

time: 94.9 us -> 85.9 us (0.905)
  starting transfers between devices: 25.2 us -> 8.98 us
  waiting for transfers between devices: 5.14 us -> 19.4 us
  blocking collectives: 29.4 us -> 24.8 us
  Pallas kernels: 22.1 us -> 17.6 us
  local copies, waits for them, and re-layouts: 10.5 us -> 12.9 us
    ppermute x8 -> x4, starting transfers between devices: 25.2 us -> 8.98 us  [the longest x3 5.74 us: body(): halos.append(lax.ppermute(chunk, 'acq', far_pairs))]
    ppermute x8 -> x4, waiting for transfers between devices: 5.14 us -> 19.4 us  [the longest x3 14.5 us: body(): halos.append(lax.ppermute(chunk, 'acq', far_pairs))]
    slice x0 -> x3, local copies, waits for them, and re-layouts: none -> 5.66 us  [body(): chunk = lax.slice_in_dim(rest, start, start + step, axis=2)]
    all_to_all x1, blocking collectives: 29.4 us -> 24.8 us  [body(): phase = lax.all_to_all(phases[-1], 'acq', split_axis=0, concat_axis=0)]
    pallas_call x5 -> x3, Pallas kernels: 17.9 us -> 13.4 us  [chunk_phase(): pl.pallas_call(functools.partial(phase_kernel, start), out_shape=jax.Shap...]
    unnamed x23 -> x13, local copies, waits for them, and re-layouts: 9.74 us -> 6.42 us
  transfers between devices with their start and end apart: 8 -> 4, of which waited for: 3 -> 4; matrix products, arithmetic and copies ran while one was open for 3% -> 6% of each run, Pallas kernels for 17% -> 16%
where the time goes in v4:
time: 85.9 us; the launch traced here: 85.5 us
  blocking collectives  24.8 us (29%)
  waiting for transfers between devices  19.4 us (23%)
  Pallas kernels  17.6 us (20%)
  local copies, waits for them, and re-layouts  12.9 us (15%)
  starting transfers between devices  8.98 us (10%)
  other arithmetic  1.73 us (2%)
    all_to_all x1, blocking collectives, body(): phase = lax.all_to_all(phases[-1], 'acq', split_axis=0, concat_axis=0)  24.8 us
    ppermute x3, waiting for transfers between devices, body(): halos.append(lax.ppermute(chunk, 'acq', far_pairs))  14.5 us
    pallas_call x3, Pallas kernels, chunk_phase(): pl.pallas_call(functools.partial(phase_kernel, start), out_shape=jax.Shap...  13.4 us
    unnamed x13, local copies, waits for them, and re-layouts  6.42 us
    ppermute x3, starting transfers between devices, body(): halos.append(lax.ppermute(chunk, 'acq', far_pairs))  5.74 us
    slice x3, local copies, waits for them, and re-layouts, body(): chunk = lax.slice_in_dim(rest, start, start + step, axis=2)  5.66 us
    ppermute x1, waiting for transfers between devices, body(): near = lax.ppermute(rest, 'acq', near_pairs)  4.87 us
    ppermute x1, starting transfers between devices, body(): near = lax.ppermute(rest, 'acq', near_pairs)  3.24 us
  transfers between devices with their start and end apart: 4, of which 4 were waited for; matrix products, arithmetic and copies ran while one was open for 6% of the time, Pallas kernels for 16%

profile of v4, /device:TPU:1, one launch (start us, length us, event | category | flops | bytes accessed | tf_op | source)
XLA Modules:
  0.0 85.5 jit_solution(4398997509454852855)
XLA Ops:
  0.0 3.3 %slice.9 = bf16[2,2,128,2048]{3,2,1,0:T(8,128)(2,1)} slice(bf16[2,2,256,2048]{3,2,1,0:T(8,128)(2,1)} %own_ref.5), slice={[0:2], [0:2], [0:128], [0:2048]} | slice | bytes 4194304 | tf_op jit(solution)/shard_map/slice | solution.py:158
  3.3 3.2 %collective-permute-start = (bf16[2,2,256,2048]{3,2,1,0:T(8,128)(2,1)S(1)}, bf16[2,2,256,2048]{3,2,1,0:T(8,128)(2,1)S(1)}, u32[]{:S(2)}, u32[]{:S(2)}) collective-permute-start(bf16[2,2,256,2048]{3,2,1,0:T(8,128)(2,1)S(1)} %copy-done), channel_id=1, source_target_pairs={{0,4},{4,0},{8,12},{12,8},{16,20},{20,16},{24,28},{28,24},{32,36},... | collective-permute-start | bytes 12582920 | tf_op jit(solution)/shard_map/ppermute | solution.py:164
  6.6 1.9 %collective-permute-start.1 = (bf16[2,2,128,2048]{3,2,1,0:T(8,128)(2,1)}, bf16[2,2,128,2048]{3,2,1,0:T(8,128)(2,1)S(1)}, u32[]{:S(2)}, u32[]{:S(2)}) collective-permute-start(bf16[2,2,128,2048]{3,2,1,0:T(8,128)(2,1)} %slice.9), channel_id=1, source_target_pairs={{4,8},{8,4},{12,16},{16,12},{20,24},{24,20},{28,32},{32,28},{36,40... | collective-permute-start | bytes 6291464 | tf_op jit(solution)/shard_map/ppermute | solution.py:160
  8.5 4.9 %collective-permute-done.near_ref = bf16[2,2,256,2048]{3,2,1,0:T(8,128)(2,1)S(1)} collective-permute-done((bf16[2,2,256,2048]{3,2,1,0:T(8,128)(2,1)S(1)}, bf16[2,2,256,2048]{3,2,1,0:T(8,128)(2,1)S(1)}, u32[]{:S(2)}, u32[]{:S(2)}) %collective-permute-start) | collective-permute-done | bytes 4194336 | tf_op jit(solution)/shard_map/ppermute | solution.py:164
  13.4 1.9 %copy-done.2 = bf16[2,2,256,2048]{3,2,1,0:T(8,128)(2,1)} copy-done((bf16[2,2,256,2048]{3,2,1,0:T(8,128)(2,1)}, bf16[2,2,256,2048]{3,2,1,0:T(8,128)(2,1)S(1)}, u32[]{:S(2)}) %copy-start.2) | copy-done | bytes 4194328
  15.3 1.3 %slice.10 = bf16[2,2,96,2048]{3,2,1,0:T(8,128)(2,1)} slice(bf16[2,2,256,2048]{3,2,1,0:T(8,128)(2,1)S(1)} %copy-done), slice={[0:2], [0:2], [128:224], [0:2048]} | slice | bytes 3145728 | tf_op jit(solution)/shard_map/slice | solution.py:158
  16.6 1.9 %collective-permute-start.3 = (bf16[2,2,96,2048]{3,2,1,0:T(8,128)(2,1)}, bf16[2,2,96,2048]{3,2,1,0:T(8,128)(2,1)}, u32[]{:S(2)}, u32[]{:S(2)}) collective-permute-start(bf16[2,2,96,2048]{3,2,1,0:T(8,128)(2,1)} %slice.10), channel_id=1, source_target_pairs={{4,8},{8,4},{12,16},{16,12},{20,24},{24,20},{28,32},{32,28},{36,40... | collective-permute-start | bytes 4718600 | tf_op jit(solution)/shard_map/ppermute | solution.py:160
  18.5 0.1 copy.6
  18.6 0.1 reshape.6
  18.8 0.7 reshape.7.owner_ref
  19.4 2.1 %slot_pinv.1.slots_ref = bf16[3,128,512]{2,1,0:T(8,128)(2,1)} custom-call(s32[1,512]{1,0:T(1,128)} %reshape.7.owner_ref, f32[128,384]{1,0:T(8,128)} %pinv_ref.1), custom_call_target="tpu_custom_call" | custom-call | tf_op jit(solution)/shard_map/slot_pinv/pallas_call | solution.py:174
  21.5 12.6 %collective-permute-done.1.far_ref = bf16[2,2,128,2048]{3,2,1,0:T(8,128)(2,1)S(1)} collective-permute-done((bf16[2,2,128,2048]{3,2,1,0:T(8,128)(2,1)}, bf16[2,2,128,2048]{3,2,1,0:T(8,128)(2,1)S(1)}, u32[]{:S(2)}, u32[]{:S(2)}) %collective-permute-start.1) | collective-permute-done | bytes 2097184 | tf_op jit(solution)/shard_map/ppermute | solution.py:160
  34.1 1.1 %slice.11 = bf16[2,2,32,2048]{3,2,1,0:T(8,128)(2,1)S(1)} slice(bf16[2,2,256,2048]{3,2,1,0:T(8,128)(2,1)} %own_ref.5), slice={[0:2], [0:2], [224:256], [0:2048]} | slice | bytes 1048576 | tf_op jit(solution)/shard_map/slice | solution.py:158
  35.2 1.9 %collective-permute-start.2 = (bf16[2,2,32,2048]{3,2,1,0:T(8,128)(2,1)S(1)}, bf16[2,2,32,2048]{3,2,1,0:T(8,128)(2,1)S(1)}, u32[]{:S(2)}, u32[]{:S(2)}) collective-permute-start(bf16[2,2,32,2048]{3,2,1,0:T(8,128)(2,1)S(1)} %slice.11), channel_id=1, source_target_pairs={{4,8},{8,4},{12,16},{16,12},{20,24},{24,20},{28,32},{32,28},{36,40... | collective-permute-start | bytes 1572872 | tf_op jit(solution)/shard_map/ppermute | solution.py:160
  37.2 1.7 %fusion.ones_ref = bf16[2048,128]{1,0:T(8,128)(2,1)S(1)} fusion(s32[2048]{0:T(1024)S(1)} %get-tuple-element.27, s32[2048]{0:T(1024)S(1)} %get-tuple-element.28, pred[2048]{0:T(1024)(128)(4,1)S(1)} %fusion.3), kind=kLoop, calls=%fused_computation.1 | loop fusion | flops 786432 | bytes 542720 | tf_op jit(solution)/shard_map/convert_element_type | solution.py:172
  38.9 2.2 %copy-done.1 = bf16[2,2,256,2048]{3,2,1,0:T(8,128)(2,1)S(1)} copy-done((bf16[2,2,256,2048]{3,2,1,0:T(8,128)(2,1)S(1)}, bf16[2,2,256,2048]{3,2,1,0:T(8,128)(2,1)}, u32[]{:S(2)}) %copy-start.1) | copy-done | bytes 4194328
  41.1 2.2 %copy-done.3 = bf16[2,2,256,2048]{3,2,1,0:T(8,128)(2,1)S(1)} copy-done((bf16[2,2,256,2048]{3,2,1,0:T(8,128)(2,1)S(1)}, bf16[2,2,256,2048]{3,2,1,0:T(8,128)(2,1)}, u32[]{:S(2)}) %copy-start.3) | copy-done | bytes 4194328
  43.2 5.9 %pair_phase.3.refs_0_ = f32[32,8,128]{2,1,0:T(8,128)S(1)} custom-call(s32[6,2]{1,0:T(8,128)S(1)} %fusion.7.pairs_ref, bf16[2,2,128,2048]{3,2,1,0:T(8,128)(2,1)S(1)} %collective-permute-done.1.far_ref, bf16[2,2,256,2048]{3,2,1,0:T(8,128)(2,1)S(1)} %copy-done.1, bf16[2,2,256,2048]{3,2,1,0:T(8,128)(2,1)S(1)} %copy-done.3, bf16[2048,128]{1,0:T(8,128)(2,1)S(1)} %fusion.ones_ref), custom_call_target="tpu_custom_call" | custom-call | tf_op jit(solution)/shard_map/pair_phase/pallas_call | solution.py:110
  49.2 1.9 %collective-permute-done.3.far_ref = bf16[2,2,96,2048]{3,2,1,0:T(8,128)(2,1)} collective-permute-done((bf16[2,2,96,2048]{3,2,1,0:T(8,128)(2,1)}, bf16[2,2,96,2048]{3,2,1,0:T(8,128)(2,1)}, u32[]{:S(2)}, u32[]{:S(2)}) %collective-permute-start.3) | collective-permute-done | bytes 1572896 | tf_op jit(solution)/shard_map/ppermute | solution.py:160
  51.1 5.4 %pair_phase.4.refs_1_ = f32[24,8,128]{2,1,0:T(8,128)S(1)} custom-call(s32[6,2]{1,0:T(8,128)S(1)} %fusion.7.pairs_ref, bf16[2,2,96,2048]{3,2,1,0:T(8,128)(2,1)} %collective-permute-done.3.far_ref, bf16[2,2,256,2048]{3,2,1,0:T(8,128)(2,1)S(1)} %copy-done.1, bf16[2,2,256,2048]{3,2,1,0:T(8,128)(2,1)S(1)} %copy-done.3, bf16[2048,128]{1,0:T(8,128)(2,1)S(1)} %fusion.ones_ref), custom_call_target="tpu_custom_call" | custom-call | tf_op jit(solution)/shard_map/pair_phase/pallas_call | solution.py:110
  56.5 0.1 collective-permute-done.2.far_ref
  56.6 2.1 %pair_phase.5 = f32[64,8,128]{2,1,0:T(8,128)S(1)} custom-call(s32[6,2]{1,0:T(8,128)S(1)} %fusion.7.pairs_ref, bf16[2,2,32,2048]{3,2,1,0:T(8,128)(2,1)S(1)} %collective-permute-done.2.far_ref, bf16[2,2,256,2048]{3,2,1,0:T(8,128)(2,1)S(1)} %copy-done.1, bf16[2,2,256,2048]{3,2,1,0:T(8,128)(2,1)S(1)} %copy-done.3, bf16[2048,128]{1,0:T(8,128)(2,1)S(1)} %fusion.ones_ref, ...), custom_call_target="tpu_custom_call" | custom-call | tf_op jit(solution)/shard_map/pair_phase/pallas_call | solution.py:110
  58.7 24.8 %all_to_all.5.phase_ref = f32[64,8,128]{2,1,0:T(8,128)} all-to-all(f32[64,8,128]{2,1,0:T(8,128)S(1)} %pair_phase.5), channel_id=1, replica_groups=mesh['acq'=64,'rng'=4] {'acq'}, dimensions={0} | all-to-all | bytes 524288 | tf_op jit(solution)/shard_map/all_to_all | solution.py:186
  83.4 2.1 %series.1 = f32[1,128,128]{2,1,0:T(8,128)} custom-call(bf16[3,128,512]{2,1,0:T(8,128)(2,1)} %slot_pinv.1.slots_ref, f32[64,8,128]{2,1,0:T(8,128)} %all_to_all.5.phase_ref), custom_call_target="tpu_custom_call" | custom-call | tf_op jit(solution)/shard_map/series/pallas_call | solution.py:187
  (13 shorter events, 0.1 us)
Async XLA Ops:
  0.0 3.3 %copy-start = (bf16[2,2,256,2048]{3,2,1,0:T(8,128)(2,1)S(1)}, bf16[2,2,256,2048]{3,2,1,0:T(8,128)(2,1)}, u32[]{:S(2)}) copy-start(bf16[2,2,256,2048]{3,2,1,0:T(8,128)(2,1)} %own_ref.5) | copy-start | bytes 12582916
  3.3 15.2 %copy-start.5 = (s32[6,2]{0,1:T(2,128)S(1)}, s32[6,2]{0,1:T(2,128)}, u32[]{:S(2)}) copy-start(s32[6,2]{0,1:T(2,128)} %param.5) | copy-start | bytes 148
  3.3 15.3 %copy-start.4 = (s32[384]{0:T(512)S(1)}, s32[384]{0:T(512)}, u32[]{:S(2)}) copy-start(s32[384]{0:T(512)} %param.6) | copy-start | bytes 4612
  3.3 10.0 %collective-permute-start = (bf16[2,2,256,2048]{3,2,1,0:T(8,128)(2,1)S(1)}, bf16[2,2,256,2048]{3,2,1,0:T(8,128)(2,1)S(1)}, u32[]{:S(2)}, u32[]{:S(2)}) collective-permute-start(bf16[2,2,256,2048]{3,2,1,0:T(8,128)(2,1)S(1)} %copy-done), channel_id=1, source_target_pairs={{0,4},{4,0},{8,12},{12,8},{16,20},{20,16},{24,28},{28,24},{32,36},... | collective-permute-start | bytes 12582920 | tf_op jit(solution)/shard_map/ppermute | solution.py:164
  6.6 27.6 %collective-permute-start.1 = (bf16[2,2,128,2048]{3,2,1,0:T(8,128)(2,1)}, bf16[2,2,128,2048]{3,2,1,0:T(8,128)(2,1)S(1)}, u32[]{:S(2)}, u32[]{:S(2)}) collective-permute-start(bf16[2,2,128,2048]{3,2,1,0:T(8,128)(2,1)} %slice.9), channel_id=1, source_target_pairs={{4,8},{8,4},{12,16},{16,12},{20,24},{24,20},{28,32},{32,28},{36,40... | collective-permute-start | bytes 6291464 | tf_op jit(solution)/shard_map/ppermute | solution.py:160
  13.4 1.9 %copy-start.2 = (bf16[2,2,256,2048]{3,2,1,0:T(8,128)(2,1)}, bf16[2,2,256,2048]{3,2,1,0:T(8,128)(2,1)S(1)}, u32[]{:S(2)}) copy-start(bf16[2,2,256,2048]{3,2,1,0:T(8,128)(2,1)S(1)} %collective-permute-done.near_ref) | copy-start | bytes 12582916
  16.6 34.5 %collective-permute-start.3 = (bf16[2,2,96,2048]{3,2,1,0:T(8,128)(2,1)}, bf16[2,2,96,2048]{3,2,1,0:T(8,128)(2,1)}, u32[]{:S(2)}, u32[]{:S(2)}) collective-permute-start(bf16[2,2,96,2048]{3,2,1,0:T(8,128)(2,1)} %slice.10), channel_id=1, source_target_pairs={{4,8},{8,4},{12,16},{16,12},{20,24},{24,20},{28,32},{32,28},{36,40... | collective-permute-start | bytes 4718600 | tf_op jit(solution)/shard_map/ppermute | solution.py:160
  35.2 21.4 %collective-permute-start.2 = (bf16[2,2,32,2048]{3,2,1,0:T(8,128)(2,1)S(1)}, bf16[2,2,32,2048]{3,2,1,0:T(8,128)(2,1)S(1)}, u32[]{:S(2)}, u32[]{:S(2)}) collective-permute-start(bf16[2,2,32,2048]{3,2,1,0:T(8,128)(2,1)S(1)} %slice.11), channel_id=1, source_target_pairs={{4,8},{8,4},{12,16},{16,12},{20,24},{24,20},{28,32},{32,28},{36,40... | collective-permute-start | bytes 1572872 | tf_op jit(solution)/shard_map/ppermute | solution.py:160
  38.9 2.2 %copy-start.1 = (bf16[2,2,256,2048]{3,2,1,0:T(8,128)(2,1)S(1)}, bf16[2,2,256,2048]{3,2,1,0:T(8,128)(2,1)}, u32[]{:S(2)}) copy-start(bf16[2,2,256,2048]{3,2,1,0:T(8,128)(2,1)} %own_ref.5) | copy-start | bytes 12582916
  41.1 2.2 %copy-start.3 = (bf16[2,2,256,2048]{3,2,1,0:T(8,128)(2,1)S(1)}, bf16[2,2,256,2048]{3,2,1,0:T(8,128)(2,1)}, u32[]{:S(2)}) copy-start(bf16[2,2,256,2048]{3,2,1,0:T(8,128)(2,1)} %copy-done.2) | copy-start | bytes 12582916

commit v5 on v4

--- a/solution.py
+++ b/solution.py
@@ -11,8 +11,10 @@
 LOOK_R = 4
 LOOK_C = 16
 LANES = 128
-CHUNKS = (128, 96, 32)
+CHUNKS = (64, 96, 64, 32)
 BAND = 32
+PHASE_VMEM = 10 * 2**20
+SMALL_VMEM = 6 * 2**20
 SLOT_PAD = 8
 UNROLL_A = 2
 UNROLL_B = 2
@@ -37,6 +39,33 @@
     return jnp.where(imag < 0, -angle, angle)
 
 
+def cut_kernel(start, scenes_ref, *refs):
+    *outs, sems = refs
+    copies = []
+    for k, out in enumerate(outs):
+        rows = out.shape[2]
+        copies.append(pltpu.make_async_copy(scenes_ref.at[:, :, pl.ds(start, rows), :], out, sems.at[k]))
+        start += rows
+    for copy in copies:
+        copy.start()
+    for copy in copies:
+        copy.wait()
+
+
+def cut_rows(scenes, start, sizes):
+    acq, parts, _, cols = scenes.shape
+    vmem = pl.BlockSpec(memory_space=pltpu.VMEM)
+    return pl.pallas_call(
+        functools.partial(cut_kernel, start),
+        out_shape=[jax.ShapeDtypeStruct((acq, parts, rows, cols), scenes.dtype) for rows in sizes],
+        in_specs=[pl.BlockSpec(memory_space=pltpu.HBM)],
+        out_specs=[vmem] * len(sizes),
+        scratch_shapes=[pltpu.SemaphoreType.DMA((len(sizes),))],
+        compiler_params=pltpu.CompilerParams(vmem_limit_bytes=SMALL_VMEM),
+        name="cut_rows",
+    )(scenes)
+
+
 def split(x, count):
     pieces = []
     for _ in range(count):
@@ -45,7 +74,7 @@
     return pieces
 
 
-def phase_kernel(start, pairs_ref, far_ref, own_ref, near_ref, ones_ref, *refs):
+def phase_kernel(pairs_ref, far_ref, own_ref, near_ref, ones_ref, *refs):
     *earlier, out_ref, stack, sums = refs
     pair_count = pairs_ref.shape[0]
     acq, _, rows, cols = far_ref.shape
@@ -54,12 +83,11 @@
     picks = [(pairs_ref[p, 0], pairs_ref[p, 1]) for p in range(pair_count)]
 
     def band(b, carry):
-        own_rows = pl.ds(pl.multiple_of(start + b * BAND, BAND), BAND)
-        far_rows = pl.ds(pl.multiple_of(b * BAND, BAND), BAND)
+        at = pl.ds(pl.multiple_of(b * BAND, BAND), BAND)
 
         def widen(j, carry):
             lanes = pl.ds(pl.multiple_of(j * LANES, LANES), LANES)
-            for side, (ref, at) in enumerate(((far_ref, far_rows), (own_ref, own_rows), (near_ref, own_rows))):
+            for side, ref in enumerate((far_ref, own_ref, near_ref)):
                 for a in range(acq):
                     for part in range(2):
                         stack[side * acq + a, part, j] = ref[a, part, at, lanes].astype(jnp.float32)
@@ -101,14 +129,14 @@
             )
 
 
-def chunk_phase(start, pairs, far, own, near, ones, earlier=()):
+def chunk_phase(pairs, far, own, near, ones, earlier=()):
     acq, parts, rows, cols = far.shape
     looked = rows // LOOK_R
     pair_count = pairs.shape[0]
     total = looked + sum(x.shape[0] for x in earlier)
     vmem = pl.BlockSpec(memory_space=pltpu.VMEM)
     return pl.pallas_call(
-        functools.partial(phase_kernel, start),
+        phase_kernel,
         out_shape=jax.ShapeDtypeStruct((total, SLOT_PAD, cols // LOOK_C), jnp.float32),
         in_specs=[pl.BlockSpec(memory_space=pltpu.SMEM)] + [vmem] * (4 + len(earlier)),
         out_specs=vmem,
@@ -116,17 +144,19 @@
             pltpu.VMEM((3 * acq, parts, cols // LANES, BAND, LANES), jnp.float32),
             pltpu.VMEM((2, rows // BAND, 2 * pair_count * BAND // LOOK_R, cols), jnp.bfloat16),
         ],
-        compiler_params=pltpu.CompilerParams(vmem_limit_bytes=24 * 2**20),
+        compiler_params=pltpu.CompilerParams(vmem_limit_bytes=PHASE_VMEM),
         name="pair_phase",
     )(pairs, far, own, near, ones, *earlier)
 
 
-def slots_kernel(owner_ref, pinv_ref, out_ref):
+def constants_kernel(owner_ref, pinv_ref, slots_ref, ones_ref):
     count = pinv_ref.shape[1]
     row = lax.broadcasted_iota(jnp.int32, (count, owner_ref.shape[1]), 0)
     pick = (row == owner_ref[...]).astype(jnp.bfloat16)
     for piece, value in enumerate(split(pinv_ref[...], 3)):
-        out_ref[piece] = jnp.dot(value, pick, preferred_element_type=jnp.float32).astype(jnp.bfloat16)
+        slots_ref[piece] = jnp.dot(value, pick, preferred_element_type=jnp.float32).astype(jnp.bfloat16)
+    col = lax.broadcasted_iota(jnp.int32, ones_ref.shape, 0) // LOOK_C
+    ones_ref[...] = (col == lax.broadcasted_iota(jnp.int32, ones_ref.shape, 1)).astype(jnp.bfloat16)
 
 
 def series_kernel(slots_ref, phase_ref, out_ref):
@@ -152,41 +182,38 @@
     local = pairs - (me - 1) * acq
     local = jnp.where(me % 2 == 1, (2 - local // acq) * acq + local % acq, local)
 
-    chunks, halos, start = [], [], 0
-    rest, near = scenes, None
-    for k, step in enumerate(CHUNKS):
-        chunk = lax.slice_in_dim(rest, start, start + step, axis=2)
-        rest, chunk = lax.optimization_barrier((rest, chunk))
-        halos.append(lax.ppermute(chunk, "acq", far_pairs))
-        chunks.append(start)
-        start += step
-        if k == 0:
-            near = lax.ppermute(rest, "acq", near_pairs)
-            rest, near = lax.optimization_barrier((rest, near))
-        else:
-            rest, halos[k - 1] = lax.optimization_barrier((rest, halos[k - 1]))
-
-    ones = (
-        lax.broadcasted_iota(jnp.int32, (cols, cols // LOOK_C), 0) // LOOK_C
-        == lax.broadcasted_iota(jnp.int32, (cols, cols // LOOK_C), 1)
-    ).astype(jnp.bfloat16)
     owner = jnp.pad(pair_owner.reshape(count, pair_count), ((0, 0), (0, SLOT_PAD - pair_count)), constant_values=-1)
-    slots = pl.pallas_call(
-        slots_kernel,
-        out_shape=jax.ShapeDtypeStruct((3, design_pinv.shape[0], count * SLOT_PAD), jnp.bfloat16),
-        name="slot_pinv",
+    slots, ones = pl.pallas_call(
+        constants_kernel,
+        out_shape=[
+            jax.ShapeDtypeStruct((3, design_pinv.shape[0], count * SLOT_PAD), jnp.bfloat16),
+            jax.ShapeDtypeStruct((cols, cols // LOOK_C), jnp.bfloat16),
+        ],
+        compiler_params=pltpu.CompilerParams(vmem_limit_bytes=SMALL_VMEM),
+        name="constants",
     )(owner.reshape(1, count * SLOT_PAD), design_pinv)
 
-    phases = []
-    for k, (start, far) in enumerate(zip(chunks, halos)):
-        if k == 0:
-            far, slots = lax.optimization_barrier((far, slots))
+    def swap(chunk):
+        return lax.ppermute(chunk, "acq", far_pairs), lax.ppermute(chunk, "acq", near_pairs)
+
+    chunks = [lax.slice_in_dim(scenes, 0, CHUNKS[0], axis=2)]
+    halos, phases = [swap(chunks[0])], []
+    rest, slots, ones, chunks[0] = lax.optimization_barrier((scenes, slots, ones, chunks[0]))
+    chunks += list(cut_rows(rest, CHUNKS[0], CHUNKS[1:]))
+    halos.append(swap(chunks[1]))
+    for k, chunk in enumerate(chunks):
+        far, near = halos[k]
         last = k == len(chunks) - 1
-        phases.append(chunk_phase(start, local, far, scenes, near, ones, phases if last else ()))
+        phases.append(chunk_phase(local, far, chunk, near, ones, phases if last else ()))
+        if k + 2 < len(chunks):
+            done = phases if k == 0 else halos
+            chunks[k + 2], done[k] = lax.optimization_barrier((chunks[k + 2], done[k]))
+            halos.append(swap(chunks[k + 2]))
     phase = lax.all_to_all(phases[-1], "acq", split_axis=0, concat_axis=0)
     return pl.pallas_call(
         series_kernel,
         out_shape=jax.ShapeDtypeStruct((1, slots.shape[1], phase.shape[2]), jnp.float32),
+        compiler_params=pltpu.CompilerParams(vmem_limit_bytes=SMALL_VMEM),
         name="series",
     )(slots, phase)
 

time: 85.9 us -> 82.5 us (0.960)
  local copies, waits for them, and re-layouts: 12.9 us -> 5.66 us
  starting transfers between devices: 8.98 us -> 13 us
  waiting for transfers between devices: 19.4 us -> 21.2 us
  other arithmetic: 1.73 us -> 0.02 us
    slice x3 -> x1, local copies, waits for them, and re-layouts: 5.66 us -> 1.33 us  [body(): chunks = [lax.slice_in_dim(scenes, 0, CHUNKS[0], axis=2)]]
    ppermute x4 -> x8, starting transfers between devices: 8.98 us -> 13 us  [the longest x4 9.61 us: swap(): lax.ppermute(chunk, 'acq', far_pairs)]
    unnamed x13 -> x17, local copies, waits for them, and re-layouts: 6.42 us -> 4.1 us
    ppermute x4 -> x8, waiting for transfers between devices: 19.4 us -> 21.2 us  [the longest x4 21.2 us: swap(): lax.ppermute(chunk, 'acq', far_pairs)]
    convert_element_type x1 -> x0, other arithmetic: 1.7 us -> none  [body(): ones = (lax.broadcasted_iota(jnp.int32, (cols, cols // LOOK_C), 0) // LOO...]
    pallas_call x1, Pallas kernels: 2.07 us -> 1 us  [body(): pl.pallas_call(series_kernel, out_shape=jax.ShapeDtypeStruct((1, slots.sh...]
    pallas_call x4 -> x6, Pallas kernels: 15.5 us -> 16.4 us  [the longest x4 15.6 us: chunk_phase(): pl.pallas_call(phase_kernel, out_shape=jax.ShapeDtypeStruct((total, SLOT_...]
  transfers between devices with their start and end apart: 4 -> 8, of which waited for: 4 -> 4; matrix products, arithmetic and copies ran while one was open for 6% -> 0% of each run, Pallas kernels for 16% -> 17%
where the time goes in v5:
time: 82.5 us; the launch traced here: 82.2 us
  blocking collectives  24.7 us (30%)
  waiting for transfers between devices  21.2 us (26%)
  Pallas kernels  17.4 us (21%)
  starting transfers between devices  13 us (16%)
  local copies, waits for them, and re-layouts  5.66 us (7%)
    all_to_all x1, blocking collectives, body(): phase = lax.all_to_all(phases[-1], 'acq', split_axis=0, concat_axis=0)  24.7 us
    ppermute x4, waiting for transfers between devices, swap(): lax.ppermute(chunk, 'acq', far_pairs)  21.2 us
    pallas_call x4, Pallas kernels, chunk_phase(): pl.pallas_call(phase_kernel, out_shape=jax.ShapeDtypeStruct((total, SLOT_...  15.6 us
    ppermute x4, starting transfers between devices, swap(): lax.ppermute(chunk, 'acq', far_pairs)  9.61 us
    unnamed x17, local copies, waits for them, and re-layouts  4.1 us
    ppermute x4, starting transfers between devices, swap(): lax.ppermute(chunk, 'acq', near_pairs)  3.43 us
  transfers between devices with their start and end apart: 8, of which 4 were waited for; matrix products, arithmetic and copies ran while one was open for 0% of the time, Pallas kernels for 17%

profile of v5, /device:TPU:1, one launch (start us, length us, event | category | flops | bytes accessed | tf_op | source)
XLA Modules:
  0.0 82.2 jit_solution(14766146826996661636)
XLA Ops:
  0.0 1.3 %slice.3.own_ref = bf16[2,2,64,2048]{3,2,1,0:T(8,128)(2,1)S(1)} slice(bf16[2,2,256,2048]{3,2,1,0:T(8,128)(2,1)} %scenes_ref), slice={[0:2], [0:2], [0:64], [0:2048]} | slice | bytes 2097152 | tf_op jit(solution)/shard_map/slice | solution.py:199
  1.3 3.3 %collective-permute-start.5 = (bf16[2,2,64,2048]{3,2,1,0:T(8,128)(2,1)S(1)}, bf16[2,2,64,2048]{3,2,1,0:T(8,128)(2,1)}, u32[]{:S(2)}, u32[]{:S(2)}) collective-permute-start(bf16[2,2,64,2048]{3,2,1,0:T(8,128)(2,1)S(1)} %slice.3.own_ref), channel_id=1, source_target_pairs={{0,4},{4,0},{8,12},{12,8},{16,20},{20,16},{24,28},{28,24},{32,36},... | collective-permute-start | bytes 3145736 | tf_op jit(solution)/shard_map/ppermute | solution.py:197
  4.7 1.9 %collective-permute-start.4 = (bf16[2,2,64,2048]{3,2,1,0:T(8,128)(2,1)S(1)}, bf16[2,2,64,2048]{3,2,1,0:T(8,128)(2,1)}, u32[]{:S(2)}, u32[]{:S(2)}) collective-permute-start(bf16[2,2,64,2048]{3,2,1,0:T(8,128)(2,1)S(1)} %slice.3.own_ref), channel_id=1, source_target_pairs={{4,8},{8,4},{12,16},{16,12},{20,24},{24,20},{28,32},{32,28},{36,40... | collective-permute-start | bytes 3145736 | tf_op jit(solution)/shard_map/ppermute | solution.py:197
  6.6 0.1 reshape.6
  6.8 0.6 constants.1
  7.4 2.2 %copy-done = bf16[2,2,256,2048]{3,2,1,0:T(8,128)(2,1)S(1)} copy-done((bf16[2,2,256,2048]{3,2,1,0:T(8,128)(2,1)S(1)}, bf16[2,2,256,2048]{3,2,1,0:T(8,128)(2,1)}, u32[]{:S(2)}) %copy-start) | copy-done | bytes 4194328
  9.6 0.2 cut_rows.1
  9.9 1.0 %copy-done.1 = bf16[2,2,64,2048]{3,2,1,0:T(8,128)(2,1)} copy-done((bf16[2,2,64,2048]{3,2,1,0:T(8,128)(2,1)}, bf16[2,2,64,2048]{3,2,1,0:T(8,128)(2,1)S(1)}, u32[]{:S(2)}) %copy-start.1) | copy-done | bytes 1048600
  10.9 0.8 copy-done.3
  11.7 3.6 %collective-permute-start = (bf16[2,2,96,2048]{3,2,1,0:T(8,128)(2,1)S(1)}, bf16[2,2,96,2048]{3,2,1,0:T(8,128)(2,1)}, u32[]{:S(2)}, u32[]{:S(2)}) collective-permute-start(bf16[2,2,96,2048]{3,2,1,0:T(8,128)(2,1)S(1)} %get-tuple-element.22.own_ref), channel_id=1, source_target_pairs={{4,8},{8,4},{12,16},{16,12},{20,24},{24,20},{28,32},{32,28},{36,40... | collective-permute-start | bytes 4718600 | tf_op jit(solution)/shard_map/ppermute | solution.py:197
  15.3 0.1 copy.6
  15.5 5.4 %collective-permute-done.4.far_ref = bf16[2,2,64,2048]{3,2,1,0:T(8,128)(2,1)} collective-permute-done((bf16[2,2,64,2048]{3,2,1,0:T(8,128)(2,1)S(1)}, bf16[2,2,64,2048]{3,2,1,0:T(8,128)(2,1)}, u32[]{:S(2)}, u32[]{:S(2)}) %collective-permute-start.4) | collective-permute-done | bytes 1048608 | tf_op jit(solution)/shard_map/ppermute | solution.py:197
  20.9 4.3 %pair_phase.4.refs_0_ = f32[16,8,128]{2,1,0:T(8,128)S(1)} custom-call(s32[6,2]{1,0:T(8,128)S(1)} %fusion.3.pairs_ref, bf16[2,2,64,2048]{3,2,1,0:T(8,128)(2,1)} %collective-permute-done.4.far_ref, bf16[2,2,64,2048]{3,2,1,0:T(8,128)(2,1)S(1)} %slice.3.own_ref, bf16[2,2,64,2048]{3,2,1,0:T(8,128)(2,1)} %collective-permute-done.5.near_ref, ...), custom_call_target="tpu_custom_call" | custom-call | tf_op jit(solution)/shard_map/pair_phase/pallas_call | solution.py:138
  25.2 0.1 collective-permute-start.7
  25.3 2.0 %collective-permute-start.6 = (bf16[2,2,64,2048]{3,2,1,0:T(8,128)(2,1)S(1)}, bf16[2,2,64,2048]{3,2,1,0:T(8,128)(2,1)S(1)}, u32[]{:S(2)}, u32[]{:S(2)}) collective-permute-start(bf16[2,2,64,2048]{3,2,1,0:T(8,128)(2,1)S(1)} %copy-done.2), channel_id=1, source_target_pairs={{4,8},{8,4},{12,16},{16,12},{20,24},{24,20},{28,32},{32,28},{36,40... | collective-permute-start | bytes 3145736 | tf_op jit(solution)/shard_map/ppermute | solution.py:197
  27.4 10.4 %collective-permute-done.far_ref = bf16[2,2,96,2048]{3,2,1,0:T(8,128)(2,1)} collective-permute-done((bf16[2,2,96,2048]{3,2,1,0:T(8,128)(2,1)S(1)}, bf16[2,2,96,2048]{3,2,1,0:T(8,128)(2,1)}, u32[]{:S(2)}, u32[]{:S(2)}) %collective-permute-start) | collective-permute-done | bytes 1572896 | tf_op jit(solution)/shard_map/ppermute | solution.py:197
  37.7 2.0 %collective-permute-start.2 = (bf16[2,2,32,2048]{3,2,1,0:T(8,128)(2,1)S(1)}, bf16[2,2,32,2048]{3,2,1,0:T(8,128)(2,1)S(1)}, u32[]{:S(2)}, u32[]{:S(2)}) collective-permute-start(bf16[2,2,32,2048]{3,2,1,0:T(8,128)(2,1)S(1)} %copy-done.4), channel_id=1, source_target_pairs={{4,8},{8,4},{12,16},{16,12},{20,24},{24,20},{28,32},{32,28},{36,40... | collective-permute-start | bytes 1572872 | tf_op jit(solution)/shard_map/ppermute | solution.py:197
  39.8 5.9 %pair_phase.5.refs_1_ = f32[24,8,128]{2,1,0:T(8,128)S(1)} custom-call(s32[6,2]{1,0:T(8,128)S(1)} %fusion.3.pairs_ref, bf16[2,2,96,2048]{3,2,1,0:T(8,128)(2,1)} %collective-permute-done.far_ref, bf16[2,2,96,2048]{3,2,1,0:T(8,128)(2,1)S(1)} %get-tuple-element.22.own_ref, bf16[2,2,96,2048]{3,2,1,0:T(8,128)(2,1)} %collective-permute-done.1.near_ref, ...), custom_call_target="tpu_custom_call" | custom-call | tf_op jit(solution)/shard_map/pair_phase/pallas_call | solution.py:138
  45.7 3.2 %collective-permute-done.6.far_ref = bf16[2,2,64,2048]{3,2,1,0:T(8,128)(2,1)S(1)} collective-permute-done((bf16[2,2,64,2048]{3,2,1,0:T(8,128)(2,1)S(1)}, bf16[2,2,64,2048]{3,2,1,0:T(8,128)(2,1)S(1)}, u32[]{:S(2)}, u32[]{:S(2)}) %collective-permute-start.6) | collective-permute-done | bytes 1048608 | tf_op jit(solution)/shard_map/ppermute | solution.py:197
  48.9 3.4 %pair_phase.6.refs_2_ = f32[16,8,128]{2,1,0:T(8,128)S(1)} custom-call(s32[6,2]{1,0:T(8,128)S(1)} %fusion.3.pairs_ref, bf16[2,2,64,2048]{3,2,1,0:T(8,128)(2,1)S(1)} %collective-permute-done.6.far_ref, bf16[2,2,64,2048]{3,2,1,0:T(8,128)(2,1)S(1)} %copy-done.2, bf16[2,2,64,2048]{3,2,1,0:T(8,128)(2,1)S(1)} %collective-permute-done.7.near_ref, ...), custom_call_target="tpu_custom_call" | custom-call | tf_op jit(solution)/shard_map/pair_phase/pallas_call | solution.py:138
  52.2 2.2 %collective-permute-done.2.far_ref = bf16[2,2,32,2048]{3,2,1,0:T(8,128)(2,1)S(1)} collective-permute-done((bf16[2,2,32,2048]{3,2,1,0:T(8,128)(2,1)S(1)}, bf16[2,2,32,2048]{3,2,1,0:T(8,128)(2,1)S(1)}, u32[]{:S(2)}, u32[]{:S(2)}) %collective-permute-start.2) | collective-permute-done | bytes 524320 | tf_op jit(solution)/shard_map/ppermute | solution.py:197
  54.5 2.0 %pair_phase.7 = f32[64,8,128]{2,1,0:T(8,128)S(1)} custom-call(s32[6,2]{1,0:T(8,128)S(1)} %fusion.3.pairs_ref, bf16[2,2,32,2048]{3,2,1,0:T(8,128)(2,1)S(1)} %collective-permute-done.2.far_ref, bf16[2,2,32,2048]{3,2,1,0:T(8,128)(2,1)S(1)} %copy-done.4, bf16[2,2,32,2048]{3,2,1,0:T(8,128)(2,1)S(1)} %collective-permute-done.3.near_ref, ...), custom_call_target="tpu_custom_call" | custom-call | tf_op jit(solution)/shard_map/pair_phase/pallas_call | solution.py:138
  56.5 24.7 %all_to_all.5.phase_ref = f32[64,8,128]{2,1,0:T(8,128)S(1)} all-to-all(f32[64,8,128]{2,1,0:T(8,128)S(1)} %pair_phase.7), channel_id=1, replica_groups=mesh['acq'=64,'rng'=4] {'acq'}, dimensions={0} | all-to-all | bytes 524288 | tf_op jit(solution)/shard_map/all_to_all | solution.py:212
  81.2 1.0 %series.1 = f32[1,128,128]{2,1,0:T(8,128)} custom-call(bf16[3,128,512]{2,1,0:T(8,128)(2,1)S(1)} %get-tuple-element.19.slots_ref, f32[64,8,128]{2,1,0:T(8,128)S(1)} %all_to_all.5.phase_ref), custom_call_target="tpu_custom_call" | custom-call | tf_op jit(solution)/shard_map/series/pallas_call | solution.py:213
  (22 shorter events, 0.2 us)
Async XLA Ops:
  0.0 6.6 %copy-start.6 = (s32[384]{0:T(512)S(1)}, s32[384]{0:T(512)}, u32[]{:S(2)}) copy-start(s32[384]{0:T(512)} %param.6) | copy-start | bytes 4612
  0.0 6.8 %copy-start.5 = (f32[128,384]{1,0:T(8,128)S(1)}, f32[128,384]{1,0:T(8,128)}, u32[]{:S(2)}) copy-start(f32[128,384]{1,0:T(8,128)} %pinv_ref.1) | copy-start | bytes 589828
  1.3 14.1 %collective-permute-start.5 = (bf16[2,2,64,2048]{3,2,1,0:T(8,128)(2,1)S(1)}, bf16[2,2,64,2048]{3,2,1,0:T(8,128)(2,1)}, u32[]{:S(2)}, u32[]{:S(2)}) collective-permute-start(bf16[2,2,64,2048]{3,2,1,0:T(8,128)(2,1)S(1)} %slice.3.own_ref), channel_id=1, source_target_pairs={{0,4},{4,0},{8,12},{12,8},{16,20},{20,16},{24,28},{28,24},{32,36},... | collective-permute-start | bytes 3145736 | tf_op jit(solution)/shard_map/ppermute | solution.py:197
  4.7 16.2 %collective-permute-start.4 = (bf16[2,2,64,2048]{3,2,1,0:T(8,128)(2,1)S(1)}, bf16[2,2,64,2048]{3,2,1,0:T(8,128)(2,1)}, u32[]{:S(2)}, u32[]{:S(2)}) collective-permute-start(bf16[2,2,64,2048]{3,2,1,0:T(8,128)(2,1)S(1)} %slice.3.own_ref), channel_id=1, source_target_pairs={{4,8},{8,4},{12,16},{16,12},{20,24},{24,20},{28,32},{32,28},{36,40... | collective-permute-start | bytes 3145736 | tf_op jit(solution)/shard_map/ppermute | solution.py:197
  7.4 2.2 %copy-start = (bf16[2,2,256,2048]{3,2,1,0:T(8,128)(2,1)S(1)}, bf16[2,2,256,2048]{3,2,1,0:T(8,128)(2,1)}, u32[]{:S(2)}) copy-start(bf16[2,2,256,2048]{3,2,1,0:T(8,128)(2,1)} %scenes_ref) | copy-start | bytes 12582916
  9.6 5.7 %copy-start.7 = (s32[6,2]{0,1:T(2,128)S(1)}, s32[6,2]{0,1:T(2,128)}, u32[]{:S(2)}) copy-start(s32[6,2]{0,1:T(2,128)} %param.5) | copy-start | bytes 148
  9.9 1.0 %copy-start.1 = (bf16[2,2,64,2048]{3,2,1,0:T(8,128)(2,1)}, bf16[2,2,64,2048]{3,2,1,0:T(8,128)(2,1)S(1)}, u32[]{:S(2)}) copy-start(bf16[2,2,64,2048]{3,2,1,0:T(8,128)(2,1)S(1)} %get-tuple-element.28.own_ref) | copy-start | bytes 3145732
  10.9 0.8 copy-start.3
  11.7 15.7 %collective-permute-start.1 = (bf16[2,2,96,2048]{3,2,1,0:T(8,128)(2,1)S(1)}, bf16[2,2,96,2048]{3,2,1,0:T(8,128)(2,1)}, u32[]{:S(2)}, u32[]{:S(2)}) collective-permute-start(bf16[2,2,96,2048]{3,2,1,0:T(8,128)(2,1)S(1)} %get-tuple-element.22.own_ref), channel_id=1, source_target_pairs={{0,4},{4,0},{8,12},{12,8},{16,20},{20,16},{24,28},{28,24},{32,36},... | collective-permute-start | bytes 4718600 | tf_op jit(solution)/shard_map/ppermute | solution.py:197
  11.7 26.1 %collective-permute-start = (bf16[2,2,96,2048]{3,2,1,0:T(8,128)(2,1)S(1)}, bf16[2,2,96,2048]{3,2,1,0:T(8,128)(2,1)}, u32[]{:S(2)}, u32[]{:S(2)}) collective-permute-start(bf16[2,2,96,2048]{3,2,1,0:T(8,128)(2,1)S(1)} %get-tuple-element.22.own_ref), channel_id=1, source_target_pairs={{4,8},{8,4},{12,16},{16,12},{20,24},{24,20},{28,32},{32,28},{36,40... | collective-permute-start | bytes 4718600 | tf_op jit(solution)/shard_map/ppermute | solution.py:197
  15.5 9.7 %copy-start.2 = (bf16[2,2,64,2048]{3,2,1,0:T(8,128)(2,1)S(1)}, bf16[2,2,64,2048]{3,2,1,0:T(8,128)(2,1)}, u32[]{:S(2)}) copy-start(bf16[2,2,64,2048]{3,2,1,0:T(8,128)(2,1)} %copy-done.1) | copy-start | bytes 3145732
  15.5 22.3 %copy-start.4 = (bf16[2,2,32,2048]{3,2,1,0:T(8,128)(2,1)S(1)}, bf16[2,2,32,2048]{3,2,1,0:T(8,128)(2,1)}, u32[]{:S(2)}) copy-start(bf16[2,2,32,2048]{3,2,1,0:T(8,128)(2,1)} %copy-done.3) | copy-start | bytes 1572868
  25.2 20.5 %collective-permute-start.7 = (bf16[2,2,64,2048]{3,2,1,0:T(8,128)(2,1)S(1)}, bf16[2,2,64,2048]{3,2,1,0:T(8,128)(2,1)S(1)}, u32[]{:S(2)}, u32[]{:S(2)}) collective-permute-start(bf16[2,2,64,2048]{3,2,1,0:T(8,128)(2,1)S(1)} %copy-done.2), channel_id=1, source_target_pairs={{0,4},{4,0},{8,12},{12,8},{16,20},{20,16},{24,28},{28,24},{32,36},... | collective-permute-start | bytes 3145736 | tf_op jit(solution)/shard_map/ppermute | solution.py:197
  25.3 23.6 %collective-permute-start.6 = (bf16[2,2,64,2048]{3,2,1,0:T(8,128)(2,1)S(1)}, bf16[2,2,64,2048]{3,2,1,0:T(8,128)(2,1)S(1)}, u32[]{:S(2)}, u32[]{:S(2)}) collective-permute-start(bf16[2,2,64,2048]{3,2,1,0:T(8,128)(2,1)S(1)} %copy-done.2), channel_id=1, source_target_pairs={{4,8},{8,4},{12,16},{16,12},{20,24},{24,20},{28,32},{32,28},{36,40... | collective-permute-start | bytes 3145736 | tf_op jit(solution)/shard_map/ppermute | solution.py:197
  37.7 14.5 %collective-permute-start.3 = (bf16[2,2,32,2048]{3,2,1,0:T(8,128)(2,1)S(1)}, bf16[2,2,32,2048]{3,2,1,0:T(8,128)(2,1)S(1)}, u32[]{:S(2)}, u32[]{:S(2)}) collective-permute-start(bf16[2,2,32,2048]{3,2,1,0:T(8,128)(2,1)S(1)} %copy-done.4), channel_id=1, source_target_pairs={{0,4},{4,0},{8,12},{12,8},{16,20},{20,16},{24,28},{28,24},{32,36},... | collective-permute-start | bytes 1572872 | tf_op jit(solution)/shard_map/ppermute | solution.py:197
  37.7 16.7 %collective-permute-start.2 = (bf16[2,2,32,2048]{3,2,1,0:T(8,128)(2,1)S(1)}, bf16[2,2,32,2048]{3,2,1,0:T(8,128)(2,1)S(1)}, u32[]{:S(2)}, u32[]{:S(2)}) collective-permute-start(bf16[2,2,32,2048]{3,2,1,0:T(8,128)(2,1)S(1)} %copy-done.4), channel_id=1, source_target_pairs={{4,8},{8,4},{12,16},{16,12},{20,24},{24,20},{28,32},{32,28},{36,40... | collective-permute-start | bytes 1572872 | tf_op jit(solution)/shard_map/ppermute | solution.py:197

commit v6 on v5

--- a/solution.py
+++ b/solution.py
@@ -15,7 +15,6 @@
 BAND = 32
 PHASE_VMEM = 10 * 2**20
 SMALL_VMEM = 6 * 2**20
-SLOT_PAD = 8
 UNROLL_A = 2
 UNROLL_B = 2
 
@@ -117,16 +116,15 @@
     dots = jnp.dot(pieces, ones_ref[...], preferred_element_type=jnp.float32)
     dots = dots.reshape(2, bands, pair_count, 2, looked, dots.shape[1])
     both = dots[0] + dots[1]
+    width = dots.shape[-1]
     angle = atan_ratio(both[:, :, 1], both[:, :, 0])
     at = 0
     for ref in earlier:
         out_ref[pl.ds(at, ref.shape[0])] = ref[...]
         at += ref.shape[0]
     for b in range(bands):
-        for p in range(SLOT_PAD):
-            out_ref[pl.ds(at + b * looked, looked), p, :] = (
-                angle[b, p] if p < pair_count else jnp.zeros_like(angle[b, 0])
-            )
+        for p in range(pair_count):
+            out_ref[pl.ds(at + b * looked, looked), 0, pl.ds(p * width, width)] = angle[b, p]
 
 
 def chunk_phase(pairs, far, own, near, ones, earlier=()):
@@ -137,7 +135,7 @@
     vmem = pl.BlockSpec(memory_space=pltpu.VMEM)
     return pl.pallas_call(
         phase_kernel,
-        out_shape=jax.ShapeDtypeStruct((total, SLOT_PAD, cols // LOOK_C), jnp.float32),
+        out_shape=jax.ShapeDtypeStruct((total, 1, pair_count * (cols // LOOK_C)), jnp.float32),
         in_specs=[pl.BlockSpec(memory_space=pltpu.SMEM)] + [vmem] * (4 + len(earlier)),
         out_specs=vmem,
         scratch_shapes=[
@@ -161,7 +159,10 @@
 
 def series_kernel(slots_ref, phase_ref, out_ref):
     acqs, width = slots_ref.shape[1:]
-    phase = split(phase_ref[...].reshape(width, phase_ref.shape[2]), 3)
+    count, _, lanes = phase_ref.shape
+    lanes = lanes * count // width
+    phase = [phase_ref[:, 0, pl.ds(p * lanes, lanes)] for p in range(width // count)]
+    phase = split(jnp.concatenate(phase, axis=0), 3)
     total = None
     for piece in reversed(range(3)):
         rows = slots_ref[pl.ds(0, 3 - piece)].reshape((3 - piece) * acqs, width)
@@ -182,16 +183,16 @@
     local = pairs - (me - 1) * acq
     local = jnp.where(me % 2 == 1, (2 - local // acq) * acq + local % acq, local)
 
-    owner = jnp.pad(pair_owner.reshape(count, pair_count), ((0, 0), (0, SLOT_PAD - pair_count)), constant_values=-1)
+    owner = pair_owner.reshape(count, pair_count).T.reshape(1, count * pair_count)
     slots, ones = pl.pallas_call(
         constants_kernel,
         out_shape=[
-            jax.ShapeDtypeStruct((3, design_pinv.shape[0], count * SLOT_PAD), jnp.bfloat16),
+            jax.ShapeDtypeStruct((3, design_pinv.shape[0], count * pair_count), jnp.bfloat16),
             jax.ShapeDtypeStruct((cols, cols // LOOK_C), jnp.bfloat16),
         ],
         compiler_params=pltpu.CompilerParams(vmem_limit_bytes=SMALL_VMEM),
         name="constants",
-    )(owner.reshape(1, count * SLOT_PAD), design_pinv)
+    )(owner, design_pinv)
 
     def swap(chunk):
         return lax.ppermute(chunk, "acq", far_pairs), lax.ppermute(chunk, "acq", near_pairs)
@@ -212,7 +213,7 @@
     phase = lax.all_to_all(phases[-1], "acq", split_axis=0, concat_axis=0)
     return pl.pallas_call(
         series_kernel,
-        out_shape=jax.ShapeDtypeStruct((1, slots.shape[1], phase.shape[2]), jnp.float32),
+        out_shape=jax.ShapeDtypeStruct((1, slots.shape[1], cols // LOOK_C), jnp.float32),
         compiler_params=pltpu.CompilerParams(vmem_limit_bytes=SMALL_VMEM),
         name="series",
     )(slots, phase)

time: 82.5 us -> 81.4 us (0.987)
  blocking collectives: 24.7 us -> 23.5 us
    all_to_all x1, blocking collectives: 24.7 us -> 23.5 us  [body(): phase = lax.all_to_all(phases[-1], 'acq', split_axis=0, concat_axis=0)]
  transfers between devices with their start and end apart: 8 -> 8, of which waited for: 4 -> 4; matrix products, arithmetic and copies ran while one was open for 0% -> 0% of each run, Pallas kernels for 17% -> 18%
where the time goes in v6:
time: 81.4 us; the launch traced here: 81.1 us
  blocking collectives  23.5 us (29%)
  waiting for transfers between devices  21.2 us (26%)
  Pallas kernels  17.4 us (21%)
  starting transfers between devices  13 us (16%)
  local copies, waits for them, and re-layouts  5.72 us (7%)
    all_to_all x1, blocking collectives, body(): phase = lax.all_to_all(phases[-1], 'acq', split_axis=0, concat_axis=0)  23.5 us
    ppermute x4, waiting for transfers between devices, swap(): lax.ppermute(chunk, 'acq', far_pairs)  21.1 us
    pallas_call x4, Pallas kernels, chunk_phase(): pl.pallas_call(phase_kernel, out_shape=jax.ShapeDtypeStruct((total, 1, pa...  15.6 us
    ppermute x4, starting transfers between devices, swap(): lax.ppermute(chunk, 'acq', far_pairs)  9.61 us
    unnamed x17, local copies, waits for them, and re-layouts  4.1 us
    ppermute x4, starting transfers between devices, swap(): lax.ppermute(chunk, 'acq', near_pairs)  3.43 us
  transfers between devices with their start and end apart: 8, of which 4 were waited for; matrix products, arithmetic and copies ran while one was open for 0% of the time, Pallas kernels for 18%

profile of v6, /device:TPU:1, one launch (start us, length us, event | category | flops | bytes accessed | tf_op | source)
XLA Modules:
  0.0 81.1 jit_solution(15174799012188828194)
XLA Ops:
  0.0 1.3 %slice.3.own_ref = bf16[2,2,64,2048]{3,2,1,0:T(8,128)(2,1)S(1)} slice(bf16[2,2,256,2048]{3,2,1,0:T(8,128)(2,1)} %scenes_ref), slice={[0:2], [0:2], [0:64], [0:2048]} | slice | bytes 2097152 | tf_op jit(solution)/shard_map/slice | solution.py:200
  1.3 3.3 %collective-permute-start.5 = (bf16[2,2,64,2048]{3,2,1,0:T(8,128)(2,1)S(1)}, bf16[2,2,64,2048]{3,2,1,0:T(8,128)(2,1)}, u32[]{:S(2)}, u32[]{:S(2)}) collective-permute-start(bf16[2,2,64,2048]{3,2,1,0:T(8,128)(2,1)S(1)} %slice.3.own_ref), channel_id=1, source_target_pairs={{0,4},{4,0},{8,12},{12,8},{16,20},{20,16},{24,28},{28,24},{32,36},... | collective-permute-start | bytes 3145736 | tf_op jit(solution)/shard_map/ppermute | solution.py:198
  4.7 1.9 %collective-permute-start.4 = (bf16[2,2,64,2048]{3,2,1,0:T(8,128)(2,1)S(1)}, bf16[2,2,64,2048]{3,2,1,0:T(8,128)(2,1)}, u32[]{:S(2)}, u32[]{:S(2)}) collective-permute-start(bf16[2,2,64,2048]{3,2,1,0:T(8,128)(2,1)S(1)} %slice.3.own_ref), channel_id=1, source_target_pairs={{4,8},{8,4},{12,16},{16,12},{20,24},{24,20},{28,32},{32,28},{36,40... | collective-permute-start | bytes 3145736 | tf_op jit(solution)/shard_map/ppermute | solution.py:198
  6.6 0.1 reshape.6
  6.9 0.5 constants.1
  7.5 2.2 %copy-done = bf16[2,2,256,2048]{3,2,1,0:T(8,128)(2,1)S(1)} copy-done((bf16[2,2,256,2048]{3,2,1,0:T(8,128)(2,1)S(1)}, bf16[2,2,256,2048]{3,2,1,0:T(8,128)(2,1)}, u32[]{:S(2)}) %copy-start) | copy-done | bytes 4194328
  9.6 0.2 cut_rows.1
  9.9 1.0 %copy-done.1 = bf16[2,2,64,2048]{3,2,1,0:T(8,128)(2,1)} copy-done((bf16[2,2,64,2048]{3,2,1,0:T(8,128)(2,1)}, bf16[2,2,64,2048]{3,2,1,0:T(8,128)(2,1)S(1)}, u32[]{:S(2)}) %copy-start.1) | copy-done | bytes 1048600
  10.9 0.8 copy-done.3
  11.7 3.6 %collective-permute-start = (bf16[2,2,96,2048]{3,2,1,0:T(8,128)(2,1)S(1)}, bf16[2,2,96,2048]{3,2,1,0:T(8,128)(2,1)}, u32[]{:S(2)}, u32[]{:S(2)}) collective-permute-start(bf16[2,2,96,2048]{3,2,1,0:T(8,128)(2,1)S(1)} %get-tuple-element.22.own_ref), channel_id=1, source_target_pairs={{4,8},{8,4},{12,16},{16,12},{20,24},{24,20},{28,32},{32,28},{36,40... | collective-permute-start | bytes 4718600 | tf_op jit(solution)/shard_map/ppermute | solution.py:198
  15.4 0.1 copy.7
  15.5 5.4 %collective-permute-done.4.far_ref = bf16[2,2,64,2048]{3,2,1,0:T(8,128)(2,1)} collective-permute-done((bf16[2,2,64,2048]{3,2,1,0:T(8,128)(2,1)S(1)}, bf16[2,2,64,2048]{3,2,1,0:T(8,128)(2,1)}, u32[]{:S(2)}, u32[]{:S(2)}) %collective-permute-start.4) | collective-permute-done | bytes 1048608 | tf_op jit(solution)/shard_map/ppermute | solution.py:198
  20.9 4.3 %pair_phase.4.refs_0_ = f32[16,1,768]{2,1,0:T(1,128)S(1)} custom-call(s32[6,2]{1,0:T(8,128)S(1)} %fusion.3.pairs_ref, bf16[2,2,64,2048]{3,2,1,0:T(8,128)(2,1)} %collective-permute-done.4.far_ref, bf16[2,2,64,2048]{3,2,1,0:T(8,128)(2,1)S(1)} %slice.3.own_ref, bf16[2,2,64,2048]{3,2,1,0:T(8,128)(2,1)} %collective-permute-done.5.near_ref, ...), custom_call_target="tpu_custom_call" | custom-call | tf_op jit(solution)/shard_map/pair_phase/pallas_call | solution.py:136
  25.2 0.1 collective-permute-start.7
  25.3 2.0 %collective-permute-start.6 = (bf16[2,2,64,2048]{3,2,1,0:T(8,128)(2,1)S(1)}, bf16[2,2,64,2048]{3,2,1,0:T(8,128)(2,1)S(1)}, u32[]{:S(2)}, u32[]{:S(2)}) collective-permute-start(bf16[2,2,64,2048]{3,2,1,0:T(8,128)(2,1)S(1)} %copy-done.2), channel_id=1, source_target_pairs={{4,8},{8,4},{12,16},{16,12},{20,24},{24,20},{28,32},{32,28},{36,40... | collective-permute-start | bytes 3145736 | tf_op jit(solution)/shard_map/ppermute | solution.py:198
  27.4 10.4 %collective-permute-done.far_ref = bf16[2,2,96,2048]{3,2,1,0:T(8,128)(2,1)} collective-permute-done((bf16[2,2,96,2048]{3,2,1,0:T(8,128)(2,1)S(1)}, bf16[2,2,96,2048]{3,2,1,0:T(8,128)(2,1)}, u32[]{:S(2)}, u32[]{:S(2)}) %collective-permute-start) | collective-permute-done | bytes 1572896 | tf_op jit(solution)/shard_map/ppermute | solution.py:198
  37.7 2.0 %collective-permute-start.2 = (bf16[2,2,32,2048]{3,2,1,0:T(8,128)(2,1)S(1)}, bf16[2,2,32,2048]{3,2,1,0:T(8,128)(2,1)S(1)}, u32[]{:S(2)}, u32[]{:S(2)}) collective-permute-start(bf16[2,2,32,2048]{3,2,1,0:T(8,128)(2,1)S(1)} %copy-done.4), channel_id=1, source_target_pairs={{4,8},{8,4},{12,16},{16,12},{20,24},{24,20},{28,32},{32,28},{36,40... | collective-permute-start | bytes 1572872 | tf_op jit(solution)/shard_map/ppermute | solution.py:198
  39.8 5.9 %pair_phase.5.refs_1_ = f32[24,1,768]{2,1,0:T(1,128)S(1)} custom-call(s32[6,2]{1,0:T(8,128)S(1)} %fusion.3.pairs_ref, bf16[2,2,96,2048]{3,2,1,0:T(8,128)(2,1)} %collective-permute-done.far_ref, bf16[2,2,96,2048]{3,2,1,0:T(8,128)(2,1)S(1)} %get-tuple-element.22.own_ref, bf16[2,2,96,2048]{3,2,1,0:T(8,128)(2,1)} %collective-permute-done.1.near_ref, ...), custom_call_target="tpu_custom_call" | custom-call | tf_op jit(solution)/shard_map/pair_phase/pallas_call | solution.py:136
  45.7 3.2 %collective-permute-done.6.far_ref = bf16[2,2,64,2048]{3,2,1,0:T(8,128)(2,1)S(1)} collective-permute-done((bf16[2,2,64,2048]{3,2,1,0:T(8,128)(2,1)S(1)}, bf16[2,2,64,2048]{3,2,1,0:T(8,128)(2,1)S(1)}, u32[]{:S(2)}, u32[]{:S(2)}) %collective-permute-start.6) | collective-permute-done | bytes 1048608 | tf_op jit(solution)/shard_map/ppermute | solution.py:198
  48.9 3.4 %pair_phase.6.refs_2_ = f32[16,1,768]{2,1,0:T(1,128)S(1)} custom-call(s32[6,2]{1,0:T(8,128)S(1)} %fusion.3.pairs_ref, bf16[2,2,64,2048]{3,2,1,0:T(8,128)(2,1)S(1)} %collective-permute-done.6.far_ref, bf16[2,2,64,2048]{3,2,1,0:T(8,128)(2,1)S(1)} %copy-done.2, bf16[2,2,64,2048]{3,2,1,0:T(8,128)(2,1)S(1)} %collective-permute-done.7.near_ref, ...), custom_call_target="tpu_custom_call" | custom-call | tf_op jit(solution)/shard_map/pair_phase/pallas_call | solution.py:136
  52.2 2.2 %collective-permute-done.2.far_ref = bf16[2,2,32,2048]{3,2,1,0:T(8,128)(2,1)S(1)} collective-permute-done((bf16[2,2,32,2048]{3,2,1,0:T(8,128)(2,1)S(1)}, bf16[2,2,32,2048]{3,2,1,0:T(8,128)(2,1)S(1)}, u32[]{:S(2)}, u32[]{:S(2)}) %collective-permute-start.2) | collective-permute-done | bytes 524320 | tf_op jit(solution)/shard_map/ppermute | solution.py:198
  54.5 2.0 %pair_phase.7 = f32[64,1,768]{2,1,0:T(1,128)S(1)} custom-call(s32[6,2]{1,0:T(8,128)S(1)} %fusion.3.pairs_ref, bf16[2,2,32,2048]{3,2,1,0:T(8,128)(2,1)S(1)} %collective-permute-done.2.far_ref, bf16[2,2,32,2048]{3,2,1,0:T(8,128)(2,1)S(1)} %copy-done.4, bf16[2,2,32,2048]{3,2,1,0:T(8,128)(2,1)S(1)} %collective-permute-done.3.near_ref, ...), custom_call_target="tpu_custom_call" | custom-call | tf_op jit(solution)/shard_map/pair_phase/pallas_call | solution.py:136
  56.5 23.5 %all_to_all.5.phase_ref = f32[64,1,768]{2,1,0:T(1,128)S(1)} all-to-all(f32[64,1,768]{2,1,0:T(1,128)S(1)} %pair_phase.7), channel_id=1, replica_groups=mesh['acq'=64,'rng'=4] {'acq'}, dimensions={0} | all-to-all | bytes 393216 | tf_op jit(solution)/shard_map/all_to_all | solution.py:213
  80.1 1.0 %series.1 = f32[1,128,128]{2,1,0:T(8,128)} custom-call(bf16[3,128,384]{2,1,0:T(8,128)(2,1)S(1)} %get-tuple-element.19.slots_ref, f32[64,1,768]{2,1,0:T(1,128)S(1)} %all_to_all.5.phase_ref), custom_call_target="tpu_custom_call" | custom-call | tf_op jit(solution)/shard_map/series/pallas_call | solution.py:214
  (22 shorter events, 0.2 us)
Async XLA Ops:
  0.0 6.6 %copy-start.6 = (s32[384]{0:T(512)S(1)}, s32[384]{0:T(512)}, u32[]{:S(2)}) copy-start(s32[384]{0:T(512)} %param.6) | copy-start | bytes 4612
  0.0 6.9 %copy-start.5 = (f32[128,384]{1,0:T(8,128)S(1)}, f32[128,384]{1,0:T(8,128)}, u32[]{:S(2)}) copy-start(f32[128,384]{1,0:T(8,128)} %pinv_ref.1) | copy-start | bytes 589828
  1.3 14.2 %collective-permute-start.5 = (bf16[2,2,64,2048]{3,2,1,0:T(8,128)(2,1)S(1)}, bf16[2,2,64,2048]{3,2,1,0:T(8,128)(2,1)}, u32[]{:S(2)}, u32[]{:S(2)}) collective-permute-start(bf16[2,2,64,2048]{3,2,1,0:T(8,128)(2,1)S(1)} %slice.3.own_ref), channel_id=1, source_target_pairs={{0,4},{4,0},{8,12},{12,8},{16,20},{20,16},{24,28},{28,24},{32,36},... | collective-permute-start | bytes 3145736 | tf_op jit(solution)/shard_map/ppermute | solution.py:198
  4.7 16.2 %collective-permute-start.4 = (bf16[2,2,64,2048]{3,2,1,0:T(8,128)(2,1)S(1)}, bf16[2,2,64,2048]{3,2,1,0:T(8,128)(2,1)}, u32[]{:S(2)}, u32[]{:S(2)}) collective-permute-start(bf16[2,2,64,2048]{3,2,1,0:T(8,128)(2,1)S(1)} %slice.3.own_ref), channel_id=1, source_target_pairs={{4,8},{8,4},{12,16},{16,12},{20,24},{24,20},{28,32},{32,28},{36,40... | collective-permute-start | bytes 3145736 | tf_op jit(solution)/shard_map/ppermute | solution.py:198
  7.4 2.2 %copy-start = (bf16[2,2,256,2048]{3,2,1,0:T(8,128)(2,1)S(1)}, bf16[2,2,256,2048]{3,2,1,0:T(8,128)(2,1)}, u32[]{:S(2)}) copy-start(bf16[2,2,256,2048]{3,2,1,0:T(8,128)(2,1)} %scenes_ref) | copy-start | bytes 12582916
  9.6 5.7 %copy-start.7 = (s32[6,2]{0,1:T(2,128)S(1)}, s32[6,2]{0,1:T(2,128)}, u32[]{:S(2)}) copy-start(s32[6,2]{0,1:T(2,128)} %param.5) | copy-start | bytes 148
  9.9 1.0 %copy-start.1 = (bf16[2,2,64,2048]{3,2,1,0:T(8,128)(2,1)}, bf16[2,2,64,2048]{3,2,1,0:T(8,128)(2,1)S(1)}, u32[]{:S(2)}) copy-start(bf16[2,2,64,2048]{3,2,1,0:T(8,128)(2,1)S(1)} %get-tuple-element.28.own_ref) | copy-start | bytes 3145732
  10.9 0.8 copy-start.3
  11.7 15.7 %collective-permute-start.1 = (bf16[2,2,96,2048]{3,2,1,0:T(8,128)(2,1)S(1)}, bf16[2,2,96,2048]{3,2,1,0:T(8,128)(2,1)}, u32[]{:S(2)}, u32[]{:S(2)}) collective-permute-start(bf16[2,2,96,2048]{3,2,1,0:T(8,128)(2,1)S(1)} %get-tuple-element.22.own_ref), channel_id=1, source_target_pairs={{0,4},{4,0},{8,12},{12,8},{16,20},{20,16},{24,28},{28,24},{32,36},... | collective-permute-start | bytes 4718600 | tf_op jit(solution)/shard_map/ppermute | solution.py:198
  11.7 26.0 %collective-permute-start = (bf16[2,2,96,2048]{3,2,1,0:T(8,128)(2,1)S(1)}, bf16[2,2,96,2048]{3,2,1,0:T(8,128)(2,1)}, u32[]{:S(2)}, u32[]{:S(2)}) collective-permute-start(bf16[2,2,96,2048]{3,2,1,0:T(8,128)(2,1)S(1)} %get-tuple-element.22.own_ref), channel_id=1, source_target_pairs={{4,8},{8,4},{12,16},{16,12},{20,24},{24,20},{28,32},{32,28},{36,40... | collective-permute-start | bytes 4718600 | tf_op jit(solution)/shard_map/ppermute | solution.py:198
  15.5 9.7 %copy-start.2 = (bf16[2,2,64,2048]{3,2,1,0:T(8,128)(2,1)S(1)}, bf16[2,2,64,2048]{3,2,1,0:T(8,128)(2,1)}, u32[]{:S(2)}) copy-start(bf16[2,2,64,2048]{3,2,1,0:T(8,128)(2,1)} %copy-done.1) | copy-start | bytes 3145732
  15.5 22.2 %copy-start.4 = (bf16[2,2,32,2048]{3,2,1,0:T(8,128)(2,1)S(1)}, bf16[2,2,32,2048]{3,2,1,0:T(8,128)(2,1)}, u32[]{:S(2)}) copy-start(bf16[2,2,32,2048]{3,2,1,0:T(8,128)(2,1)} %copy-done.3) | copy-start | bytes 1572868
  25.2 20.5 %collective-permute-start.7 = (bf16[2,2,64,2048]{3,2,1,0:T(8,128)(2,1)S(1)}, bf16[2,2,64,2048]{3,2,1,0:T(8,128)(2,1)S(1)}, u32[]{:S(2)}, u32[]{:S(2)}) collective-permute-start(bf16[2,2,64,2048]{3,2,1,0:T(8,128)(2,1)S(1)} %copy-done.2), channel_id=1, source_target_pairs={{0,4},{4,0},{8,12},{12,8},{16,20},{20,16},{24,28},{28,24},{32,36},... | collective-permute-start | bytes 3145736 | tf_op jit(solution)/shard_map/ppermute | solution.py:198
  25.3 23.6 %collective-permute-start.6 = (bf16[2,2,64,2048]{3,2,1,0:T(8,128)(2,1)S(1)}, bf16[2,2,64,2048]{3,2,1,0:T(8,128)(2,1)S(1)}, u32[]{:S(2)}, u32[]{:S(2)}) collective-permute-start(bf16[2,2,64,2048]{3,2,1,0:T(8,128)(2,1)S(1)} %copy-done.2), channel_id=1, source_target_pairs={{4,8},{8,4},{12,16},{16,12},{20,24},{24,20},{28,32},{32,28},{36,40... | collective-permute-start | bytes 3145736 | tf_op jit(solution)/shard_map/ppermute | solution.py:198
  37.7 14.5 %collective-permute-start.3 = (bf16[2,2,32,2048]{3,2,1,0:T(8,128)(2,1)S(1)}, bf16[2,2,32,2048]{3,2,1,0:T(8,128)(2,1)S(1)}, u32[]{:S(2)}, u32[]{:S(2)}) collective-permute-start(bf16[2,2,32,2048]{3,2,1,0:T(8,128)(2,1)S(1)} %copy-done.4), channel_id=1, source_target_pairs={{0,4},{4,0},{8,12},{12,8},{16,20},{20,16},{24,28},{28,24},{32,36},... | collective-permute-start | bytes 1572872 | tf_op jit(solution)/shard_map/ppermute | solution.py:198
  37.7 16.7 %collective-permute-start.2 = (bf16[2,2,32,2048]{3,2,1,0:T(8,128)(2,1)S(1)}, bf16[2,2,32,2048]{3,2,1,0:T(8,128)(2,1)S(1)}, u32[]{:S(2)}, u32[]{:S(2)}) collective-permute-start(bf16[2,2,32,2048]{3,2,1,0:T(8,128)(2,1)S(1)} %copy-done.4), channel_id=1, source_target_pairs={{4,8},{8,4},{12,16},{16,12},{20,24},{24,20},{28,32},{32,28},{36,40... | collective-permute-start | bytes 1572872 | tf_op jit(solution)/shard_map/ppermute | solution.py:198

commit v7 on v6

--- a/solution.py
+++ b/solution.py
@@ -73,7 +73,7 @@
     return pieces
 
 
-def phase_kernel(pairs_ref, far_ref, own_ref, near_ref, ones_ref, *refs):
+def phase_kernel(pairs_ref, near_ref, own_ref, far_ref, ones_ref, *refs):
     *earlier, out_ref, stack, sums = refs
     pair_count = pairs_ref.shape[0]
     acq, _, rows, cols = far_ref.shape
@@ -107,8 +107,8 @@
                     sums[piece, b, pl.ds(p * 2 * looked, 2 * looked), lanes] = value
             return carry
 
-        lax.fori_loop(0, blocks, widen, 0, unroll=2)
-        lax.fori_loop(0, blocks, form, 0, unroll=2)
+        lax.fori_loop(0, blocks, widen, 0, unroll=4)
+        lax.fori_loop(0, blocks, form, 0, unroll=4)
         return carry
 
     lax.fori_loop(0, bands, band, 0)
@@ -144,7 +144,7 @@
         ],
         compiler_params=pltpu.CompilerParams(vmem_limit_bytes=PHASE_VMEM),
         name="pair_phase",
-    )(pairs, far, own, near, ones, *earlier)
+    )(pairs, near, own, far, ones, *earlier)
 
 
 def constants_kernel(owner_ref, pinv_ref, slots_ref, ones_ref):
@@ -195,7 +195,8 @@
     )(owner, design_pinv)
 
     def swap(chunk):
-        return lax.ppermute(chunk, "acq", far_pairs), lax.ppermute(chunk, "acq", near_pairs)
+        near = lax.ppermute(chunk, "acq", near_pairs)
+        return lax.ppermute(chunk, "acq", far_pairs), near
 
     chunks = [lax.slice_in_dim(scenes, 0, CHUNKS[0], axis=2)]
     halos, phases = [swap(chunks[0])], []

time: 81.4 us -> 80.6 us (level)
  waiting for transfers between devices: 21.2 us -> 16.8 us
  starting transfers between devices: 13 us -> 15.6 us
  blocking collectives: 23.5 us -> 25.2 us
    ppermute x8, waiting for transfers between devices: 21.2 us -> 16.8 us  [the longest x4 16.8 us: swap(): return (lax.ppermute(chunk, 'acq', far_pairs), near)]
    ppermute x8, starting transfers between devices: 13 us -> 15.6 us  [the longest x4 14.8 us: swap(): return (lax.ppermute(chunk, 'acq', far_pairs), near)]
    all_to_all x1, blocking collectives: 23.5 us -> 25.2 us  [body(): phase = lax.all_to_all(phases[-1], 'acq', split_axis=0, concat_axis=0)]
  transfers between devices with their start and end apart: 8 -> 8, of which waited for: 4 -> 4; matrix products, arithmetic and copies ran while one was open for 0% -> 0% of each run, Pallas kernels for 18% -> 17%
where the time goes in v7:
time: 80.6 us; the launch traced here: 80.3 us
  blocking collectives  25.2 us (31%)
  Pallas kernels  16.8 us (21%)
  waiting for transfers between devices  16.8 us (21%)
  starting transfers between devices  15.6 us (19%)
  local copies, waits for them, and re-layouts  5.71 us (7%)
    all_to_all x1, blocking collectives, body(): phase = lax.all_to_all(phases[-1], 'acq', split_axis=0, concat_axis=0)  25.2 us
    ppermute x4, waiting for transfers between devices, swap(): return (lax.ppermute(chunk, 'acq', far_pairs), near)  16.8 us
    pallas_call x4, Pallas kernels, chunk_phase(): pl.pallas_call(phase_kernel, out_shape=jax.ShapeDtypeStruct((total, 1, pa...  14.9 us
    ppermute x4, starting transfers between devices, swap(): return (lax.ppermute(chunk, 'acq', far_pairs), near)  14.8 us
    unnamed x17, local copies, waits for them, and re-layouts  4.1 us
  transfers between devices with their start and end apart: 8, of which 4 were waited for; matrix products, arithmetic and copies ran while one was open for 0% of the time, Pallas kernels for 17%

profile of v7, /device:TPU:1, one launch (start us, length us, event | category | flops | bytes accessed | tf_op | source)
XLA Modules:
  0.0 80.3 jit_solution(16269122360960353003)
XLA Ops:
  0.0 1.3 %slice.3.own_ref = bf16[2,2,64,2048]{3,2,1,0:T(8,128)(2,1)S(1)} slice(bf16[2,2,256,2048]{3,2,1,0:T(8,128)(2,1)} %scenes_ref), slice={[0:2], [0:2], [0:64], [0:2048]} | slice | bytes 2097152 | tf_op jit(solution)/shard_map/slice | solution.py:201
  1.3 4.5 %collective-permute-start.5 = (bf16[2,2,64,2048]{3,2,1,0:T(8,128)(2,1)S(1)}, bf16[2,2,64,2048]{3,2,1,0:T(8,128)(2,1)}, u32[]{:S(2)}, u32[]{:S(2)}) collective-permute-start(bf16[2,2,64,2048]{3,2,1,0:T(8,128)(2,1)S(1)} %slice.3.own_ref), channel_id=1, source_target_pairs={{4,8},{8,4},{12,16},{16,12},{20,24},{24,20},{28,32},{32,28},{36,40... | collective-permute-start | bytes 3145736 | tf_op jit(solution)/shard_map/ppermute | solution.py:199
  5.9 0.4 collective-permute-start.4
  6.2 0.1 reshape.6
  6.5 0.5 constants.1
  7.1 2.2 %copy-done = bf16[2,2,256,2048]{3,2,1,0:T(8,128)(2,1)S(1)} copy-done((bf16[2,2,256,2048]{3,2,1,0:T(8,128)(2,1)S(1)}, bf16[2,2,256,2048]{3,2,1,0:T(8,128)(2,1)}, u32[]{:S(2)}) %copy-start) | copy-done | bytes 4194328
  9.3 0.2 cut_rows.1
  9.5 1.0 %copy-done.1 = bf16[2,2,64,2048]{3,2,1,0:T(8,128)(2,1)} copy-done((bf16[2,2,64,2048]{3,2,1,0:T(8,128)(2,1)}, bf16[2,2,64,2048]{3,2,1,0:T(8,128)(2,1)S(1)}, u32[]{:S(2)}) %copy-start.1) | copy-done | bytes 1048600
  10.5 0.8 copy-done.3
  11.3 0.2 collective-permute-start.1
  11.6 3.0 %collective-permute-start = (bf16[2,2,96,2048]{3,2,1,0:T(8,128)(2,1)S(1)}, bf16[2,2,96,2048]{3,2,1,0:T(8,128)(2,1)}, u32[]{:S(2)}, u32[]{:S(2)}) collective-permute-start(bf16[2,2,96,2048]{3,2,1,0:T(8,128)(2,1)S(1)} %get-tuple-element.22.own_ref), channel_id=1, source_target_pairs={{4,8},{8,4},{12,16},{16,12},{20,24},{24,20},{28,32},{32,28},{36,40... | collective-permute-start | bytes 4718600 | tf_op jit(solution)/shard_map/ppermute | solution.py:199
  14.6 0.1 copy.7
  14.7 3.7 %collective-permute-done.5.far_ref = bf16[2,2,64,2048]{3,2,1,0:T(8,128)(2,1)} collective-permute-done((bf16[2,2,64,2048]{3,2,1,0:T(8,128)(2,1)S(1)}, bf16[2,2,64,2048]{3,2,1,0:T(8,128)(2,1)}, u32[]{:S(2)}, u32[]{:S(2)}) %collective-permute-start.5) | collective-permute-done | bytes 1048608 | tf_op jit(solution)/shard_map/ppermute | solution.py:199
  18.4 4.1 %pair_phase.4.refs_0_ = f32[16,1,768]{2,1,0:T(1,128)S(1)} custom-call(s32[6,2]{1,0:T(8,128)S(1)} %fusion.3.pairs_ref, bf16[2,2,64,2048]{3,2,1,0:T(8,128)(2,1)} %collective-permute-done.4.near_ref, bf16[2,2,64,2048]{3,2,1,0:T(8,128)(2,1)S(1)} %slice.3.own_ref, bf16[2,2,64,2048]{3,2,1,0:T(8,128)(2,1)} %collective-permute-done.5.far_ref, ...), custom_call_target="tpu_custom_call" | custom-call | tf_op jit(solution)/shard_map/pair_phase/pallas_call | solution.py:136
  22.6 3.6 %collective-permute-start.7 = (bf16[2,2,64,2048]{3,2,1,0:T(8,128)(2,1)S(1)}, bf16[2,2,64,2048]{3,2,1,0:T(8,128)(2,1)S(1)}, u32[]{:S(2)}, u32[]{:S(2)}) collective-permute-start(bf16[2,2,64,2048]{3,2,1,0:T(8,128)(2,1)S(1)} %copy-done.2), channel_id=1, source_target_pairs={{4,8},{8,4},{12,16},{16,12},{20,24},{24,20},{28,32},{32,28},{36,40... | collective-permute-start | bytes 3145736 | tf_op jit(solution)/shard_map/ppermute | solution.py:199
  26.3 8.9 %collective-permute-done.far_ref = bf16[2,2,96,2048]{3,2,1,0:T(8,128)(2,1)} collective-permute-done((bf16[2,2,96,2048]{3,2,1,0:T(8,128)(2,1)S(1)}, bf16[2,2,96,2048]{3,2,1,0:T(8,128)(2,1)}, u32[]{:S(2)}, u32[]{:S(2)}) %collective-permute-start) | collective-permute-done | bytes 1572896 | tf_op jit(solution)/shard_map/ppermute | solution.py:199
  35.3 3.6 %collective-permute-start.3 = (bf16[2,2,32,2048]{3,2,1,0:T(8,128)(2,1)S(1)}, bf16[2,2,32,2048]{3,2,1,0:T(8,128)(2,1)S(1)}, u32[]{:S(2)}, u32[]{:S(2)}) collective-permute-start(bf16[2,2,32,2048]{3,2,1,0:T(8,128)(2,1)S(1)} %copy-done.4), channel_id=1, source_target_pairs={{4,8},{8,4},{12,16},{16,12},{20,24},{24,20},{28,32},{32,28},{36,40... | collective-permute-start | bytes 1572872 | tf_op jit(solution)/shard_map/ppermute | solution.py:199
  39.0 5.7 %pair_phase.5.refs_1_ = f32[24,1,768]{2,1,0:T(1,128)S(1)} custom-call(s32[6,2]{1,0:T(8,128)S(1)} %fusion.3.pairs_ref, bf16[2,2,96,2048]{3,2,1,0:T(8,128)(2,1)} %collective-permute-done.1.near_ref, bf16[2,2,96,2048]{3,2,1,0:T(8,128)(2,1)S(1)} %get-tuple-element.22.own_ref, bf16[2,2,96,2048]{3,2,1,0:T(8,128)(2,1)} %collective-permute-done.far_ref, ...), custom_call_target="tpu_custom_call" | custom-call | tf_op jit(solution)/shard_map/pair_phase/pallas_call | solution.py:136
  44.7 1.7 %collective-permute-done.7.far_ref = bf16[2,2,64,2048]{3,2,1,0:T(8,128)(2,1)S(1)} collective-permute-done((bf16[2,2,64,2048]{3,2,1,0:T(8,128)(2,1)S(1)}, bf16[2,2,64,2048]{3,2,1,0:T(8,128)(2,1)S(1)}, u32[]{:S(2)}, u32[]{:S(2)}) %collective-permute-start.7) | collective-permute-done | bytes 1048608 | tf_op jit(solution)/shard_map/ppermute | solution.py:199
  46.4 3.2 %pair_phase.6.refs_2_ = f32[16,1,768]{2,1,0:T(1,128)S(1)} custom-call(s32[6,2]{1,0:T(8,128)S(1)} %fusion.3.pairs_ref, bf16[2,2,64,2048]{3,2,1,0:T(8,128)(2,1)S(1)} %collective-permute-done.6.near_ref, bf16[2,2,64,2048]{3,2,1,0:T(8,128)(2,1)S(1)} %copy-done.2, bf16[2,2,64,2048]{3,2,1,0:T(8,128)(2,1)S(1)} %collective-permute-done.7.far_ref, ...), custom_call_target="tpu_custom_call" | custom-call | tf_op jit(solution)/shard_map/pair_phase/pallas_call | solution.py:136
  49.6 2.4 %collective-permute-done.3.far_ref = bf16[2,2,32,2048]{3,2,1,0:T(8,128)(2,1)S(1)} collective-permute-done((bf16[2,2,32,2048]{3,2,1,0:T(8,128)(2,1)S(1)}, bf16[2,2,32,2048]{3,2,1,0:T(8,128)(2,1)S(1)}, u32[]{:S(2)}, u32[]{:S(2)}) %collective-permute-start.3) | collective-permute-done | bytes 524320 | tf_op jit(solution)/shard_map/ppermute | solution.py:199
  52.0 2.0 %pair_phase.7 = f32[64,1,768]{2,1,0:T(1,128)S(1)} custom-call(s32[6,2]{1,0:T(8,128)S(1)} %fusion.3.pairs_ref, bf16[2,2,32,2048]{3,2,1,0:T(8,128)(2,1)S(1)} %collective-permute-done.2.near_ref, bf16[2,2,32,2048]{3,2,1,0:T(8,128)(2,1)S(1)} %copy-done.4, bf16[2,2,32,2048]{3,2,1,0:T(8,128)(2,1)S(1)} %collective-permute-done.3.far_ref, ...), custom_call_target="tpu_custom_call" | custom-call | tf_op jit(solution)/shard_map/pair_phase/pallas_call | solution.py:136
  54.0 25.2 %all_to_all.5.phase_ref = f32[64,1,768]{2,1,0:T(1,128)S(1)} all-to-all(f32[64,1,768]{2,1,0:T(1,128)S(1)} %pair_phase.7), channel_id=1, replica_groups=mesh['acq'=64,'rng'=4] {'acq'}, dimensions={0} | all-to-all | bytes 393216 | tf_op jit(solution)/shard_map/all_to_all | solution.py:214
  79.2 1.0 %series.1 = f32[1,128,128]{2,1,0:T(8,128)} custom-call(bf16[3,128,384]{2,1,0:T(8,128)(2,1)S(1)} %get-tuple-element.19.slots_ref, f32[64,1,768]{2,1,0:T(1,128)S(1)} %all_to_all.5.phase_ref), custom_call_target="tpu_custom_call" | custom-call | tf_op jit(solution)/shard_map/series/pallas_call | solution.py:215
  (22 shorter events, 0.4 us)
Async XLA Ops:
  0.0 6.2 %copy-start.6 = (s32[384]{0:T(512)S(1)}, s32[384]{0:T(512)}, u32[]{:S(2)}) copy-start(s32[384]{0:T(512)} %param.6) | copy-start | bytes 4612
  0.0 6.5 %copy-start.5 = (f32[128,384]{1,0:T(8,128)S(1)}, f32[128,384]{1,0:T(8,128)}, u32[]{:S(2)}) copy-start(f32[128,384]{1,0:T(8,128)} %pinv_ref.1) | copy-start | bytes 589828
  1.3 17.1 %collective-permute-start.5 = (bf16[2,2,64,2048]{3,2,1,0:T(8,128)(2,1)S(1)}, bf16[2,2,64,2048]{3,2,1,0:T(8,128)(2,1)}, u32[]{:S(2)}, u32[]{:S(2)}) collective-permute-start(bf16[2,2,64,2048]{3,2,1,0:T(8,128)(2,1)S(1)} %slice.3.own_ref), channel_id=1, source_target_pairs={{4,8},{8,4},{12,16},{16,12},{20,24},{24,20},{28,32},{32,28},{36,40... | collective-permute-start | bytes 3145736 | tf_op jit(solution)/shard_map/ppermute | solution.py:199
  5.9 12.6 %collective-permute-start.4 = (bf16[2,2,64,2048]{3,2,1,0:T(8,128)(2,1)S(1)}, bf16[2,2,64,2048]{3,2,1,0:T(8,128)(2,1)}, u32[]{:S(2)}, u32[]{:S(2)}) collective-permute-start(bf16[2,2,64,2048]{3,2,1,0:T(8,128)(2,1)S(1)} %slice.3.own_ref), channel_id=1, source_target_pairs={{0,4},{4,0},{8,12},{12,8},{16,20},{20,16},{24,28},{28,24},{32,36},... | collective-permute-start | bytes 3145736 | tf_op jit(solution)/shard_map/ppermute | solution.py:198
  7.1 2.2 %copy-start = (bf16[2,2,256,2048]{3,2,1,0:T(8,128)(2,1)S(1)}, bf16[2,2,256,2048]{3,2,1,0:T(8,128)(2,1)}, u32[]{:S(2)}) copy-start(bf16[2,2,256,2048]{3,2,1,0:T(8,128)(2,1)} %scenes_ref) | copy-start | bytes 12582916
  9.3 5.3 %copy-start.7 = (s32[6,2]{0,1:T(2,128)S(1)}, s32[6,2]{0,1:T(2,128)}, u32[]{:S(2)}) copy-start(s32[6,2]{0,1:T(2,128)} %param.5) | copy-start | bytes 148
  9.5 1.0 %copy-start.1 = (bf16[2,2,64,2048]{3,2,1,0:T(8,128)(2,1)}, bf16[2,2,64,2048]{3,2,1,0:T(8,128)(2,1)S(1)}, u32[]{:S(2)}) copy-start(bf16[2,2,64,2048]{3,2,1,0:T(8,128)(2,1)S(1)} %get-tuple-element.28.own_ref) | copy-start | bytes 3145732
  10.5 0.8 %copy-start.3 = (bf16[2,2,32,2048]{3,2,1,0:T(8,128)(2,1)}, bf16[2,2,32,2048]{3,2,1,0:T(8,128)(2,1)S(1)}, u32[]{:S(2)}) copy-start(bf16[2,2,32,2048]{3,2,1,0:T(8,128)(2,1)S(1)} %get-tuple-element.23.own_ref) | copy-start | bytes 1572868
  11.3 15.0 %collective-permute-start.1 = (bf16[2,2,96,2048]{3,2,1,0:T(8,128)(2,1)S(1)}, bf16[2,2,96,2048]{3,2,1,0:T(8,128)(2,1)}, u32[]{:S(2)}, u32[]{:S(2)}) collective-permute-start(bf16[2,2,96,2048]{3,2,1,0:T(8,128)(2,1)S(1)} %get-tuple-element.22.own_ref), channel_id=1, source_target_pairs={{0,4},{4,0},{8,12},{12,8},{16,20},{20,16},{24,28},{28,24},{32,36},... | collective-permute-start | bytes 4718600 | tf_op jit(solution)/shard_map/ppermute | solution.py:198
  11.6 23.7 %collective-permute-start = (bf16[2,2,96,2048]{3,2,1,0:T(8,128)(2,1)S(1)}, bf16[2,2,96,2048]{3,2,1,0:T(8,128)(2,1)}, u32[]{:S(2)}, u32[]{:S(2)}) collective-permute-start(bf16[2,2,96,2048]{3,2,1,0:T(8,128)(2,1)S(1)} %get-tuple-element.22.own_ref), channel_id=1, source_target_pairs={{4,8},{8,4},{12,16},{16,12},{20,24},{24,20},{28,32},{32,28},{36,40... | collective-permute-start | bytes 4718600 | tf_op jit(solution)/shard_map/ppermute | solution.py:199
  14.7 7.8 %copy-start.2 = (bf16[2,2,64,2048]{3,2,1,0:T(8,128)(2,1)S(1)}, bf16[2,2,64,2048]{3,2,1,0:T(8,128)(2,1)}, u32[]{:S(2)}) copy-start(bf16[2,2,64,2048]{3,2,1,0:T(8,128)(2,1)} %copy-done.1) | copy-start | bytes 3145732
  14.7 20.6 %copy-start.4 = (bf16[2,2,32,2048]{3,2,1,0:T(8,128)(2,1)S(1)}, bf16[2,2,32,2048]{3,2,1,0:T(8,128)(2,1)}, u32[]{:S(2)}) copy-start(bf16[2,2,32,2048]{3,2,1,0:T(8,128)(2,1)} %copy-done.3) | copy-start | bytes 1572868
  22.6 23.8 %collective-permute-start.7 = (bf16[2,2,64,2048]{3,2,1,0:T(8,128)(2,1)S(1)}, bf16[2,2,64,2048]{3,2,1,0:T(8,128)(2,1)S(1)}, u32[]{:S(2)}, u32[]{:S(2)}) collective-permute-start(bf16[2,2,64,2048]{3,2,1,0:T(8,128)(2,1)S(1)} %copy-done.2), channel_id=1, source_target_pairs={{4,8},{8,4},{12,16},{16,12},{20,24},{24,20},{28,32},{32,28},{36,40... | collective-permute-start | bytes 3145736 | tf_op jit(solution)/shard_map/ppermute | solution.py:199
  26.2 20.2 %collective-permute-start.6 = (bf16[2,2,64,2048]{3,2,1,0:T(8,128)(2,1)S(1)}, bf16[2,2,64,2048]{3,2,1,0:T(8,128)(2,1)S(1)}, u32[]{:S(2)}, u32[]{:S(2)}) collective-permute-start(bf16[2,2,64,2048]{3,2,1,0:T(8,128)(2,1)S(1)} %copy-done.2), channel_id=1, source_target_pairs={{0,4},{4,0},{8,12},{12,8},{16,20},{20,16},{24,28},{28,24},{32,36},... | collective-permute-start | bytes 3145736 | tf_op jit(solution)/shard_map/ppermute | solution.py:198
  35.3 16.7 %collective-permute-start.3 = (bf16[2,2,32,2048]{3,2,1,0:T(8,128)(2,1)S(1)}, bf16[2,2,32,2048]{3,2,1,0:T(8,128)(2,1)S(1)}, u32[]{:S(2)}, u32[]{:S(2)}) collective-permute-start(bf16[2,2,32,2048]{3,2,1,0:T(8,128)(2,1)S(1)} %copy-done.4), channel_id=1, source_target_pairs={{4,8},{8,4},{12,16},{16,12},{20,24},{24,20},{28,32},{32,28},{36,40... | collective-permute-start | bytes 1572872 | tf_op jit(solution)/shard_map/ppermute | solution.py:199
  38.9 13.1 %collective-permute-start.2 = (bf16[2,2,32,2048]{3,2,1,0:T(8,128)(2,1)S(1)}, bf16[2,2,32,2048]{3,2,1,0:T(8,128)(2,1)S(1)}, u32[]{:S(2)}, u32[]{:S(2)}) collective-permute-start(bf16[2,2,32,2048]{3,2,1,0:T(8,128)(2,1)S(1)} %copy-done.4), channel_id=1, source_target_pairs={{0,4},{4,0},{8,12},{12,8},{16,20},{20,16},{24,28},{28,24},{32,36},... | collective-permute-start | bytes 1572872 | tf_op jit(solution)/shard_map/ppermute | solution.py:198

commit v8 on v7

--- a/solution.py
+++ b/solution.py
@@ -15,8 +15,6 @@
 BAND = 32
 PHASE_VMEM = 10 * 2**20
 SMALL_VMEM = 6 * 2**20
-UNROLL_A = 2
-UNROLL_B = 2
 
 ATAN = (
     0.0030499680532062342, -0.016827448459262765, 0.04385559893448732,
@@ -38,30 +36,30 @@
     return jnp.where(imag < 0, -angle, angle)
 
 
-def cut_kernel(start, scenes_ref, *refs):
+def cut_kernel(places, scenes_ref, *refs):
     *outs, sems = refs
     copies = []
-    for k, out in enumerate(outs):
-        rows = out.shape[2]
-        copies.append(pltpu.make_async_copy(scenes_ref.at[:, :, pl.ds(start, rows), :], out, sems.at[k]))
-        start += rows
+    for k, (out, (row, col)) in enumerate(zip(outs, places)):
+        _, _, rows, cols = out.shape
+        source = scenes_ref.at[:, :, pl.ds(row, rows), pl.ds(col, cols)]
+        copies.append(pltpu.make_async_copy(source, out, sems.at[k]))
     for copy in copies:
         copy.start()
     for copy in copies:
         copy.wait()
 
 
-def cut_rows(scenes, start, sizes):
-    acq, parts, _, cols = scenes.shape
+def cut(scenes, places, sizes):
+    acq, parts = scenes.shape[:2]
     vmem = pl.BlockSpec(memory_space=pltpu.VMEM)
     return pl.pallas_call(
-        functools.partial(cut_kernel, start),
-        out_shape=[jax.ShapeDtypeStruct((acq, parts, rows, cols), scenes.dtype) for rows in sizes],
+        functools.partial(cut_kernel, places),
+        out_shape=[jax.ShapeDtypeStruct((acq, parts, rows, cols), scenes.dtype) for rows, cols in sizes],
         in_specs=[pl.BlockSpec(memory_space=pltpu.HBM)],
         out_specs=[vmem] * len(sizes),
         scratch_shapes=[pltpu.SemaphoreType.DMA((len(sizes),))],
         compiler_params=pltpu.CompilerParams(vmem_limit_bytes=SMALL_VMEM),
-        name="cut_rows",
+        name="cut",
     )(scenes)
 
 
@@ -73,8 +71,9 @@
     return pieces
 
 
-def phase_kernel(pairs_ref, near_ref, own_ref, far_ref, ones_ref, *refs):
+def phase_kernel(first_col, has_partial, keep_sums, pairs_ref, near_ref, own_ref, far_ref, ones_ref, *refs):
     *earlier, out_ref, stack, sums = refs
+    partial = earlier.pop() if has_partial else None
     pair_count = pairs_ref.shape[0]
     acq, _, rows, cols = far_ref.shape
     bands, looked = rows // BAND, BAND // LOOK_R
@@ -86,10 +85,11 @@
 
         def widen(j, carry):
             lanes = pl.ds(pl.multiple_of(j * LANES, LANES), LANES)
-            for side, ref in enumerate((far_ref, own_ref, near_ref)):
+            wide = pl.ds(pl.multiple_of(first_col + j * LANES, LANES), LANES)
+            for side, (ref, cut) in enumerate(((far_ref, lanes), (own_ref, wide), (near_ref, wide))):
                 for a in range(acq):
                     for part in range(2):
-                        stack[side * acq + a, part, j] = ref[a, part, at, lanes].astype(jnp.float32)
+                        stack[side * acq + a, part, j] = ref[a, part, at, cut].astype(jnp.float32)
             return carry
 
         def form(j, carry):
@@ -113,30 +113,35 @@
 
     lax.fori_loop(0, bands, band, 0)
     pieces = sums[...].reshape(2 * bands * sums.shape[2], cols)
-    dots = jnp.dot(pieces, ones_ref[...], preferred_element_type=jnp.float32)
+    dots = jnp.dot(pieces, ones_ref[pl.ds(first_col, cols)], preferred_element_type=jnp.float32)
     dots = dots.reshape(2, bands, pair_count, 2, looked, dots.shape[1])
     both = dots[0] + dots[1]
-    width = dots.shape[-1]
+    if partial is not None:
+        both = both + partial[...].reshape(both.shape)
+    if keep_sums:
+        out_ref[...] = both.reshape(out_ref.shape)
+        return
     angle = atan_ratio(both[:, :, 1], both[:, :, 0])
     at = 0
     for ref in earlier:
-        out_ref[pl.ds(at, ref.shape[0])] = ref[...]
-        at += ref.shape[0]
+        out_ref[pl.ds(at * pair_count, ref.shape[0]), :] = ref[...]
+        at += ref.shape[0] // pair_count
     for b in range(bands):
         for p in range(pair_count):
-            out_ref[pl.ds(at + b * looked, looked), 0, pl.ds(p * width, width)] = angle[b, p]
-
-
-def chunk_phase(pairs, far, own, near, ones, earlier=()):
+            out_ref[pl.ds((at + b * looked) * pair_count + p, looked, stride=pair_count), :] = angle[b, p]
+
+
+def chunk_phase(pairs, far, own, near, ones, earlier=(), first_col=0, partial=None, keep_sums=False):
     acq, parts, rows, cols = far.shape
     looked = rows // LOOK_R
     pair_count = pairs.shape[0]
-    total = looked + sum(x.shape[0] for x in earlier)
+    total = pair_count * looked * (2 if keep_sums else 1) + sum(x.shape[0] for x in earlier)
+    more = list(earlier) + ([] if partial is None else [partial])
     vmem = pl.BlockSpec(memory_space=pltpu.VMEM)
     return pl.pallas_call(
-        phase_kernel,
-        out_shape=jax.ShapeDtypeStruct((total, 1, pair_count * (cols // LOOK_C)), jnp.float32),
-        in_specs=[pl.BlockSpec(memory_space=pltpu.SMEM)] + [vmem] * (4 + len(earlier)),
+        functools.partial(phase_kernel, first_col, partial is not None, keep_sums),
+        out_shape=jax.ShapeDtypeStruct((total, own.shape[3] // LOOK_C), jnp.float32),
+        in_specs=[pl.BlockSpec(memory_space=pltpu.SMEM)] + [vmem] * (4 + len(more)),
         out_specs=vmem,
         scratch_shapes=[
             pltpu.VMEM((3 * acq, parts, cols // LANES, BAND, LANES), jnp.float32),
@@ -144,7 +149,7 @@
         ],
         compiler_params=pltpu.CompilerParams(vmem_limit_bytes=PHASE_VMEM),
         name="pair_phase",
-    )(pairs, near, own, far, ones, *earlier)
+    )(pairs, near, own, far, ones, *more)
 
 
 def constants_kernel(owner_ref, pinv_ref, slots_ref, ones_ref):
@@ -159,10 +164,7 @@
 
 def series_kernel(slots_ref, phase_ref, out_ref):
     acqs, width = slots_ref.shape[1:]
-    count, _, lanes = phase_ref.shape
-    lanes = lanes * count // width
-    phase = [phase_ref[:, 0, pl.ds(p * lanes, lanes)] for p in range(width // count)]
-    phase = split(jnp.concatenate(phase, axis=0), 3)
+    phase = split(phase_ref[...], 3)
     total = None
     for piece in reversed(range(3)):
         rows = slots_ref[pl.ds(0, 3 - piece)].reshape((3 - piece) * acqs, width)
@@ -183,7 +185,7 @@
     local = pairs - (me - 1) * acq
     local = jnp.where(me % 2 == 1, (2 - local // acq) * acq + local % acq, local)
 
-    owner = pair_owner.reshape(count, pair_count).T.reshape(1, count * pair_count)
+    owner = pair_owner.reshape(1, count * pair_count)
     slots, ones = pl.pallas_call(
         constants_kernel,
         out_shape=[
@@ -194,24 +196,36 @@
         name="constants",
     )(owner, design_pinv)
 
-    def swap(chunk):
-        near = lax.ppermute(chunk, "acq", near_pairs)
-        return lax.ppermute(chunk, "acq", far_pairs), near
-
+    def far_of(chunk):
+        return lax.ppermute(chunk, "acq", far_pairs)
+
+    def near_of(chunk):
+        return lax.ppermute(chunk, "acq", near_pairs)
+
+    starts = [sum(CHUNKS[:k]) for k in range(len(CHUNKS))]
+    half = cols // 2
+    places = [(start, 0) for start in starts[1:]] + [(starts[-1], 0), (starts[-1], half)]
+    sizes = [(step, cols) for step in CHUNKS[1:]] + [(CHUNKS[-1], half)] * 2
     chunks = [lax.slice_in_dim(scenes, 0, CHUNKS[0], axis=2)]
-    halos, phases = [swap(chunks[0])], []
+    nears, fars, phases = [near_of(chunks[0])], [far_of(chunks[0])], []
     rest, slots, ones, chunks[0] = lax.optimization_barrier((scenes, slots, ones, chunks[0]))
-    chunks += list(cut_rows(rest, CHUNKS[0], CHUNKS[1:]))
-    halos.append(swap(chunks[1]))
-    for k, chunk in enumerate(chunks):
-        far, near = halos[k]
-        last = k == len(chunks) - 1
-        phases.append(chunk_phase(local, far, chunk, near, ones, phases if last else ()))
-        if k + 2 < len(chunks):
-            done = phases if k == 0 else halos
-            chunks[k + 2], done[k] = lax.optimization_barrier((chunks[k + 2], done[k]))
-            halos.append(swap(chunks[k + 2]))
-    phase = lax.all_to_all(phases[-1], "acq", split_axis=0, concat_axis=0)
+    *others, left, right = cut(rest, places, sizes)
+    chunks += others
+    nears.append(near_of(chunks[1]))
+    fars.append(far_of(chunks[1]))
+    for k, chunk in enumerate(chunks[:-1]):
+        phases.append(chunk_phase(local, fars[k], chunk, nears[k], ones))
+        if k == 0:
+            chunks[2], phases[0] = lax.optimization_barrier((chunks[2], phases[0]))
+            nears.append(near_of(chunks[2]))
+            fars.append(far_of(chunks[2]))
+            chunks[3], left, right, nears[2] = lax.optimization_barrier((chunks[3], left, right, nears[2]))
+            nears.append(near_of(chunks[3]))
+            fars += [far_of(left), far_of(right)]
+    part = chunk_phase(local, fars[3], chunks[3], nears[3], ones, keep_sums=True)
+    phases.append(chunk_phase(local, fars[4], chunks[3], nears[3], ones, phases, half, part))
+    phase = lax.all_to_all(phases[-1].reshape(count, 1, -1), "acq", split_axis=0, concat_axis=0)
+    phase = phase.reshape(count * pair_count, -1)
     return pl.pallas_call(
         series_kernel,
         out_shape=jax.ShapeDtypeStruct((1, slots.shape[1], cols // LOOK_C), jnp.float32),

time: 80.6 us -> 79.9 us (level)
  waiting for transfers between devices: 16.8 us -> 11 us
  starting transfers between devices: 15.6 us -> 19.5 us
  Pallas kernels: 16.8 us -> 18.5 us
    ppermute x8 -> x9, waiting for transfers between devices: 16.8 us -> 11 us  [the longest x5 11 us: far_of(): return lax.ppermute(chunk, 'acq', far_pairs)]
    ppermute x8 -> x9, starting transfers between devices: 15.6 us -> 19.5 us  [the longest x5 18.5 us: far_of(): return lax.ppermute(chunk, 'acq', far_pairs)]
    pallas_call x5 -> x6, Pallas kernels: 15.2 us -> 17.1 us  [the longest x5 15.6 us: chunk_phase(): pl.pallas_call(functools.partial(phase_kernel, first_col, partial is not...]
  transfers between devices with their start and end apart: 8 -> 9, of which waited for: 4 -> 4; matrix products, arithmetic and copies ran while one was open for 0% -> 0% of each run, Pallas kernels for 17% -> 20%
where the time goes in v8:
time: 79.9 us; the launch traced here: 79.6 us
  blocking collectives  25.2 us (32%)
  starting transfers between devices  19.5 us (24%)
  Pallas kernels  18.5 us (23%)
  waiting for transfers between devices  11 us (14%)
  local copies, waits for them, and re-layouts  5.07 us (6%)
    all_to_all x1, blocking collectives, body(): lax.all_to_all(phases[-1].reshape(count, 1, -1), 'acq', split_axis=0, con...  25.2 us
    ppermute x5, starting transfers between devices, far_of(): return lax.ppermute(chunk, 'acq', far_pairs)  18.5 us
    pallas_call x5, Pallas kernels, chunk_phase(): pl.pallas_call(functools.partial(phase_kernel, first_col, partial is not...  15.6 us
    ppermute x5, waiting for transfers between devices, far_of(): return lax.ppermute(chunk, 'acq', far_pairs)  11 us
    unnamed x17, local copies, waits for them, and re-layouts  3.74 us
  transfers between devices with their start and end apart: 9, of which 4 were waited for; matrix products, arithmetic and copies ran while one was open for 0% of the time, Pallas kernels for 20%

profile of v8, /device:TPU:1, one launch (start us, length us, event | category | flops | bytes accessed | tf_op | source)
XLA Modules:
  0.0 79.6 jit_solution(9594980501016593985)
XLA Ops:
  0.0 1.3 %slice.3.own_ref = bf16[2,2,64,2048]{3,2,1,0:T(8,128)(2,1)S(1)} slice(bf16[2,2,256,2048]{3,2,1,0:T(8,128)(2,1)} %scenes_ref), slice={[0:2], [0:2], [0:64], [0:2048]} | slice | bytes 2097152 | tf_op jit(solution)/shard_map/slice | solution.py:209
  1.3 4.5 %collective-permute-start.1 = (bf16[2,2,64,2048]{3,2,1,0:T(8,128)(2,1)S(1)}, bf16[2,2,64,2048]{3,2,1,0:T(8,128)(2,1)}, u32[]{:S(2)}, u32[]{:S(2)}) collective-permute-start(bf16[2,2,64,2048]{3,2,1,0:T(8,128)(2,1)S(1)} %slice.3.own_ref), channel_id=1, source_target_pairs={{4,8},{8,4},{12,16},{16,12},{20,24},{24,20},{28,32},{32,28},{36,40... | collective-permute-start | bytes 3145736 | tf_op jit(solution)/shard_map/ppermute | solution.py:200
  5.9 0.4 collective-permute-start
  6.2 0.5 constants.1
  6.8 2.2 %copy-done = bf16[2,2,256,2048]{3,2,1,0:T(8,128)(2,1)S(1)} copy-done((bf16[2,2,256,2048]{3,2,1,0:T(8,128)(2,1)S(1)}, bf16[2,2,256,2048]{3,2,1,0:T(8,128)(2,1)}, u32[]{:S(2)}) %copy-start) | copy-done | bytes 4194328
  9.0 1.5 %cut.1 = (bf16[2,2,96,2048]{3,2,1,0:T(8,128)(2,1)}, bf16[2,2,64,2048]{3,2,1,0:T(8,128)(2,1)S(1)}, bf16[2,2,32,2048]{3,2,1,0:T(8,128)(2,1)S(1)}, bf16[2,2,32,1024...) custom-call(bf16[2,2,256,2048]{3,2,1,0:T(8,128)(2,1)S(1)} %copy-done), custom_call_target="tpu_custom_call" | custom-call | tf_op jit(solution)/shard_map/cut/pallas_call | solution.py:55
  10.4 0.7 copy-done.2
  11.2 0.7 copy-done.4
  11.9 3.2 %collective-permute-start.6 = (bf16[2,2,96,2048]{3,2,1,0:T(8,128)(2,1)}, bf16[2,2,96,2048]{3,2,1,0:T(8,128)(2,1)}, u32[]{:S(2)}, u32[]{:S(2)}) collective-permute-start(bf16[2,2,96,2048]{3,2,1,0:T(8,128)(2,1)} %get-tuple-element.36.own_ref), channel_id=1, source_target_pairs={{4,8},{8,4},{12,16},{16,12},{20,24},{24,20},{28,32},{32,28},{36,40... | collective-permute-start | bytes 4718600 | tf_op jit(solution)/shard_map/ppermute | solution.py:200
  15.3 3.2 %collective-permute-done.1.far_ref = bf16[2,2,64,2048]{3,2,1,0:T(8,128)(2,1)} collective-permute-done((bf16[2,2,64,2048]{3,2,1,0:T(8,128)(2,1)S(1)}, bf16[2,2,64,2048]{3,2,1,0:T(8,128)(2,1)}, u32[]{:S(2)}, u32[]{:S(2)}) %collective-permute-start.1) | collective-permute-done | bytes 1048608 | tf_op jit(solution)/shard_map/ppermute | solution.py:200
  18.4 4.1 %pair_phase.5.refs_0_ = f32[96,128]{1,0:T(8,128)S(1)} custom-call(s32[6,2]{1,0:T(8,128)S(1)} %fusion.3.pairs_ref, bf16[2,2,64,2048]{3,2,1,0:T(8,128)(2,1)} %collective-permute-done.near_ref, bf16[2,2,64,2048]{3,2,1,0:T(8,128)(2,1)S(1)} %slice.3.own_ref, bf16[2,2,64,2048]{3,2,1,0:T(8,128)(2,1)} %collective-permute-done.1.far_ref, ...), custom_call_target="tpu_custom_call" | custom-call | tf_op jit(solution)/shard_map/pair_phase/pallas_call | solution.py:141
  22.6 0.5 collective-permute-start.5
  23.1 3.6 %collective-permute-start.7 = (bf16[2,2,64,2048]{3,2,1,0:T(8,128)(2,1)S(1)}, bf16[2,2,64,2048]{3,2,1,0:T(8,128)(2,1)S(1)}, u32[]{:S(2)}, u32[]{:S(2)}) collective-permute-start(bf16[2,2,64,2048]{3,2,1,0:T(8,128)(2,1)S(1)} %get-tuple-element.32.own_ref), channel_id=1, source_target_pairs={{4,8},{8,4},{12,16},{16,12},{20,24},{24,20},{28,32},{32,28},{36,40... | collective-permute-start | bytes 3145736 | tf_op jit(solution)/shard_map/ppermute | solution.py:200
  26.9 3.5 %collective-permute-start.8 = (bf16[2,2,32,1024]{3,2,1,0:T(8,128)(2,1)S(1)}, bf16[2,2,32,1024]{3,2,1,0:T(8,128)(2,1)S(1)}, u32[]{:S(2)}, u32[]{:S(2)}) collective-permute-start(bf16[2,2,32,1024]{3,2,1,0:T(8,128)(2,1)S(1)} %copy-done.5), channel_id=1, source_target_pairs={{4,8},{8,4},{12,16},{16,12},{20,24},{24,20},{28,32},{32,28},{36,40... | collective-permute-start | bytes 786440 | tf_op jit(solution)/shard_map/ppermute | solution.py:200
  30.4 4.9 %collective-permute-done.6.far_ref = bf16[2,2,96,2048]{3,2,1,0:T(8,128)(2,1)} collective-permute-done((bf16[2,2,96,2048]{3,2,1,0:T(8,128)(2,1)}, bf16[2,2,96,2048]{3,2,1,0:T(8,128)(2,1)}, u32[]{:S(2)}, u32[]{:S(2)}) %collective-permute-start.6) | collective-permute-done | bytes 1572896 | tf_op jit(solution)/shard_map/ppermute | solution.py:200
  35.3 3.6 %collective-permute-start.4 = (bf16[2,2,32,1024]{3,2,1,0:T(8,128)(2,1)S(1)}, bf16[2,2,32,1024]{3,2,1,0:T(8,128)(2,1)S(1)}, u32[]{:S(2)}, u32[]{:S(2)}) collective-permute-start(bf16[2,2,32,1024]{3,2,1,0:T(8,128)(2,1)S(1)} %copy-done.3), channel_id=1, source_target_pairs={{4,8},{8,4},{12,16},{16,12},{20,24},{24,20},{28,32},{32,28},{36,40... | collective-permute-start | bytes 786440 | tf_op jit(solution)/shard_map/ppermute | solution.py:200
  38.9 5.6 %pair_phase.6.refs_1_ = f32[144,128]{1,0:T(8,128)S(1)} custom-call(s32[6,2]{1,0:T(8,128)S(1)} %fusion.3.pairs_ref, bf16[2,2,96,2048]{3,2,1,0:T(8,128)(2,1)S(1)} %collective-permute-done.5.near_ref, bf16[2,2,96,2048]{3,2,1,0:T(8,128)(2,1)} %get-tuple-element.36.own_ref, bf16[2,2,96,2048]{3,2,1,0:T(8,128)(2,1)} %collective-permute-done.6.far_ref, ...), custom_call_target="tpu_custom_call" | custom-call | tf_op jit(solution)/shard_map/pair_phase/pallas_call | solution.py:141
  44.6 1.8 %collective-permute-done.7.far_ref = bf16[2,2,64,2048]{3,2,1,0:T(8,128)(2,1)S(1)} collective-permute-done((bf16[2,2,64,2048]{3,2,1,0:T(8,128)(2,1)S(1)}, bf16[2,2,64,2048]{3,2,1,0:T(8,128)(2,1)S(1)}, u32[]{:S(2)}, u32[]{:S(2)}) %collective-permute-start.7) | collective-permute-done | bytes 1048608 | tf_op jit(solution)/shard_map/ppermute | solution.py:200
  46.4 3.2 %pair_phase.7.refs_2_ = f32[96,128]{1,0:T(8,128)S(1)} custom-call(s32[6,2]{1,0:T(8,128)S(1)} %fusion.3.pairs_ref, bf16[2,2,64,2048]{3,2,1,0:T(8,128)(2,1)S(1)} %collective-permute-done.2.near_ref, bf16[2,2,64,2048]{3,2,1,0:T(8,128)(2,1)S(1)} %get-tuple-element.32.own_ref, bf16[2,2,64,2048]{3,2,1,0:T(8,128)(2,1)S(1)} %collective-permute-done.7.far_ref, ...), custom_call_target="tpu_custom_call" | custom-call | tf_op jit(solution)/shard_map/pair_phase/pallas_call | solution.py:141
  49.6 1.3 %pair_phase.8.refs_3_ = f32[96,128]{1,0:T(8,128)S(1)} custom-call(s32[6,2]{1,0:T(8,128)S(1)} %fusion.3.pairs_ref, bf16[2,2,32,2048]{3,2,1,0:T(8,128)(2,1)S(1)} %collective-permute-done.3.near_ref, bf16[2,2,32,2048]{3,2,1,0:T(8,128)(2,1)S(1)} %get-tuple-element.33.own_ref, bf16[2,2,32,1024]{3,2,1,0:T(8,128)(2,1)S(1)} %collective-permute-done.8.far_ref, ...), custom_call_target="tpu_custom_call" | custom-call | tf_op jit(solution)/shard_map/pair_phase/pallas_call | solution.py:141
  50.9 1.1 %collective-permute-done.4.far_ref = bf16[2,2,32,1024]{3,2,1,0:T(8,128)(2,1)S(1)} collective-permute-done((bf16[2,2,32,1024]{3,2,1,0:T(8,128)(2,1)S(1)}, bf16[2,2,32,1024]{3,2,1,0:T(8,128)(2,1)S(1)}, u32[]{:S(2)}, u32[]{:S(2)}) %collective-permute-start.4) | collective-permute-done | bytes 262176 | tf_op jit(solution)/shard_map/ppermute | solution.py:200
  52.0 1.4 %pair_phase.9 = f32[384,128]{1,0:T(8,128)S(1)} custom-call(s32[6,2]{1,0:T(8,128)S(1)} %fusion.3.pairs_ref, bf16[2,2,32,2048]{3,2,1,0:T(8,128)(2,1)S(1)} %collective-permute-done.3.near_ref, bf16[2,2,32,2048]{3,2,1,0:T(8,128)(2,1)S(1)} %get-tuple-element.33.own_ref, bf16[2,2,32,1024]{3,2,1,0:T(8,128)(2,1)S(1)} %collective-permute-done.4.far_ref, ...), custom_call_target="tpu_custom_call" | custom-call | tf_op jit(solution)/shard_map/pair_phase/pallas_call | solution.py:141
  53.4 25.2 %all_to_all.5 = f32[64,1,768]{2,1,0:T(1,128)S(1)} all-to-all(f32[64,1,768]{2,1,0:T(1,128)S(1)} %bitcast.2), channel_id=1, replica_groups=mesh['acq'=64,'rng'=4] {'acq'}, dimensions={0} | all-to-all | bytes 393216 | tf_op jit(solution)/shard_map/all_to_all | solution.py:227
  78.6 0.9 %series.1 = f32[1,128,128]{2,1,0:T(8,128)} custom-call(bf16[3,128,384]{2,1,0:T(8,128)(2,1)S(1)} %get-tuple-element.24.slots_ref, f32[384,128]{1,0:T(8,128)S(1)} %bitcast.3), custom_call_target="tpu_custom_call" | custom-call | tf_op jit(solution)/shard_map/series/pallas_call | solution.py:229
  (23 shorter events, 0.3 us)
Async XLA Ops:
  0.0 6.2 %copy-start.6 = (s32[384]{0:T(512)S(1)}, s32[384]{0:T(512)}, u32[]{:S(2)}) copy-start(s32[384]{0:T(512)} %param.6) | copy-start | bytes 4612
  0.0 6.2 %copy-start.1 = (f32[128,384]{1,0:T(8,128)S(1)}, f32[128,384]{1,0:T(8,128)}, u32[]{:S(2)}) copy-start(f32[128,384]{1,0:T(8,128)} %pinv_ref.1) | copy-start | bytes 589828
  1.3 17.1 %collective-permute-start.1 = (bf16[2,2,64,2048]{3,2,1,0:T(8,128)(2,1)S(1)}, bf16[2,2,64,2048]{3,2,1,0:T(8,128)(2,1)}, u32[]{:S(2)}, u32[]{:S(2)}) collective-permute-start(bf16[2,2,64,2048]{3,2,1,0:T(8,128)(2,1)S(1)} %slice.3.own_ref), channel_id=1, source_target_pairs={{4,8},{8,4},{12,16},{16,12},{20,24},{24,20},{28,32},{32,28},{36,40... | collective-permute-start | bytes 3145736 | tf_op jit(solution)/shard_map/ppermute | solution.py:200
  5.9 12.6 %collective-permute-start = (bf16[2,2,64,2048]{3,2,1,0:T(8,128)(2,1)S(1)}, bf16[2,2,64,2048]{3,2,1,0:T(8,128)(2,1)}, u32[]{:S(2)}, u32[]{:S(2)}) collective-permute-start(bf16[2,2,64,2048]{3,2,1,0:T(8,128)(2,1)S(1)} %slice.3.own_ref), channel_id=1, source_target_pairs={{0,4},{4,0},{8,12},{12,8},{16,20},{20,16},{24,28},{28,24},{32,36},... | collective-permute-start | bytes 3145736 | tf_op jit(solution)/shard_map/ppermute | solution.py:203
  6.8 2.2 %copy-start = (bf16[2,2,256,2048]{3,2,1,0:T(8,128)(2,1)S(1)}, bf16[2,2,256,2048]{3,2,1,0:T(8,128)(2,1)}, u32[]{:S(2)}) copy-start(bf16[2,2,256,2048]{3,2,1,0:T(8,128)(2,1)} %scenes_ref) | copy-start | bytes 12582916
  9.0 6.2 %copy-start.7 = (s32[6,2]{0,1:T(2,128)S(1)}, s32[6,2]{0,1:T(2,128)}, u32[]{:S(2)}) copy-start(s32[6,2]{0,1:T(2,128)} %param.5) | copy-start | bytes 148
  10.4 0.7 copy-start.2
  11.2 0.7 copy-start.4
  11.9 23.4 %collective-permute-start.6 = (bf16[2,2,96,2048]{3,2,1,0:T(8,128)(2,1)}, bf16[2,2,96,2048]{3,2,1,0:T(8,128)(2,1)}, u32[]{:S(2)}, u32[]{:S(2)}) collective-permute-start(bf16[2,2,96,2048]{3,2,1,0:T(8,128)(2,1)} %get-tuple-element.36.own_ref), channel_id=1, source_target_pairs={{4,8},{8,4},{12,16},{16,12},{20,24},{24,20},{28,32},{32,28},{36,40... | collective-permute-start | bytes 4718600 | tf_op jit(solution)/shard_map/ppermute | solution.py:200
  15.3 11.6 %copy-start.5 = (bf16[2,2,32,1024]{3,2,1,0:T(8,128)(2,1)S(1)}, bf16[2,2,32,1024]{3,2,1,0:T(8,128)(2,1)}, u32[]{:S(2)}) copy-start(bf16[2,2,32,1024]{3,2,1,0:T(8,128)(2,1)} %copy-done.4) | copy-start | bytes 786436
  15.3 20.0 %copy-start.3 = (bf16[2,2,32,1024]{3,2,1,0:T(8,128)(2,1)S(1)}, bf16[2,2,32,1024]{3,2,1,0:T(8,128)(2,1)}, u32[]{:S(2)}) copy-start(bf16[2,2,32,1024]{3,2,1,0:T(8,128)(2,1)} %copy-done.2) | copy-start | bytes 786436
  22.5 4.2 %collective-permute-start.2 = (bf16[2,2,64,2048]{3,2,1,0:T(8,128)(2,1)S(1)}, bf16[2,2,64,2048]{3,2,1,0:T(8,128)(2,1)S(1)}, u32[]{:S(2)}, u32[]{:S(2)}) collective-permute-start(bf16[2,2,64,2048]{3,2,1,0:T(8,128)(2,1)S(1)} %get-tuple-element.32.own_ref), channel_id=1, source_target_pairs={{0,4},{4,0},{8,12},{12,8},{16,20},{20,16},{24,28},{28,24},{32,36},... | collective-permute-start | bytes 3145736 | tf_op jit(solution)/shard_map/ppermute | solution.py:203
  22.6 16.3 %collective-permute-start.5 = (bf16[2,2,96,2048]{3,2,1,0:T(8,128)(2,1)}, bf16[2,2,96,2048]{3,2,1,0:T(8,128)(2,1)S(1)}, u32[]{:S(2)}, u32[]{:S(2)}) collective-permute-start(bf16[2,2,96,2048]{3,2,1,0:T(8,128)(2,1)} %get-tuple-element.36.own_ref), channel_id=1, source_target_pairs={{0,4},{4,0},{8,12},{12,8},{16,20},{20,16},{24,28},{28,24},{32,36},... | collective-permute-start | bytes 4718600 | tf_op jit(solution)/shard_map/ppermute | solution.py:203
  23.1 23.3 %collective-permute-start.7 = (bf16[2,2,64,2048]{3,2,1,0:T(8,128)(2,1)S(1)}, bf16[2,2,64,2048]{3,2,1,0:T(8,128)(2,1)S(1)}, u32[]{:S(2)}, u32[]{:S(2)}) collective-permute-start(bf16[2,2,64,2048]{3,2,1,0:T(8,128)(2,1)S(1)} %get-tuple-element.32.own_ref), channel_id=1, source_target_pairs={{4,8},{8,4},{12,16},{16,12},{20,24},{24,20},{28,32},{32,28},{36,40... | collective-permute-start | bytes 3145736 | tf_op jit(solution)/shard_map/ppermute | solution.py:200
  26.8 22.8 %collective-permute-start.3 = (bf16[2,2,32,2048]{3,2,1,0:T(8,128)(2,1)S(1)}, bf16[2,2,32,2048]{3,2,1,0:T(8,128)(2,1)S(1)}, u32[]{:S(2)}, u32[]{:S(2)}) collective-permute-start(bf16[2,2,32,2048]{3,2,1,0:T(8,128)(2,1)S(1)} %get-tuple-element.33.own_ref), channel_id=1, source_target_pairs={{0,4},{4,0},{8,12},{12,8},{16,20},{20,16},{24,28},{28,24},{32,36},... | collective-permute-start | bytes 1572872 | tf_op jit(solution)/shard_map/ppermute | solution.py:203
  26.9 22.7 %collective-permute-start.8 = (bf16[2,2,32,1024]{3,2,1,0:T(8,128)(2,1)S(1)}, bf16[2,2,32,1024]{3,2,1,0:T(8,128)(2,1)S(1)}, u32[]{:S(2)}, u32[]{:S(2)}) collective-permute-start(bf16[2,2,32,1024]{3,2,1,0:T(8,128)(2,1)S(1)} %copy-done.5), channel_id=1, source_target_pairs={{4,8},{8,4},{12,16},{16,12},{20,24},{24,20},{28,32},{32,28},{36,40... | collective-permute-start | bytes 786440 | tf_op jit(solution)/shard_map/ppermute | solution.py:200
  35.3 16.7 %collective-permute-start.4 = (bf16[2,2,32,1024]{3,2,1,0:T(8,128)(2,1)S(1)}, bf16[2,2,32,1024]{3,2,1,0:T(8,128)(2,1)S(1)}, u32[]{:S(2)}, u32[]{:S(2)}) collective-permute-start(bf16[2,2,32,1024]{3,2,1,0:T(8,128)(2,1)S(1)} %copy-done.3), channel_id=1, source_target_pairs={{4,8},{8,4},{12,16},{16,12},{20,24},{24,20},{28,32},{32,28},{36,40... | collective-permute-start | bytes 786440 | tf_op jit(solution)/shard_map/ppermute | solution.py:200

commit v9 on v8

--- a/solution.py
+++ b/solution.py
@@ -141,7 +141,7 @@
     return pl.pallas_call(
         functools.partial(phase_kernel, first_col, partial is not None, keep_sums),
         out_shape=jax.ShapeDtypeStruct((total, own.shape[3] // LOOK_C), jnp.float32),
-        in_specs=[pl.BlockSpec(memory_space=pltpu.SMEM)] + [vmem] * (4 + len(more)),
+        in_specs=[vmem] * (5 + len(more)),
         out_specs=vmem,
         scratch_shapes=[
             pltpu.VMEM((3 * acq, parts, cols // LANES, BAND, LANES), jnp.float32),

time: 79.9 us -> 79.4 us (level)
  Pallas kernels: 18.5 us -> 17.2 us
  waiting for transfers between devices: 11 us -> 11.8 us
    pallas_call x5, Pallas kernels: 15.6 us -> 14.3 us  [chunk_phase(): pl.pallas_call(functools.partial(phase_kernel, first_col, partial is not...]
    ppermute x5, waiting for transfers between devices: 11 us -> 11.8 us  [far_of(): return lax.ppermute(chunk, 'acq', far_pairs)]
  transfers between devices with their start and end apart: 9 -> 9, of which waited for: 4 -> 5; matrix products, arithmetic and copies ran while one was open for 0% -> 0% of each run, Pallas kernels for 20% -> 20%
where the time goes in v9:
time: 79.4 us; the launch traced here: 79.1 us
  blocking collectives  25.2 us (32%)
  starting transfers between devices  19.5 us (25%)
  Pallas kernels  17.2 us (22%)
  waiting for transfers between devices  11.8 us (15%)
  local copies, waits for them, and re-layouts  5.07 us (6%)
    all_to_all x1, blocking collectives, body(): lax.all_to_all(phases[-1].reshape(count, 1, -1), 'acq', split_axis=0, con...  25.2 us
    ppermute x5, starting transfers between devices, far_of(): return lax.ppermute(chunk, 'acq', far_pairs)  18.5 us
    pallas_call x5, Pallas kernels, chunk_phase(): pl.pallas_call(functools.partial(phase_kernel, first_col, partial is not...  14.3 us
    ppermute x5, waiting for transfers between devices, far_of(): return lax.ppermute(chunk, 'acq', far_pairs)  11.8 us
    unnamed x17, local copies, waits for them, and re-layouts  3.74 us
  transfers between devices with their start and end apart: 9, of which 5 were waited for; matrix products, arithmetic and copies ran while one was open for 0% of the time, Pallas kernels for 20%

profile of v9, /device:TPU:1, one launch (start us, length us, event | category | flops | bytes accessed | tf_op | source)
XLA Modules:
  0.0 79.1 jit_solution(2551070659929616491)
XLA Ops:
  0.0 1.3 %slice.3.own_ref = bf16[2,2,64,2048]{3,2,1,0:T(8,128)(2,1)S(1)} slice(bf16[2,2,256,2048]{3,2,1,0:T(8,128)(2,1)} %scenes_ref), slice={[0:2], [0:2], [0:64], [0:2048]} | slice | bytes 2097152 | tf_op jit(solution)/shard_map/slice | solution.py:209
  1.3 4.5 %collective-permute-start.1 = (bf16[2,2,64,2048]{3,2,1,0:T(8,128)(2,1)S(1)}, bf16[2,2,64,2048]{3,2,1,0:T(8,128)(2,1)}, u32[]{:S(2)}, u32[]{:S(2)}) collective-permute-start(bf16[2,2,64,2048]{3,2,1,0:T(8,128)(2,1)S(1)} %slice.3.own_ref), channel_id=1, source_target_pairs={{4,8},{8,4},{12,16},{16,12},{20,24},{24,20},{28,32},{32,28},{36,40... | collective-permute-start | bytes 3145736 | tf_op jit(solution)/shard_map/ppermute | solution.py:200
  5.9 0.4 collective-permute-start
  6.2 0.5 constants.1
  6.8 2.2 %copy-done = bf16[2,2,256,2048]{3,2,1,0:T(8,128)(2,1)S(1)} copy-done((bf16[2,2,256,2048]{3,2,1,0:T(8,128)(2,1)S(1)}, bf16[2,2,256,2048]{3,2,1,0:T(8,128)(2,1)}, u32[]{:S(2)}) %copy-start) | copy-done | bytes 4194328
  9.0 1.5 %cut.1 = (bf16[2,2,96,2048]{3,2,1,0:T(8,128)(2,1)}, bf16[2,2,64,2048]{3,2,1,0:T(8,128)(2,1)S(1)}, bf16[2,2,32,2048]{3,2,1,0:T(8,128)(2,1)S(1)}, bf16[2,2,32,1024...) custom-call(bf16[2,2,256,2048]{3,2,1,0:T(8,128)(2,1)S(1)} %copy-done), custom_call_target="tpu_custom_call" | custom-call | tf_op jit(solution)/shard_map/cut/pallas_call | solution.py:55
  10.4 0.7 copy-done.2
  11.2 0.7 copy-done.4
  11.9 3.2 %collective-permute-start.6 = (bf16[2,2,96,2048]{3,2,1,0:T(8,128)(2,1)}, bf16[2,2,96,2048]{3,2,1,0:T(8,128)(2,1)}, u32[]{:S(2)}, u32[]{:S(2)}) collective-permute-start(bf16[2,2,96,2048]{3,2,1,0:T(8,128)(2,1)} %get-tuple-element.36.own_ref), channel_id=1, source_target_pairs={{4,8},{8,4},{12,16},{16,12},{20,24},{24,20},{28,32},{32,28},{36,40... | collective-permute-start | bytes 4718600 | tf_op jit(solution)/shard_map/ppermute | solution.py:200
  15.3 3.2 %collective-permute-done.1.far_ref = bf16[2,2,64,2048]{3,2,1,0:T(8,128)(2,1)} collective-permute-done((bf16[2,2,64,2048]{3,2,1,0:T(8,128)(2,1)S(1)}, bf16[2,2,64,2048]{3,2,1,0:T(8,128)(2,1)}, u32[]{:S(2)}, u32[]{:S(2)}) %collective-permute-start.1) | collective-permute-done | bytes 1048608 | tf_op jit(solution)/shard_map/ppermute | solution.py:200
  18.4 4.2 %pair_phase.5.refs_0_ = f32[96,128]{1,0:T(8,128)S(1)} custom-call(s32[6,2]{1,0:T(8,128)S(1)} %fusion.3.pairs_ref, bf16[2,2,64,2048]{3,2,1,0:T(8,128)(2,1)} %collective-permute-done.near_ref, bf16[2,2,64,2048]{3,2,1,0:T(8,128)(2,1)S(1)} %slice.3.own_ref, bf16[2,2,64,2048]{3,2,1,0:T(8,128)(2,1)} %collective-permute-done.1.far_ref, ...), custom_call_target="tpu_custom_call" | custom-call | tf_op jit(solution)/shard_map/pair_phase/pallas_call | solution.py:141
  22.7 0.5 collective-permute-start.5
  23.2 3.6 %collective-permute-start.7 = (bf16[2,2,64,2048]{3,2,1,0:T(8,128)(2,1)S(1)}, bf16[2,2,64,2048]{3,2,1,0:T(8,128)(2,1)S(1)}, u32[]{:S(2)}, u32[]{:S(2)}) collective-permute-start(bf16[2,2,64,2048]{3,2,1,0:T(8,128)(2,1)S(1)} %get-tuple-element.32.own_ref), channel_id=1, source_target_pairs={{4,8},{8,4},{12,16},{16,12},{20,24},{24,20},{28,32},{32,28},{36,40... | collective-permute-start | bytes 3145736 | tf_op jit(solution)/shard_map/ppermute | solution.py:200
  27.0 3.5 %collective-permute-start.8 = (bf16[2,2,32,1024]{3,2,1,0:T(8,128)(2,1)S(1)}, bf16[2,2,32,1024]{3,2,1,0:T(8,128)(2,1)S(1)}, u32[]{:S(2)}, u32[]{:S(2)}) collective-permute-start(bf16[2,2,32,1024]{3,2,1,0:T(8,128)(2,1)S(1)} %copy-done.5), channel_id=1, source_target_pairs={{4,8},{8,4},{12,16},{16,12},{20,24},{24,20},{28,32},{32,28},{36,40... | collective-permute-start | bytes 786440 | tf_op jit(solution)/shard_map/ppermute | solution.py:200
  30.5 4.8 %collective-permute-done.6.far_ref = bf16[2,2,96,2048]{3,2,1,0:T(8,128)(2,1)} collective-permute-done((bf16[2,2,96,2048]{3,2,1,0:T(8,128)(2,1)}, bf16[2,2,96,2048]{3,2,1,0:T(8,128)(2,1)}, u32[]{:S(2)}, u32[]{:S(2)}) %collective-permute-start.6) | collective-permute-done | bytes 1572896 | tf_op jit(solution)/shard_map/ppermute | solution.py:200
  35.3 3.6 %collective-permute-start.4 = (bf16[2,2,32,1024]{3,2,1,0:T(8,128)(2,1)S(1)}, bf16[2,2,32,1024]{3,2,1,0:T(8,128)(2,1)S(1)}, u32[]{:S(2)}, u32[]{:S(2)}) collective-permute-start(bf16[2,2,32,1024]{3,2,1,0:T(8,128)(2,1)S(1)} %copy-done.3), channel_id=1, source_target_pairs={{4,8},{8,4},{12,16},{16,12},{20,24},{24,20},{28,32},{32,28},{36,40... | collective-permute-start | bytes 786440 | tf_op jit(solution)/shard_map/ppermute | solution.py:200
  38.9 5.7 %pair_phase.6.refs_1_ = f32[144,128]{1,0:T(8,128)S(1)} custom-call(s32[6,2]{1,0:T(8,128)S(1)} %fusion.3.pairs_ref, bf16[2,2,96,2048]{3,2,1,0:T(8,128)(2,1)S(1)} %collective-permute-done.5.near_ref, bf16[2,2,96,2048]{3,2,1,0:T(8,128)(2,1)} %get-tuple-element.36.own_ref, bf16[2,2,96,2048]{3,2,1,0:T(8,128)(2,1)} %collective-permute-done.6.far_ref, ...), custom_call_target="tpu_custom_call" | custom-call | tf_op jit(solution)/shard_map/pair_phase/pallas_call | solution.py:141
  44.7 1.7 %collective-permute-done.7.far_ref = bf16[2,2,64,2048]{3,2,1,0:T(8,128)(2,1)S(1)} collective-permute-done((bf16[2,2,64,2048]{3,2,1,0:T(8,128)(2,1)S(1)}, bf16[2,2,64,2048]{3,2,1,0:T(8,128)(2,1)S(1)}, u32[]{:S(2)}, u32[]{:S(2)}) %collective-permute-start.7) | collective-permute-done | bytes 1048608 | tf_op jit(solution)/shard_map/ppermute | solution.py:200
  46.4 2.7 %pair_phase.7.refs_2_ = f32[96,128]{1,0:T(8,128)S(1)} custom-call(s32[6,2]{1,0:T(8,128)S(1)} %fusion.3.pairs_ref, bf16[2,2,64,2048]{3,2,1,0:T(8,128)(2,1)S(1)} %collective-permute-done.2.near_ref, bf16[2,2,64,2048]{3,2,1,0:T(8,128)(2,1)S(1)} %get-tuple-element.32.own_ref, bf16[2,2,64,2048]{3,2,1,0:T(8,128)(2,1)S(1)} %collective-permute-done.7.far_ref, ...), custom_call_target="tpu_custom_call" | custom-call | tf_op jit(solution)/shard_map/pair_phase/pallas_call | solution.py:141
  49.2 0.8 %pair_phase.8.refs_3_ = f32[96,128]{1,0:T(8,128)S(1)} custom-call(s32[6,2]{1,0:T(8,128)S(1)} %fusion.3.pairs_ref, bf16[2,2,32,2048]{3,2,1,0:T(8,128)(2,1)S(1)} %collective-permute-done.3.near_ref, bf16[2,2,32,2048]{3,2,1,0:T(8,128)(2,1)S(1)} %get-tuple-element.33.own_ref, bf16[2,2,32,1024]{3,2,1,0:T(8,128)(2,1)S(1)} %collective-permute-done.8.far_ref, ...), custom_call_target="tpu_custom_call" | custom-call | tf_op jit(solution)/shard_map/pair_phase/pallas_call | solution.py:141
  50.1 2.0 %collective-permute-done.4.far_ref = bf16[2,2,32,1024]{3,2,1,0:T(8,128)(2,1)S(1)} collective-permute-done((bf16[2,2,32,1024]{3,2,1,0:T(8,128)(2,1)S(1)}, bf16[2,2,32,1024]{3,2,1,0:T(8,128)(2,1)S(1)}, u32[]{:S(2)}, u32[]{:S(2)}) %collective-permute-start.4) | collective-permute-done | bytes 262176 | tf_op jit(solution)/shard_map/ppermute | solution.py:200
  52.0 0.9 %pair_phase.9 = f32[384,128]{1,0:T(8,128)S(1)} custom-call(s32[6,2]{1,0:T(8,128)S(1)} %fusion.3.pairs_ref, bf16[2,2,32,2048]{3,2,1,0:T(8,128)(2,1)S(1)} %collective-permute-done.3.near_ref, bf16[2,2,32,2048]{3,2,1,0:T(8,128)(2,1)S(1)} %get-tuple-element.33.own_ref, bf16[2,2,32,1024]{3,2,1,0:T(8,128)(2,1)S(1)} %collective-permute-done.4.far_ref, ...), custom_call_target="tpu_custom_call" | custom-call | tf_op jit(solution)/shard_map/pair_phase/pallas_call | solution.py:141
  52.9 25.2 %all_to_all.5 = f32[64,1,768]{2,1,0:T(1,128)S(1)} all-to-all(f32[64,1,768]{2,1,0:T(1,128)S(1)} %bitcast.2), channel_id=1, replica_groups=mesh['acq'=64,'rng'=4] {'acq'}, dimensions={0} | all-to-all | bytes 393216 | tf_op jit(solution)/shard_map/all_to_all | solution.py:227
  78.1 0.9 %series.1 = f32[1,128,128]{2,1,0:T(8,128)} custom-call(bf16[3,128,384]{2,1,0:T(8,128)(2,1)S(1)} %get-tuple-element.24.slots_ref, f32[384,128]{1,0:T(8,128)S(1)} %bitcast.3), custom_call_target="tpu_custom_call" | custom-call | tf_op jit(solution)/shard_map/series/pallas_call | solution.py:229
  (23 shorter events, 0.5 us)
Async XLA Ops:
  0.0 6.2 %copy-start.6 = (s32[384]{0:T(512)S(1)}, s32[384]{0:T(512)}, u32[]{:S(2)}) copy-start(s32[384]{0:T(512)} %param.6) | copy-start | bytes 4612
  0.0 6.2 %copy-start.1 = (f32[128,384]{1,0:T(8,128)S(1)}, f32[128,384]{1,0:T(8,128)}, u32[]{:S(2)}) copy-start(f32[128,384]{1,0:T(8,128)} %pinv_ref.1) | copy-start | bytes 589828
  1.3 17.1 %collective-permute-start.1 = (bf16[2,2,64,2048]{3,2,1,0:T(8,128)(2,1)S(1)}, bf16[2,2,64,2048]{3,2,1,0:T(8,128)(2,1)}, u32[]{:S(2)}, u32[]{:S(2)}) collective-permute-start(bf16[2,2,64,2048]{3,2,1,0:T(8,128)(2,1)S(1)} %slice.3.own_ref), channel_id=1, source_target_pairs={{4,8},{8,4},{12,16},{16,12},{20,24},{24,20},{28,32},{32,28},{36,40... | collective-permute-start | bytes 3145736 | tf_op jit(solution)/shard_map/ppermute | solution.py:200
  5.9 12.6 %collective-permute-start = (bf16[2,2,64,2048]{3,2,1,0:T(8,128)(2,1)S(1)}, bf16[2,2,64,2048]{3,2,1,0:T(8,128)(2,1)}, u32[]{:S(2)}, u32[]{:S(2)}) collective-permute-start(bf16[2,2,64,2048]{3,2,1,0:T(8,128)(2,1)S(1)} %slice.3.own_ref), channel_id=1, source_target_pairs={{0,4},{4,0},{8,12},{12,8},{16,20},{20,16},{24,28},{28,24},{32,36},... | collective-permute-start | bytes 3145736 | tf_op jit(solution)/shard_map/ppermute | solution.py:203
  6.8 2.2 %copy-start = (bf16[2,2,256,2048]{3,2,1,0:T(8,128)(2,1)S(1)}, bf16[2,2,256,2048]{3,2,1,0:T(8,128)(2,1)}, u32[]{:S(2)}) copy-start(bf16[2,2,256,2048]{3,2,1,0:T(8,128)(2,1)} %scenes_ref) | copy-start | bytes 12582916
  9.0 6.2 %copy-start.7 = (s32[6,2]{0,1:T(2,128)S(1)}, s32[6,2]{0,1:T(2,128)}, u32[]{:S(2)}) copy-start(s32[6,2]{0,1:T(2,128)} %param.5) | copy-start | bytes 148
  10.4 0.7 copy-start.2
  11.2 0.7 copy-start.4
  11.9 23.4 %collective-permute-start.6 = (bf16[2,2,96,2048]{3,2,1,0:T(8,128)(2,1)}, bf16[2,2,96,2048]{3,2,1,0:T(8,128)(2,1)}, u32[]{:S(2)}, u32[]{:S(2)}) collective-permute-start(bf16[2,2,96,2048]{3,2,1,0:T(8,128)(2,1)} %get-tuple-element.36.own_ref), channel_id=1, source_target_pairs={{4,8},{8,4},{12,16},{16,12},{20,24},{24,20},{28,32},{32,28},{36,40... | collective-permute-start | bytes 4718600 | tf_op jit(solution)/shard_map/ppermute | solution.py:200
  15.3 11.7 %copy-start.5 = (bf16[2,2,32,1024]{3,2,1,0:T(8,128)(2,1)S(1)}, bf16[2,2,32,1024]{3,2,1,0:T(8,128)(2,1)}, u32[]{:S(2)}) copy-start(bf16[2,2,32,1024]{3,2,1,0:T(8,128)(2,1)} %copy-done.4) | copy-start | bytes 786436
  15.3 20.0 %copy-start.3 = (bf16[2,2,32,1024]{3,2,1,0:T(8,128)(2,1)S(1)}, bf16[2,2,32,1024]{3,2,1,0:T(8,128)(2,1)}, u32[]{:S(2)}) copy-start(bf16[2,2,32,1024]{3,2,1,0:T(8,128)(2,1)} %copy-done.2) | copy-start | bytes 786436
  22.6 4.2 %collective-permute-start.2 = (bf16[2,2,64,2048]{3,2,1,0:T(8,128)(2,1)S(1)}, bf16[2,2,64,2048]{3,2,1,0:T(8,128)(2,1)S(1)}, u32[]{:S(2)}, u32[]{:S(2)}) collective-permute-start(bf16[2,2,64,2048]{3,2,1,0:T(8,128)(2,1)S(1)} %get-tuple-element.32.own_ref), channel_id=1, source_target_pairs={{0,4},{4,0},{8,12},{12,8},{16,20},{20,16},{24,28},{28,24},{32,36},... | collective-permute-start | bytes 3145736 | tf_op jit(solution)/shard_map/ppermute | solution.py:203
  22.7 16.2 %collective-permute-start.5 = (bf16[2,2,96,2048]{3,2,1,0:T(8,128)(2,1)}, bf16[2,2,96,2048]{3,2,1,0:T(8,128)(2,1)S(1)}, u32[]{:S(2)}, u32[]{:S(2)}) collective-permute-start(bf16[2,2,96,2048]{3,2,1,0:T(8,128)(2,1)} %get-tuple-element.36.own_ref), channel_id=1, source_target_pairs={{0,4},{4,0},{8,12},{12,8},{16,20},{20,16},{24,28},{28,24},{32,36},... | collective-permute-start | bytes 4718600 | tf_op jit(solution)/shard_map/ppermute | solution.py:203
  23.2 23.2 %collective-permute-start.7 = (bf16[2,2,64,2048]{3,2,1,0:T(8,128)(2,1)S(1)}, bf16[2,2,64,2048]{3,2,1,0:T(8,128)(2,1)S(1)}, u32[]{:S(2)}, u32[]{:S(2)}) collective-permute-start(bf16[2,2,64,2048]{3,2,1,0:T(8,128)(2,1)S(1)} %get-tuple-element.32.own_ref), channel_id=1, source_target_pairs={{4,8},{8,4},{12,16},{16,12},{20,24},{24,20},{28,32},{32,28},{36,40... | collective-permute-start | bytes 3145736 | tf_op jit(solution)/shard_map/ppermute | solution.py:200
  26.9 22.3 %collective-permute-start.3 = (bf16[2,2,32,2048]{3,2,1,0:T(8,128)(2,1)S(1)}, bf16[2,2,32,2048]{3,2,1,0:T(8,128)(2,1)S(1)}, u32[]{:S(2)}, u32[]{:S(2)}) collective-permute-start(bf16[2,2,32,2048]{3,2,1,0:T(8,128)(2,1)S(1)} %get-tuple-element.33.own_ref), channel_id=1, source_target_pairs={{0,4},{4,0},{8,12},{12,8},{16,20},{20,16},{24,28},{28,24},{32,36},... | collective-permute-start | bytes 1572872 | tf_op jit(solution)/shard_map/ppermute | solution.py:203
  27.0 22.2 %collective-permute-start.8 = (bf16[2,2,32,1024]{3,2,1,0:T(8,128)(2,1)S(1)}, bf16[2,2,32,1024]{3,2,1,0:T(8,128)(2,1)S(1)}, u32[]{:S(2)}, u32[]{:S(2)}) collective-permute-start(bf16[2,2,32,1024]{3,2,1,0:T(8,128)(2,1)S(1)} %copy-done.5), channel_id=1, source_target_pairs={{4,8},{8,4},{12,16},{16,12},{20,24},{24,20},{28,32},{32,28},{36,40... | collective-permute-start | bytes 786440 | tf_op jit(solution)/shard_map/ppermute | solution.py:200
  35.3 16.7 %collective-permute-start.4 = (bf16[2,2,32,1024]{3,2,1,0:T(8,128)(2,1)S(1)}, bf16[2,2,32,1024]{3,2,1,0:T(8,128)(2,1)S(1)}, u32[]{:S(2)}, u32[]{:S(2)}) collective-permute-start(bf16[2,2,32,1024]{3,2,1,0:T(8,128)(2,1)S(1)} %copy-done.3), channel_id=1, source_target_pairs={{4,8},{8,4},{12,16},{16,12},{20,24},{24,20},{28,32},{32,28},{36,40... | collective-permute-start | bytes 786440 | tf_op jit(solution)/shard_map/ppermute | solution.py:200
